TPU v7x, 128 devices: a whole 4x4x4 slice. The times are simulated.
128 devices in a mesh: grp: 4 (over z), dev: 32 (over y, x, core).
Axes of the slice: x: 4, y: 4, z: 4, core: 2. Of those that a mesh axis runs over, the one named last changes fastest.
Arguments:
- inputs: bfloat16 [262144, 1536], P(('grp', 'dev')), may hold values from -6 to 6
- gate_in: bfloat16 [262144, 1536], P(('grp', 'dev')), may hold values from -6 to 6
- b_proj: bfloat16 [262144, 128], P(('grp', 'dev')), may hold values from -2 to 2
- c_proj: bfloat16 [262144, 128], P(('grp', 'dev')), may hold values from -2 to 2
- log_decay: float32 [24, 262144], P(None, ('grp', 'dev')), may hold values from -0.8 to 0
- d_skip: float32 [24], replicated, may hold values from 0.5 to 2
- norm_gain: float32 [1536], replicated, may hold values from 0.1 to 1.9
Outputs:
- result: bfloat16 [262144, 1536], P(('grp', 'dev'))
All inputs are finite; a program needn't handle non-finite values.
Results may differ from a plain program's by a relative error of at most 0.0051.
Values sent between devices are 32-bit elements; how exact they have to be, the bound alone decides.
No kernel may reach another device: no remote copies, remote signals or barrier semaphores. Data moves between devices by JAX's collectives and lax.ppermute only.
A program may use at most 384 MiB of HBM per device.

v0:
```python
import jax
import jax.numpy as jnp
from jax import lax
from jax.sharding import PartitionSpec as P

Q = 256


def entering_2(part, axis, combine, identity):
    place = lax.axis_index(axis)
    gathered = jax.tree.map(lambda a: lax.all_gather(a, axis), part)
    state = jax.tree.map(lambda a, e: jnp.zeros_like(a) + jnp.asarray(e, a.dtype), part, identity)

    def one(lap, state):
        return combine(
            state, jax.tree.map(lambda a: lax.dynamic_index_in_dim(a, lap, 0, False), gathered)
        )

    return lax.fori_loop(0, place, one, state)


def broadcast(block, axis, source):
    block = jnp.where(lax.axis_index(axis) == source, block, jnp.zeros_like(block))
    return lax.psum(block, axis)


def combine(earlier, later):
    early_log, early_state = earlier
    late_log, late_state = later
    return (early_log + late_log, jnp.exp(late_log)[:, None, None] * early_state + late_state)


def block_terms(element):
    piece, b_rows, c_rows, decay_rows = element
    length = decay_rows.shape[1]
    cumul = jnp.cumsum(decay_rows, axis=1)
    scores = jnp.dot(c_rows, b_rows.T, preferred_element_type=jnp.float32)
    causal = jnp.tril(jnp.ones((length, length), dtype=bool))
    spread = jnp.where(causal[None], cumul[:, :, None] - cumul[:, None, :], -jnp.inf)
    weight = (scores[None] * jnp.exp(spread)).astype(jnp.bfloat16)
    within = jnp.einsum("hts,shp->thp", weight, piece, preferred_element_type=jnp.float32)
    fading = jnp.exp(cumul[:, -1:] - cumul)
    scaled_b = (fading[:, :, None] * b_rows.astype(jnp.float32)[None]).astype(jnp.bfloat16)
    summary = jnp.einsum("hqn,qhp->hnp", scaled_b, piece, preferred_element_type=jnp.float32)
    return (within, summary, cumul)


def on_device(inputs, gate_in, b_proj, c_proj, log_decay, d_skip, norm_gain):
    row_count = inputs.shape[0]
    full_width = inputs.shape[1]
    head_count = log_decay.shape[0]
    head_dim = full_width // head_count
    state_dim = b_proj.shape[1]
    blocks = row_count // Q
    values = inputs.reshape(blocks, Q, head_count, head_dim)
    c_blocks = c_proj.reshape(blocks, Q, state_dim)
    decays = log_decay.reshape(head_count, blocks, Q).transpose(1, 0, 2)
    within, summary, cumul = lax.map(
        block_terms, (values, b_proj.reshape(blocks, Q, state_dim), c_blocks, decays)
    )

    def advance(running, element):
        run_log, run_state = running
        block_log, block_state = element
        updated = (run_log + block_log, jnp.exp(block_log)[:, None, None] * run_state + block_state)
        return (updated, running)

    empty_log = jnp.zeros((head_count,), jnp.float32)
    empty_state = jnp.zeros((head_count, state_dim, head_dim), jnp.float32)
    (own_log, own_state), (start_log, start_state) = lax.scan(
        advance, (empty_log, empty_state), (cumul[:, :, -1], summary)
    )
    identity = (empty_log, empty_state)
    member_log, member_state = entering_2((own_log, own_state), "dev", combine, identity)
    group_log, group_state = combine((member_log, member_state), (own_log, own_state))
    last_member = lax.axis_size("dev") - 1
    whole_log, whole_state = (
        broadcast(group_log, "dev", last_member),
        broadcast(group_state, "dev", last_member),
    )
    outer_log, outer_state = entering_2((whole_log, whole_state), "grp", combine, identity)
    incoming_log, incoming_state = combine((outer_log, outer_state), (member_log, member_state))
    entering = start_state + jnp.exp(start_log)[:, :, None, None] * incoming_state[None]
    rounded = entering.astype(jnp.bfloat16)
    carried = jnp.einsum("cqn,chnp->cqhp", c_blocks, rounded, preferred_element_type=jnp.float32)
    carried = carried * jnp.exp(cumul).transpose(0, 2, 1)[:, :, :, None]
    summed = within + carried + d_skip[None, None, :, None] * values.astype(jnp.float32)
    gated_out = summed * jax.nn.silu(
        gate_in.reshape(blocks, Q, head_count, head_dim).astype(jnp.float32)
    )
    inverse = lax.rsqrt(jnp.mean(gated_out * gated_out, axis=-1, keepdims=True) + 1e-05)
    result = (gated_out * inverse).reshape(row_count, full_width) * norm_gain[None]
    return result.astype(jnp.bfloat16)


def solution(mesh):
    return jax.shard_map(
        on_device,
        mesh=mesh,
        in_specs=(
            P(("grp", "dev"), None),
            P(("grp", "dev"), None),
            P(("grp", "dev"), None),
            P(("grp", "dev"), None),
            P(None, ("grp", "dev")),
            P(),
            P(),
        ),
        out_specs=P(("grp", "dev"), None),
        check_vma=False,
    )
```

profile of v0, /device:TPU:96, one launch (start us, length us, event | category | flops | bytes accessed | tf_op | source)
XLA Modules:
  0.0 713.2 jit_solution(6770344821279443986)
XLA Ops:
  7.5 16.3 %reshape.153 = bf16[8,256,24,64]{3,2,1,0:T(8,128)(2,1)} reshape(bf16[2048,1536]{1,0:T(8,128)(2,1)} %param.15) | data formatting | bytes 12582912 | tf_op jit(solution)/shard_map/reshape | solution.py:55
  23.8 13.1 %copy.52 = bf16[8,256,24,64]{1,3,2,0:T(8,128)(2,1)} copy(bf16[8,256,24,64]{3,2,1,0:T(8,128)(2,1)} %reshape.153) | data formatting | bytes 12582912 | tf_op jit(solution)/shard_map/while | solution.py:58
  36.9 83.4 %while.55 = (s32[]{:T(128)}, f32[8,256,24,64]{1,3,2,0:T(8,128)}, f32[8,24,128,64]{2,3,1,0:T(8,128)}, f32[8,24,256]{2,1,0:T(8,128)S(1)}, bf16[8,256,24,64]{1,3,2,...) while((s32[]{:T(128)}, f32[8,256,24,64]{1,3,2,0:T(8,128)}, ...), condition=%wide.region_3.4_spmd, body=%wide.region_0.3_spmd.sunk | while | flops 327534656 | bytes 5567681 | solution.py:58
  40.2 3.2 fusion.56
  43.3 4.0 bitcast_dynamic-update-slice_fusion.4
  50.6 3.2 fusion.56
  53.8 3.9 bitcast_dynamic-update-slice_fusion.4
  61.0 3.2 fusion.56
  64.2 4.0 bitcast_dynamic-update-slice_fusion.4
  71.5 3.2 fusion.56
  74.6 4.0 bitcast_dynamic-update-slice_fusion.4
  81.9 3.2 fusion.56
  85.1 4.0 bitcast_dynamic-update-slice_fusion.4
  92.3 3.2 fusion.56
  95.5 4.0 bitcast_dynamic-update-slice_fusion.4
  102.8 3.2 fusion.56
  105.9 3.9 bitcast_dynamic-update-slice_fusion.4
  113.2 3.1 fusion.56
  116.3 4.0 bitcast_dynamic-update-slice_fusion.4
  120.7 42.9 %while.58 = (s32[]{:T(128)}, f32[24]{0:T(128)S(1)}, f32[24,128,64]{2,1,0:T(8,128)S(1)}, f32[8,24]{1,0:T(8,128)S(1)}, f32[8,24,128,64]{3,2,1,0:T(8,128)}, /*index...) while((s32[]{:T(128)}, f32[24]{0:T(128)S(1)}, ...), condition=%wide.region_5.6_spmd.clone, body=%wide.region_4.5_spmd.clone.sunk | while | flops 786483 | bytes 7865217 | solution.py:70
  120.8 2.1 constant_dynamic-slice_fusion.13
  122.9 1.6 copy.100
  124.5 1.3 bitcast_dynamic-update-slice_fusion.5
  126.2 2.1 constant_dynamic-slice_fusion.13
  128.3 1.6 copy.100
  131.5 2.1 constant_dynamic-slice_fusion.13
  133.6 1.6 copy.100
  136.9 2.1 constant_dynamic-slice_fusion.13
  139.0 1.6 copy.100
  142.3 2.1 constant_dynamic-slice_fusion.13
  144.4 1.6 copy.100
  147.6 2.1 constant_dynamic-slice_fusion.13
  149.7 1.6 copy.100
  153.0 2.1 constant_dynamic-slice_fusion.13
  155.1 1.6 copy.100
  158.3 2.1 constant_dynamic-slice_fusion.13
  160.4 1.6 copy.100
  163.6 1.3 copy.56
  166.5 68.5 %all-reduce = f32[768]{0:T(1024)S(1)} all-reduce(f32[768]{0:T(1024)S(1)} %dynamic-update-slice), channel_id=2, replica_groups=mesh['grp'=4,'dev'=32] {'dev'}, use_global_device_ids=true, to_apply=%add | all-reduce | flops 768 | bytes 6144
  235.1 23.7 %all-gather.8.cloned.1.call-done = f32[768,128,64]{1,2,0:T(8,128)} async-done(((f32[24,128,64]{1,2,0:T(8,128)}), f32[768,128,64]{1,2,0:T(8,128)}) %all-gather.8.cloned.1.call-update) | async-done | bytes 25165840 | tf_op jit(solution)/shard_map/all_gather | solution.py:11
  259.4 2.2 select_bitcast_fusion
  261.7 228.2 %all-reduce.3.cloned.1.call-done = f32[1,24,128,64]{2,3,1,0:T(8,128)} async-done(((f32[1,24,128,64]{2,3,1,0:T(8,128)}), f32[1,24,128,64]{2,3,1,0:T(8,128)}) %all-reduce.3.cloned.1.call-update) | async-done | bytes 786448 | tf_op jit(solution)/shard_map/psum | solution.py:24
  489.9 17.0 %reshape.154 = f32[8,256,24,64]{3,2,1,0:T(8,128)} reshape(bf16[2048,1536]{1,0:T(8,128)(2,1)} %param.16) | data formatting | bytes 18874368 | tf_op jit(solution)/shard_map/convert_element_type | solution.py:89
  506.9 18.7 %copy.67 = f32[8,256,24,64]{1,3,2,0:T(8,128)} copy(f32[8,256,24,64]{3,2,1,0:T(8,128)} %reshape.154) | data formatting | bytes 25165824 | tf_op jit(solution)/shard_map/convert_element_type | solution.py:89
  525.6 66.1 %psum.14 = f32[1,24]{1,0:T(1,128)S(1)} all-reduce(f32[1,24]{1,0:T(1,128)S(1)} %get-tuple-element.330), channel_id=1, replica_groups=mesh['grp'=4,'dev'=32] {'dev'}, use_global_device_ids=true, to_apply=%region_8.9 | all-reduce | flops 24 | bytes 192 | tf_op jit(solution)/shard_map/psum | solution.py:24
  591.7 6.7 all-gather.2
  598.4 1.3 broadcast.55.clone.1
  599.7 19.4 %while.57 = (s32[]{:T(128)}, f32[24,128,64]{2,1,0:T(8,128)}, s32[]{:T(128)}, f32[4,24]{1,0:T(4,128)S(1)}, f32[4,24,128,64]{2,3,1,0:T(8,128)}, /*index=5*/s32[]{:T(128)}, s32[]{:T(128)}, s32[]{:T(128)}) while((s32[]{:T(128)}, f32[24,128,64]{2,1,0:T(8,128)}, s32[]{:T(128)}, f32[4,24]{1,0:T(4,128)S(1)}, f32[4,24,128,64]{2,3,1,0:T(8,128)}, ...), condition=%wide.region_11.12_spmd, body=%wide.region_10.11_spmd.sunk | while | flops 393221 | bytes 5505447 | solution.py:19
  599.8 2.1 constant_dynamic-slice_fusion.12
  601.8 1.6 copy.99
  603.5 2.8 bitcast_add_fusion.8
  606.2 2.1 constant_dynamic-slice_fusion.12
  608.3 1.6 copy.99
  609.9 2.8 bitcast_add_fusion.8
  612.7 2.1 constant_dynamic-slice_fusion.12
  614.8 1.6 copy.99
  616.4 2.8 bitcast_add_fusion.8
  619.2 1.6 multiply_add_fusion
  620.8 21.4 %multiply_reduce_fusion = (f32[8,256,24]{1,2,0:T(8,128)S(1)}, f32[8,256,24,64]{1,3,2,0:T(8,128)}) fusion(f32[8,256,24,64]{1,3,2,0:T(8,128)} %copy.67, bf16[8,256,24,64]{1,3,2,0:T(8,128)(2,1)} %get-tuple-element.619, f32[24]{0:T(128)S(1)} %copy-done.1, f32[8,256,24,64]{1,3,2,0:T(8,128)} %get-tuple-element.167, ...), kind=kOutput, calls=%fused_computation.58 | convolution fusion | flops 847724544 | bytes 52036448 | tf_op jit(solution)/shard_map/cqn,chnp->cqhp/dot_general | solution.py:85
  642.3 12.1 %broadcast_multiply_fusion = f32[8,256,24,64]{1,3,2,0:T(8,128)} fusion(f32[8,256,24,64]{1,3,2,0:T(8,128)} %get-tuple-element.333, f32[8,256,24]{1,2,0:T(8,128)S(1)} %add_rsqrt_fusion), kind=kLoop, calls=%fused_computation.61 | loop fusion | flops 3145728 | bytes 25362432 | tf_op jit(solution)/shard_map/mul | solution.py:92
  654.4 20.3 %copy.68 = f32[8,256,24,64]{1,0,3,2:T(8,128)} copy(f32[8,256,24,64]{1,3,2,0:T(8,128)} %broadcast_multiply_fusion) | data formatting | bytes 25165824 | tf_op jit(solution)/shard_map/mul | solution.py:92
  674.7 15.4 %copy.83 = f32[192,8,8,256]{3,1,2,0:T(8,128)} copy(f32[192,8,8,256]{3,2,1,0:T(8,128)} %bitcast.124) | data formatting | bytes 25165824
  690.2 7.9 %multiply_convert_fusion.10 = bf16[2048,1536]{0,1:T(8,128)(2,1)} fusion(f32[2048,1536]{0,1:T(8,128)} %bitcast.125, f32[1536]{0:T(1024)S(1)} %copy-done), kind=kLoop, calls=%fused_computation.57 | loop fusion | flops 6291456 | bytes 18880512 | tf_op jit(solution)/shard_map/convert_element_type | solution.py:93
  698.1 8.6 %copy.69 = bf16[2048,1536]{1,0:T(8,128)(2,1)} copy(bf16[2048,1536]{0,1:T(8,128)(2,1)} %multiply_convert_fusion.10) | data formatting | bytes 12582912 | tf_op jit(solution)/shard_map/convert_element_type | solution.py:93
  (197 shorter events, 40.6 us)
Async XLA Ops:
  6.5 252.3 %all-gather.8.cloned.1.call-start = ((), (), s32[]{:S(2)}) async-start(), calls=%async_computation.2 | async-start | bytes 25952256 | tf_op jit(solution)/shard_map/all_gather | solution.py:11
  120.7 44.3 %copy-start.2 = (u32[128]{0:T(128)S(1)}, u32[128]{0:T(128)}, u32[]{:S(2)}) copy-start(u32[128]{0:T(128)} %constant.97) | copy-start | bytes 1540
  165.0 324.9 %all-reduce.3.cloned.1.call-start = ((), (), s32[]{:S(2)}) async-start(), calls=%async_computation | async-start | bytes 1572864 | tf_op jit(solution)/shard_map/psum | solution.py:24
  261.6 336.8 %all-gather.6.cloned.1.call-start = ((), (), s32[]{:S(2)}) async-start(), calls=%async_computation.1 | async-start | bytes 3932160 | tf_op jit(solution)/shard_map/all_gather | solution.py:11
  599.7 21.1 %copy-start.1 = (f32[24]{0:T(128)S(1)}, f32[24]{0:T(128)}, u32[]{:S(2)}) copy-start(f32[24]{0:T(128)} %param.20) | copy-start | bytes 292
  674.7 15.4 %copy-start = (f32[1536]{0:T(1024)S(1)}, f32[1536]{0:T(1024)}, u32[]{:S(2)}) copy-start(f32[1536]{0:T(1024)} %param.21) | copy-start | bytes 18436
Sparse Core Ops, SparseCore 0:
  165.1 93.6 all-gather.7
  262.0 227.7 all-reduce.2
  491.5 37.0 all-gather.5
where the time goes:
time: 720 us; the launch traced here: 713 us
  waiting for transfers between devices  252 us (35%)
  local copies, waits for them, and re-layouts  159 us (22%)
  blocking collectives  141 us (20%)
  matrix products  86.9 us (12%)
  other arithmetic  58.8 us (8%)
  between operations  13.9 us (2%)
    psum x1, waiting for transfers between devices, broadcast(): return lax.psum(block, axis)  228 us
    unnamed x1, blocking collectives  68.5 us
    psum x1, blocking collectives, broadcast(): return lax.psum(block, axis)  66.1 us
    convert_element_type x2, local copies, waits for them, and re-layouts, on_device(): gate_in.reshape(blocks, Q, head_count, head_dim).astype(jnp.float32)  35.7 us
    dot_general x8, matrix products, block_terms(): jnp.einsum('hts,shp->thp', weight, piece, preferred_element_type=jnp.floa...  31.8 us
    dynamic_slice x16, local copies, waits for them, and re-layouts, on_device(): lax.scan(advance, (empty_log, empty_state), (cumul[:, :, -1], summary))  29.7 us
    dot_general x8, matrix products, block_terms(): jnp.einsum('hqn,qhp->hnp', scaled_b, piece, preferred_element_type=jnp.fl...  25.2 us
    all_gather x2, waiting for transfers between devices, entering_2(): gathered = jax.tree.map(lambda a: lax.all_gather(a, axis), part)  23.7 us
  transfers between devices with their start and end apart: 3, of which 2 were waited for; matrix products, arithmetic and copies ran while one was open for 5% of the time, Pallas kernels for 0%

commit v1 on v0

v1 whole, which is shorter than its diff:
```python
import jax
import jax.numpy as jnp
from jax import lax
from jax.experimental import pallas as pl
from jax.experimental.pallas import tpu as pltpu
from jax.sharding import PartitionSpec as P

HEADS = 24
HEAD = 64
STATE = 128
WIDTH = HEADS * HEAD
HALF = WIDTH // 2
SUB = 128
STEP = 256
GROUP = 256
ROWS = STATE + 8
SHIFT = 74
SHIFT_LOG = 51.29289136
GRID = 8
QUARTER = STATE // 4
F32 = jnp.float32
BF16 = jnp.bfloat16


def dot(a, b, dims=((1,), (0,))):
    return lax.dot_general(a, b, (dims, ((), ())), preferred_element_type=F32)


def iota(shape, dim):
    return lax.broadcasted_iota(jnp.int32, shape, dim)


def three(v):
    high = v.astype(BF16)
    rest = v - high.astype(F32)
    middle = rest.astype(BF16)
    low = (rest - middle.astype(F32)).astype(BF16)
    return high, middle, low


def spread_parts(v):
    high, middle, low = three(v)
    lane = iota(v.shape, 1)
    picked = jnp.where(
        lane < HEADS, high.astype(F32), jnp.where(lane < 2 * HEADS, middle.astype(F32), low.astype(F32))
    )
    return picked.astype(BF16)


def decay_sums(matrix, decay):
    high, middle, low = three(decay)
    nt = ((1,), (1,))
    return dot(matrix, high, nt) + (dot(matrix, middle, nt) + dot(matrix, low, nt))


def spread_matrix():
    k = iota((3 * HEADS, WIDTH), 0)
    head = iota((3 * HEADS, WIDTH), 1) // HEAD
    hit = (k == head) | (k == head + HEADS) | (k == head + 2 * HEADS)
    return jnp.where(hit, 1.0, 0.0).astype(BF16)


def end_state_kernel(core_ref, x_ref, b_ref, decay_ref, spread_ref, keep_ref, send_ref, acc):
    step = pl.program_id(0)

    @pl.when(step == 0)
    def _():
        acc[:STATE] = jnp.zeros((STATE, WIDTH), F32)
        acc[STATE:] = jnp.ones((8, WIDTH), F32)

    decay = decay_ref[...]
    decay = jnp.concatenate([decay] * 3, axis=0)
    row, col = iota((STEP + 16, STEP), 0), iota((STEP + 16, STEP), 1)
    later = jnp.where((col > row) | (row >= STEP), 1.0, 0.0).astype(BF16)
    factors = spread_parts(jnp.exp(decay_sums(later, decay)))
    b = b_ref[...]
    for g in range(WIDTH // GROUP):
        lanes = slice(g * GROUP, (g + 1) * GROUP)
        wide = dot(factors, spread_ref[:, lanes])
        scaled = (x_ref[:, lanes].astype(F32) * wide[:STEP]).astype(BF16)
        total = wide[STEP : STEP + 1]
        acc[:STATE, lanes] = acc[:STATE, lanes] * total + dot(b, scaled, ((0,), (0,)))
        acc[STATE:, lanes] = acc[STATE:, lanes] * total

    @pl.when(step == pl.num_programs(0) - 1)
    def _():
        mine = pl.multiple_of(core_ref[0] * HALF, HALF)
        other = pl.multiple_of((1 - core_ref[0]) * HALF, HALF)
        keep_ref[...] = acc[:, pl.ds(mine, HALF)]
        send_ref[...] = acc[:, pl.ds(other, HALF)]


def end_state(core, x, b, decay, spread):
    tokens = x.shape[0]
    half = jax.ShapeDtypeStruct((ROWS, HALF), F32)
    return pl.pallas_call(
        end_state_kernel,
        grid_spec=pltpu.PrefetchScalarGridSpec(
            num_scalar_prefetch=1,
            grid=(tokens // STEP,),
            in_specs=[
                pl.BlockSpec((STEP, WIDTH), lambda i, c: (i, 0)),
                pl.BlockSpec((STEP, STATE), lambda i, c: (i, 0)),
                pl.BlockSpec((HEADS, STEP), lambda i, c: (0, i)),
                pl.BlockSpec((3 * HEADS, WIDTH), lambda i, c: (0, 0)),
            ],
            out_specs=[
                pl.BlockSpec((ROWS, HALF), lambda i, c: (0, 0)),
                pl.BlockSpec((ROWS, HALF), lambda i, c: (0, 0)),
            ],
            scratch_shapes=[pltpu.VMEM((ROWS, WIDTH), F32)],
        ),
        out_shape=[half, half],
        name="end_state",
        compiler_params=pltpu.CompilerParams(vmem_limit_bytes=40 * 1024 * 1024),
    )(core, x, b, decay, spread)


def small_call(kernel, name, place, args, outs):
    vmem = pl.BlockSpec(memory_space=pltpu.VMEM)
    return pl.pallas_call(
        kernel,
        in_specs=[pl.BlockSpec(memory_space=pltpu.SMEM)] + [vmem] * len(args),
        out_specs=[vmem] * len(outs),
        out_shape=[jax.ShapeDtypeStruct(s, F32) for s in outs],
        name=name,
    )(place, *args)


Z, Y, X, CORE = 0, 1, 2, 3


def pair_kernel(place, keep, recv, own, *sends):
    flip = place[CORE] == 1
    kept, got = keep[STATE : STATE + 8], recv[STATE : STATE + 8]
    late = jnp.where(flip, kept, got)[:1]
    decay = kept * got
    for shift, out in enumerate((own,) + sends):
        chunk = (place[X] + shift) % 4
        rows = pl.ds(pl.multiple_of(chunk * QUARTER, QUARTER), QUARTER)
        a, b = keep[rows], recv[rows]
        out[:QUARTER] = late * jnp.where(flip, b, a) + jnp.where(flip, a, b)
        out[QUARTER:] = decay


def ordered(place, axis, refs, j):
    shift = (place[axis] - j + 4) % 4
    value = refs[0][...]
    for s in (1, 2, 3):
        value = jnp.where(shift == s, refs[s][...], value)
    return value


def line_kernel(place, u0, u1, u2, u3, total):
    state = jnp.zeros((QUARTER, HALF), F32)
    decay = jnp.ones((8, HALF), F32)
    for j in range(4):
        u = ordered(place, X, (u0, u1, u2, u3), j)
        state = u[QUARTER : QUARTER + 1] * state + u[:QUARTER]
        decay = decay * u[QUARTER:]
    total[:QUARTER] = state
    total[QUARTER:] = decay


def plane_kernel(place, v0, v1, v2, v3, total, before):
    state = jnp.zeros((QUARTER, HALF), F32)
    decay = jnp.ones((8, HALF), F32)
    for j in range(4):

        @pl.when(place[Y] == j)
        def _(state=state, decay=decay):
            before[:QUARTER] = state
            before[QUARTER:] = decay

        v = ordered(place, Y, (v0, v1, v2, v3), j)
        state = v[QUARTER : QUARTER + 1] * state + v[:QUARTER]
        decay = decay * v[QUARTER:]
    total[:QUARTER] = state
    total[QUARTER:] = decay


def enter_kernel(place, w0, w1, w2, w3, before, u0, u1, u2, u3, own, *sends):
    state = jnp.zeros((QUARTER, HALF), F32)
    for j in range(3):
        w = ordered(place, Z, (w0, w1, w2, w3), j)
        updated = w[QUARTER : QUARTER + 1] * state + w[:QUARTER]
        state = jnp.where(j < place[Z], updated, state)
    state = before[QUARTER : QUARTER + 1] * state + before[:QUARTER]
    for j in range(4):
        for shift, out in enumerate((own,) + sends):

            @pl.when((place[X] + shift) % 4 == j)
            def _(state=state, out=out):
                out[...] = state

        if j < 3:
            u = ordered(place, X, (u0, u1, u2, u3), j)
            state = u[QUARTER : QUARTER + 1] * state + u[:QUARTER]


def chip_kernel(place, e0, e1, e2, e3, keep, recv, own, send):
    flip = place[CORE] == 1
    first = jnp.where(flip, recv[STATE : STATE + 1], keep[STATE : STATE + 1])
    for shift, e in enumerate((e0, e1, e2, e3)):
        chunk = (place[X] - shift + 4) % 4
        rows = pl.ds(pl.multiple_of(chunk * QUARTER, QUARTER), QUARTER)
        at_first = e[...]
        at_second = first * at_first + jnp.where(flip, recv[rows], keep[rows])
        own[rows] = jnp.where(flip, at_second, at_first)
        send[rows] = jnp.where(flip, at_first, at_second)


def output_kernel(
    core_ref, x_ref, gate_ref, b_ref, c_ref, decay_ref, spread_ref, skip_ref, gain_ref, own_ref, other_ref,
    out_ref, state,
):
    @pl.when(pl.program_id(0) == 0)
    def _():
        mine = pl.multiple_of(core_ref[0] * HALF, HALF)
        other = pl.multiple_of((1 - core_ref[0]) * HALF, HALF)
        state[:, pl.ds(mine, HALF)] = own_ref[...]
        state[:, pl.ds(other, HALF)] = other_ref[...]

    row, col = iota((SUB, SUB), 0), iota((SUB, SUB), 1)
    causal = col <= row
    upto = jnp.where(causal, 1.0, 0.0).astype(BF16)
    same = iota((GROUP, GROUP), 0) // HEAD == iota((GROUP, GROUP), 1) // HEAD
    mean = jnp.where(same, 1.0 / HEAD, 0.0).astype(BF16)
    down = 2.0**-SHIFT
    for s in range(STEP // SUB):
        rows = slice(s * SUB, (s + 1) * SUB)
        decay = decay_ref[:, rows]
        cumul = decay_sums(upto, jnp.concatenate([decay] * 3, axis=0))
        at_end = cumul[SUB - 1 : SUB] + SHIFT_LOG
        exponents = jnp.concatenate([at_end - cumul, cumul - at_end, jnp.broadcast_to(at_end, (16, 3 * HEADS))], axis=0)
        factors = spread_parts(jnp.exp(exponents))
        b, c = b_ref[rows], c_ref[rows]
        scores = jnp.where(causal, dot(c, b, ((1,), (1,))), 0.0).astype(BF16)
        b_t = jnp.transpose(b.astype(F32)).astype(BF16)
        upper = jnp.concatenate([scores, c], axis=1)
        lower = jnp.concatenate([b_t, jnp.zeros((STATE, STATE), BF16)], axis=1)
        left = jnp.concatenate([upper, lower], axis=0)
        for g in range(WIDTH // GROUP):
            lanes = slice(g * GROUP, (g + 1) * GROUP)
            wide = dot(factors, spread_ref[:, lanes])
            x = x_ref[rows, lanes].astype(F32)
            scaled = (x * wide[:SUB]).astype(BF16)
            carried = state[:, lanes] * wide[2 * SUB : 2 * SUB + 1]
            both = dot(left, jnp.concatenate([scaled, carried.astype(BF16)], axis=0))
            state[:, lanes] = (carried + both[SUB:]) * down
            summed = both[:SUB] * wide[SUB : 2 * SUB] + skip_ref[:, lanes] * x
            h = 0.5 * gate_ref[rows, lanes].astype(F32)
            gated = summed * (h + h * jnp.tanh(h))
            square = dot((gated * gated).astype(BF16), mean)
            out = gated * lax.rsqrt(square + 1e-5) * gain_ref[:, lanes]
            out_ref[rows, lanes] = out.astype(BF16)


def output(core, x, gate, b, c, decay, spread, skip, gain, own, other):
    tokens = x.shape[0]
    wide = pl.BlockSpec((STEP, WIDTH), lambda i, c: (i, 0))
    narrow = pl.BlockSpec((STEP, STATE), lambda i, c: (i, 0))
    line = pl.BlockSpec((1, WIDTH), lambda i, c: (0, 0))
    half = pl.BlockSpec((STATE, HALF), lambda i, c: (0, 0))
    return pl.pallas_call(
        output_kernel,
        grid_spec=pltpu.PrefetchScalarGridSpec(
            num_scalar_prefetch=1,
            grid=(tokens // STEP,),
            in_specs=[
                wide, wide, narrow, narrow,
                pl.BlockSpec((HEADS, STEP), lambda i, c: (0, i)),
                pl.BlockSpec((3 * HEADS, WIDTH), lambda i, c: (0, 0)),
                line, line, half, half,
            ],
            out_specs=wide,
            scratch_shapes=[pltpu.VMEM((STATE, WIDTH), F32)],
        ),
        out_shape=jax.ShapeDtypeStruct((tokens, WIDTH), BF16),
        name="output",
        compiler_params=pltpu.CompilerParams(vmem_limit_bytes=40 * 1024 * 1024),
    )(core, x, gate, b, c, decay, spread, skip, gain, own, other)


def device_of(z, y, x, core):
    return ((z * 4 + y) * 4 + x) * 2 + core


def moved(value, axis, shift):
    sizes = (4, 4, 4, 2)
    pairs = []
    for z in range(4):
        for y in range(4):
            for x in range(4):
                for core in range(2):
                    to = [z, y, x, core]
                    to[axis] = (to[axis] + shift) % sizes[axis]
                    pairs.append((device_of(z, y, x, core), device_of(*to)))
    return lax.ppermute(value, ("grp", "dev"), pairs)


def on_device(x, gate, b, c, decay, d_skip, norm_gain):
    z, r = lax.axis_index("grp"), lax.axis_index("dev")
    place = jnp.stack([z, r // 8, (r // 2) % 4, r % 2]).astype(jnp.int32)
    core = place[CORE:]
    spread = spread_matrix()
    piece, chunk = (QUARTER + 8, HALF), (QUARTER, HALF)

    keep, send = end_state(core, x, b, decay, spread)
    recv = moved(send, CORE, 1)
    u0, *sends = small_call(pair_kernel, "pair", place, (keep, recv), [piece] * 4)
    lines = [u0] + [moved(v, X, s + 1) for s, v in enumerate(sends)]
    (v0,) = small_call(line_kernel, "line", place, lines, [piece])
    columns = [v0] + [moved(v0, Y, s) for s in (1, 2, 3)]
    w0, before = small_call(plane_kernel, "plane", place, columns, [piece] * 2)
    planes = [w0] + [moved(w0, Z, s) for s in (1, 2, 3)]
    e0, *sends = small_call(enter_kernel, "enter", place, planes + [before] + lines, [chunk] * 4)
    entering = [e0] + [moved(v, X, s + 1) for s, v in enumerate(sends)]
    own, send = small_call(chip_kernel, "chip", place, entering + [keep, recv], [(STATE, HALF)] * 2)
    other = moved(send, CORE, 1)
    skip = jnp.repeat(d_skip, HEAD)[None]
    return output(core, x, gate, b, c, decay, spread, skip, norm_gain[None], own, other)


def solution(mesh):
    return jax.shard_map(
        on_device,
        mesh=mesh,
        in_specs=(
            P(("grp", "dev"), None),
            P(("grp", "dev"), None),
            P(("grp", "dev"), None),
            P(("grp", "dev"), None),
            P(None, ("grp", "dev")),
            P(),
            P(),
        ),
        out_specs=P(("grp", "dev"), None),
        check_vma=False,
    )
```

time: 720 us -> 121 us (0.17)
  the two profiles are of different devices: /device:TPU:96 before, /device:TPU:1 now
where the time goes in v1:
time: 121 us; the launch traced here: 120 us
  Pallas kernels  59.7 us (49%)
  waiting for transfers between devices  27 us (22%)
  starting transfers between devices  19.8 us (16%)
  local copies, waits for them, and re-layouts  12.8 us (11%)
    pallas_call x1, Pallas kernels, output(): pl.pallas_call(output_kernel, grid_spec=pltpu.PrefetchScalarGridSpec(num_...  35 us
    ppermute x14, waiting for transfers between devices, moved(): return lax.ppermute(value, ('grp', 'dev'), pairs)  27 us
    ppermute x14, starting transfers between devices, moved(): return lax.ppermute(value, ('grp', 'dev'), pairs)  19.8 us
    pallas_call x1, Pallas kernels, end_state(): pl.pallas_call(end_state_kernel, grid_spec=pltpu.PrefetchScalarGridSpec(n...  14.1 us
    unnamed x48, local copies, waits for them, and re-layouts  12.7 us
    pallas_call x5, Pallas kernels, small_call(): pl.pallas_call(kernel, in_specs=[pl.BlockSpec(memory_space=pltpu.SMEM)] +...  10.6 us
  transfers between devices with their start and end apart: 14, of which 13 were waited for; matrix products, arithmetic and copies ran while one was open for 1% of the time, Pallas kernels for 0%

profile of v1, /device:TPU:1, one launch (start us, length us, event | category | flops | bytes accessed | tf_op | source)
XLA Modules:
  0.0 120.3 jit_solution(1208966960524181409)
XLA Ops:
  0.1 0.1 select_convert_fusion.spread_ref
  0.2 0.0 copy-start
  0.2 2.8 %copy-done = bf16[2048,1536]{1,0:T(8,128)(2,1)S(1)} copy-done((bf16[2048,1536]{1,0:T(8,128)(2,1)S(1)}, bf16[2048,1536]{1,0:T(8,128)(2,1)}, u32[]{:S(2)}) %copy-start) | copy-done | bytes 6291480
  3.0 1.0 copy-done.2
  4.0 0.9 copy-done.5
  4.9 14.1 %end_state.1 = (f32[136,768]{1,0:T(8,128)S(1)}, f32[136,768]{1,0:T(8,128)S(1)}) custom-call(s32[1]{0:T(128)} %bitcast.core_ref, bf16[2048,1536]{1,0:T(8,128)(2,1)S(1)} %copy-done, bf16[2048,128]{1,0:T(8,128)(2,1)S(1)} %copy-done.2, f32[24,2048]{1,0:T(8,128)S(1)} %copy-done.5, bf16[72,1536]{1,0:T(8,128)(2,1)S(1)} %select_convert_fusion.spread_ref), custom_call_target="tpu_custom_call" | custom-call | tf_op jit(solution)/shard_map/end_state/pallas_call | solution.py:96
  19.0 0.0 copy-start.4
  19.0 0.7 copy-done.4
  19.8 1.4 %collective-permute-start = (f32[136,768]{1,0:T(8,128)S(1)}, f32[136,768]{1,0:T(8,128)S(1)}, u32[]{:S(2)}, u32[]{:S(2)}) collective-permute-start(f32[136,768]{1,0:T(8,128)S(1)} %get-tuple-element.20), channel_id=1, source_target_pairs={{0,1},{1,0},{2,3},{3,2},{4,5},{5,4},{6,7},{7,6},{8,9},{9,8},{10,11... | collective-permute-start | bytes 1253384 | tf_op jit(solution)/shard_map/ppermute | solution.py:299
  21.2 0.7 pad_add_fusion.place
  21.8 0.7 collective-permute-done.recv
  22.6 0.7 copy-done.9
  23.3 2.0 %pair.1 = (f32[40,768]{1,0:T(8,128)}, f32[40,768]{1,0:T(8,128)}, f32[40,768]{1,0:T(8,128)}, f32[40,768]{1,0:T(8,128)}) custom-call(s32[4]{0:T(128)} %pad_add_fusion.place, f32[136,768]{1,0:T(8,128)} %copy-done.4, f32[136,768]{1,0:T(8,128)} %copy-done.9), custom_call_target="tpu_custom_call" | custom-call | tf_op jit(solution)/shard_map/pair/pallas_call | solution.py:121
  25.3 1.3 %collective-permute-start.1 = (f32[40,768]{1,0:T(8,128)}, f32[40,768]{1,0:T(8,128)S(1)}, u32[]{:S(2)}, u32[]{:S(2)}) collective-permute-start(f32[40,768]{1,0:T(8,128)} %get-tuple-element.22), channel_id=1, source_target_pairs={{0,2},{1,3},{2,4},{3,5},{4,6},{5,7},{6,0},{7,1},{8,10},{9,11},{10,... | collective-permute-start | bytes 368648 | tf_op jit(solution)/shard_map/ppermute | solution.py:299
  26.6 2.5 %collective-permute-start.2 = (f32[40,768]{1,0:T(8,128)}, f32[40,768]{1,0:T(8,128)S(1)}, u32[]{:S(2)}, u32[]{:S(2)}) collective-permute-start(f32[40,768]{1,0:T(8,128)} %get-tuple-element.23), channel_id=1, source_target_pairs={{0,4},{1,5},{2,6},{3,7},{4,0},{5,1},{6,2},{7,3},{8,12},{9,13},{10,... | collective-permute-start | bytes 368648 | tf_op jit(solution)/shard_map/ppermute | solution.py:299
  29.1 1.1 collective-permute-start.3
  30.2 1.0 collective-permute-done.1.u1
  31.3 3.7 %collective-permute-done.2.u2 = f32[40,768]{1,0:T(8,128)S(1)} collective-permute-done((f32[40,768]{1,0:T(8,128)}, f32[40,768]{1,0:T(8,128)S(1)}, u32[]{:S(2)}, u32[]{:S(2)}) %collective-permute-start.2) | collective-permute-done | bytes 122912 | tf_op jit(solution)/shard_map/ppermute | solution.py:299
  35.0 0.0 collective-permute-done.3.u3
  35.0 0.0 copy-done.10
  35.0 0.6 copy-done.11
  35.6 0.0 copy-done.12
  35.7 1.8 %line.1.v0 = f32[40,768]{1,0:T(8,128)} custom-call(s32[4]{0:T(128)} %pad_add_fusion.place, f32[40,768]{1,0:T(8,128)} %get-tuple-element.21.u0, f32[40,768]{1,0:T(8,128)} %copy-done.10, f32[40,768]{1,0:T(8,128)} %copy-done.11, f32[40,768]{1,0:T(8,128)} %copy-done.12), custom_call_target="tpu_custom_call" | custom-call | tf_op jit(solution)/shard_map/line/pallas_call | solution.py:121
  37.5 2.7 %collective-permute-start.6 = (f32[40,768]{1,0:T(8,128)}, f32[40,768]{1,0:T(8,128)S(1)}, u32[]{:S(2)}, u32[]{:S(2)}) collective-permute-start(f32[40,768]{1,0:T(8,128)} %line.1.v0), channel_id=1, source_target_pairs={{0,24},{1,25},{2,26},{3,27},{4,28},{5,29},{6,30},{7,31},{8,0},{9,1... | collective-permute-start | bytes 368648 | tf_op jit(solution)/shard_map/ppermute | solution.py:299
  40.3 0.4 collective-permute-start.5
  40.6 0.7 collective-permute-start.4
  41.3 1.6 %collective-permute-done.6.v3 = f32[40,768]{1,0:T(8,128)S(1)} collective-permute-done((f32[40,768]{1,0:T(8,128)}, f32[40,768]{1,0:T(8,128)S(1)}, u32[]{:S(2)}, u32[]{:S(2)}) %collective-permute-start.6) | collective-permute-done | bytes 122912 | tf_op jit(solution)/shard_map/ppermute | solution.py:299
  42.9 2.9 %collective-permute-done.5.v2 = f32[40,768]{1,0:T(8,128)S(1)} collective-permute-done((f32[40,768]{1,0:T(8,128)}, f32[40,768]{1,0:T(8,128)S(1)}, u32[]{:S(2)}, u32[]{:S(2)}) %collective-permute-start.5) | collective-permute-done | bytes 122912 | tf_op jit(solution)/shard_map/ppermute | solution.py:299
  45.8 3.2 %collective-permute-done.4.v1 = f32[40,768]{1,0:T(8,128)S(1)} collective-permute-done((f32[40,768]{1,0:T(8,128)}, f32[40,768]{1,0:T(8,128)S(1)}, u32[]{:S(2)}, u32[]{:S(2)}) %collective-permute-start.4) | collective-permute-done | bytes 122912 | tf_op jit(solution)/shard_map/ppermute | solution.py:299
  49.1 0.0 copy-done.13
  49.1 0.0 copy-done.14
  49.1 0.7 copy-done.15
  49.7 1.9 %plane.1 = (f32[40,768]{1,0:T(8,128)}, f32[40,768]{1,0:T(8,128)}) custom-call(s32[4]{0:T(128)} %pad_add_fusion.place, f32[40,768]{1,0:T(8,128)} %line.1.v0, f32[40,768]{1,0:T(8,128)} %copy-done.15, f32[40,768]{1,0:T(8,128)} %copy-done.14, f32[40,768]{1,0:T(8,128)} %copy-done.13), custom_call_target="tpu_custom_call" | custom-call | tf_op jit(solution)/shard_map/plane/pallas_call | solution.py:121
  51.6 3.8 %collective-permute-start.9 = (f32[40,768]{1,0:T(8,128)}, f32[40,768]{1,0:T(8,128)S(1)}, u32[]{:S(2)}, u32[]{:S(2)}) collective-permute-start(f32[40,768]{1,0:T(8,128)} %get-tuple-element.25.w0), channel_id=1, source_target_pairs={{0,96},{1,97},{2,98},{3,99},{4,100},{5,101},{6,102},{7,103},{8,104... | collective-permute-start | bytes 368648 | tf_op jit(solution)/shard_map/ppermute | solution.py:299
  55.4 0.0 collective-permute-start.8
  55.4 0.7 collective-permute-start.7
  56.1 4.6 %collective-permute-done.9.w3 = f32[40,768]{1,0:T(8,128)S(1)} collective-permute-done((f32[40,768]{1,0:T(8,128)}, f32[40,768]{1,0:T(8,128)S(1)}, u32[]{:S(2)}, u32[]{:S(2)}) %collective-permute-start.9) | collective-permute-done | bytes 122912 | tf_op jit(solution)/shard_map/ppermute | solution.py:299
  60.7 0.2 collective-permute-done.8.w2
  60.9 3.1 %collective-permute-done.7.w1 = f32[40,768]{1,0:T(8,128)S(1)} collective-permute-done((f32[40,768]{1,0:T(8,128)}, f32[40,768]{1,0:T(8,128)S(1)}, u32[]{:S(2)}, u32[]{:S(2)}) %collective-permute-start.7) | collective-permute-done | bytes 122912 | tf_op jit(solution)/shard_map/ppermute | solution.py:299
  64.0 0.0 copy-done.16
  64.0 0.0 copy-done.17
  64.0 0.6 copy-done.18
  64.7 2.5 %enter.1 = (f32[32,768]{1,0:T(8,128)}, f32[32,768]{1,0:T(8,128)}, f32[32,768]{1,0:T(8,128)}, f32[32,768]{1,0:T(8,128)}) custom-call(s32[4]{0:T(128)} %pad_add_fusion.place, f32[40,768]{1,0:T(8,128)} %get-tuple-element.25.w0, f32[40,768]{1,0:T(8,128)} %copy-done.18, f32[40,768]{1,0:T(8,128)} %copy-done.17, f32[40,768]{1,0:T(8,128)} %copy-done.16, ...), custom_call_target="tpu_custom_call" | custom-call | tf_op jit(solution)/shard_map/enter/pallas_call | solution.py:121
  67.1 0.9 collective-permute-start.10
  68.1 2.3 %collective-permute-start.11 = (f32[32,768]{1,0:T(8,128)}, f32[32,768]{1,0:T(8,128)S(1)}, u32[]{:S(2)}, u32[]{:S(2)}) collective-permute-start(f32[32,768]{1,0:T(8,128)} %get-tuple-element.29), channel_id=1, source_target_pairs={{0,4},{1,5},{2,6},{3,7},{4,0},{5,1},{6,2},{7,3},{8,12},{9,13},{10,... | collective-permute-start | bytes 294920 | tf_op jit(solution)/shard_map/ppermute | solution.py:299
  70.4 0.2 collective-permute-start.12
  70.6 1.5 %collective-permute-done.10.e1 = f32[32,768]{1,0:T(8,128)S(1)} collective-permute-done((f32[32,768]{1,0:T(8,128)}, f32[32,768]{1,0:T(8,128)S(1)}, u32[]{:S(2)}, u32[]{:S(2)}) %collective-permute-start.10) | collective-permute-done | bytes 98336 | tf_op jit(solution)/shard_map/ppermute | solution.py:299
  72.0 2.1 %collective-permute-done.11.e2 = f32[32,768]{1,0:T(8,128)S(1)} collective-permute-done((f32[32,768]{1,0:T(8,128)}, f32[32,768]{1,0:T(8,128)S(1)}, u32[]{:S(2)}, u32[]{:S(2)}) %collective-permute-start.11) | collective-permute-done | bytes 98336 | tf_op jit(solution)/shard_map/ppermute | solution.py:299
  74.1 0.9 collective-permute-done.12.e3
  75.1 0.0 copy-done.19
  75.1 0.0 copy-done.20
  75.1 0.6 copy-done.21
  75.7 2.4 %chip.1 = (f32[128,768]{1,0:T(8,128)}, f32[128,768]{1,0:T(8,128)}) custom-call(s32[4]{0:T(128)} %pad_add_fusion.place, f32[32,768]{1,0:T(8,128)} %get-tuple-element.27.e0, f32[32,768]{1,0:T(8,128)} %copy-done.19, f32[32,768]{1,0:T(8,128)} %copy-done.20, f32[32,768]{1,0:T(8,128)} %copy-done.21, f32[136,768]{1,0:T(8,128)} %copy-done.4, f32[136,768]{1,0:T(8,128)} %copy-done.9), custom_call_target="tpu_custom_call" | custom-call | tf_op jit(solution)/shard_map/chip/pallas_call | solution.py:121
  78.1 1.8 %collective-permute-start.13 = (f32[128,768]{1,0:T(8,128)}, f32[128,768]{1,0:T(8,128)S(1)}, u32[]{:S(2)}, u32[]{:S(2)}) collective-permute-start(f32[128,768]{1,0:T(8,128)} %get-tuple-element.32), channel_id=1, source_target_pairs={{0,1},{1,0},{2,3},{3,2},{4,5},{5,4},{6,7},{7,6},{8,9},{9,8},{10,11... | collective-permute-start | bytes 1179656 | tf_op jit(solution)/shard_map/ppermute | solution.py:299
  79.9 0.0 copy-done.22
  79.9 0.0 copy-done.23
  79.9 0.1 broadcast_in_dim.16
  80.0 0.1 broadcast_in_dim_reshape.3.skip_ref
  80.1 1.4 %collective-permute-done.13.other_ref = f32[128,768]{1,0:T(8,128)S(1)} collective-permute-done((f32[128,768]{1,0:T(8,128)}, f32[128,768]{1,0:T(8,128)S(1)}, u32[]{:S(2)}, u32[]{:S(2)}) %collective-permute-start.13) | collective-permute-done | bytes 393248 | tf_op jit(solution)/shard_map/ppermute | solution.py:299
  81.5 0.0 copy-done.6
  81.5 0.0 copy-done.3
  81.5 2.8 %copy-done.1 = bf16[2048,1536]{1,0:T(8,128)(2,1)S(1)} copy-done((bf16[2048,1536]{1,0:T(8,128)(2,1)S(1)}, bf16[2048,1536]{1,0:T(8,128)(2,1)}, u32[]{:S(2)}) %copy-start.1) | copy-done | bytes 6291480
  84.3 1.0 copy-done.8
  85.3 35.0 %output.1 = bf16[2048,1536]{1,0:T(8,128)(2,1)} custom-call(s32[1]{0:T(128)} %bitcast.core_ref, bf16[2048,1536]{1,0:T(8,128)(2,1)S(1)} %copy-done.1, bf16[2048,1536]{1,0:T(8,128)(2,1)} %gate_ref.1, bf16[2048,128]{1,0:T(8,128)(2,1)S(1)} %copy-done.3, bf16[2048,128]{1,0:T(8,128)(2,1)S(1)} %copy-done.7, f32[24,2048]{1,0:T(8,128)S(1)} %copy-done.6, ...), custom_call_target="tpu_custom_call" | custom-call | tf_op jit(solution)/shard_map/output/pallas_call | solution.py:265
  (26 shorter events, 0.1 us)
Async XLA Ops:
  0.0 81.5 %copy-start.6 = (f32[24,2048]{1,0:T(8,128)S(1)}, f32[24,2048]{1,0:T(8,128)}, u32[]{:S(2)}) copy-start(f32[24,2048]{1,0:T(8,128)} %decay_ref.3) | copy-start | bytes 589828
  0.0 79.9 %copy-start.22 = (f32[1536]{0:T(1024)S(1)}, f32[1536]{0:T(1024)}, u32[]{:S(2)}) copy-start(f32[1536]{0:T(1024)} %param.13) | copy-start | bytes 18436
  0.0 79.9 %copy-start.23 = (f32[24]{0:T(128)S(1)}, f32[24]{0:T(128)}, u32[]{:S(2)}) copy-start(f32[24]{0:T(128)} %param.12) | copy-start | bytes 292
  0.2 2.8 %copy-start = (bf16[2048,1536]{1,0:T(8,128)(2,1)S(1)}, bf16[2048,1536]{1,0:T(8,128)(2,1)}, u32[]{:S(2)}) copy-start(bf16[2048,1536]{1,0:T(8,128)(2,1)} %x_ref.3) | copy-start | bytes 18874372
  3.0 1.0 copy-start.2
  4.0 0.9 copy-start.5
  4.9 76.5 %copy-start.3 = (bf16[2048,128]{1,0:T(8,128)(2,1)S(1)}, bf16[2048,128]{1,0:T(8,128)(2,1)}, u32[]{:S(2)}) copy-start(bf16[2048,128]{1,0:T(8,128)(2,1)} %b_ref.3) | copy-start | bytes 1572868
  4.9 76.5 %copy-start.7 = (bf16[2048,128]{1,0:T(8,128)(2,1)S(1)}, bf16[2048,128]{1,0:T(8,128)(2,1)}, u32[]{:S(2)}) copy-start(bf16[2048,128]{1,0:T(8,128)(2,1)} %c_ref.1) | copy-start | bytes 1572868
  19.0 0.8 copy-start.4
  19.8 2.8 %collective-permute-start = (f32[136,768]{1,0:T(8,128)S(1)}, f32[136,768]{1,0:T(8,128)S(1)}, u32[]{:S(2)}, u32[]{:S(2)}) collective-permute-start(f32[136,768]{1,0:T(8,128)S(1)} %get-tuple-element.20), channel_id=1, source_target_pairs={{0,1},{1,0},{2,3},{3,2},{4,5},{5,4},{6,7},{7,6},{8,9},{9,8},{10,11... | collective-permute-start | bytes 1253384 | tf_op jit(solution)/shard_map/ppermute | solution.py:299
  22.6 0.8 copy-start.9
  25.3 6.0 %collective-permute-start.1 = (f32[40,768]{1,0:T(8,128)}, f32[40,768]{1,0:T(8,128)S(1)}, u32[]{:S(2)}, u32[]{:S(2)}) collective-permute-start(f32[40,768]{1,0:T(8,128)} %get-tuple-element.22), channel_id=1, source_target_pairs={{0,2},{1,3},{2,4},{3,5},{4,6},{5,7},{6,0},{7,1},{8,10},{9,11},{10,... | collective-permute-start | bytes 368648 | tf_op jit(solution)/shard_map/ppermute | solution.py:299
  26.6 8.4 %collective-permute-start.2 = (f32[40,768]{1,0:T(8,128)}, f32[40,768]{1,0:T(8,128)S(1)}, u32[]{:S(2)}, u32[]{:S(2)}) collective-permute-start(f32[40,768]{1,0:T(8,128)} %get-tuple-element.23), channel_id=1, source_target_pairs={{0,4},{1,5},{2,6},{3,7},{4,0},{5,1},{6,2},{7,3},{8,12},{9,13},{10,... | collective-permute-start | bytes 368648 | tf_op jit(solution)/shard_map/ppermute | solution.py:299
  29.1 5.9 %collective-permute-start.3 = (f32[40,768]{1,0:T(8,128)}, f32[40,768]{1,0:T(8,128)S(1)}, u32[]{:S(2)}, u32[]{:S(2)}) collective-permute-start(f32[40,768]{1,0:T(8,128)} %get-tuple-element.24), channel_id=1, source_target_pairs={{0,6},{1,7},{2,0},{3,1},{4,2},{5,3},{6,4},{7,5},{8,14},{9,15},{10,... | collective-permute-start | bytes 368648 | tf_op jit(solution)/shard_map/ppermute | solution.py:299
  31.3 3.7 %copy-start.10 = (f32[40,768]{1,0:T(8,128)}, f32[40,768]{1,0:T(8,128)S(1)}, u32[]{:S(2)}) copy-start(f32[40,768]{1,0:T(8,128)S(1)} %collective-permute-done.1.u1) | copy-start | bytes 368644
  35.0 0.7 copy-start.11
  35.0 0.7 copy-start.12
  37.5 5.3 %collective-permute-start.6 = (f32[40,768]{1,0:T(8,128)}, f32[40,768]{1,0:T(8,128)S(1)}, u32[]{:S(2)}, u32[]{:S(2)}) collective-permute-start(f32[40,768]{1,0:T(8,128)} %line.1.v0), channel_id=1, source_target_pairs={{0,24},{1,25},{2,26},{3,27},{4,28},{5,29},{6,30},{7,31},{8,0},{9,1... | collective-permute-start | bytes 368648 | tf_op jit(solution)/shard_map/ppermute | solution.py:299
  40.3 5.5 %collective-permute-start.5 = (f32[40,768]{1,0:T(8,128)}, f32[40,768]{1,0:T(8,128)S(1)}, u32[]{:S(2)}, u32[]{:S(2)}) collective-permute-start(f32[40,768]{1,0:T(8,128)} %line.1.v0), channel_id=1, source_target_pairs={{0,16},{1,17},{2,18},{3,19},{4,20},{5,21},{6,22},{7,23},{8,24},{9,... | collective-permute-start | bytes 368648 | tf_op jit(solution)/shard_map/ppermute | solution.py:299
  40.6 8.4 %collective-permute-start.4 = (f32[40,768]{1,0:T(8,128)}, f32[40,768]{1,0:T(8,128)S(1)}, u32[]{:S(2)}, u32[]{:S(2)}) collective-permute-start(f32[40,768]{1,0:T(8,128)} %line.1.v0), channel_id=1, source_target_pairs={{0,8},{1,9},{2,10},{3,11},{4,12},{5,13},{6,14},{7,15},{8,16},{9,17... | collective-permute-start | bytes 368648 | tf_op jit(solution)/shard_map/ppermute | solution.py:299
  42.9 6.2 %copy-start.13 = (f32[40,768]{1,0:T(8,128)}, f32[40,768]{1,0:T(8,128)S(1)}, u32[]{:S(2)}) copy-start(f32[40,768]{1,0:T(8,128)S(1)} %collective-permute-done.6.v3) | copy-start | bytes 368644
  45.8 3.3 %copy-start.14 = (f32[40,768]{1,0:T(8,128)}, f32[40,768]{1,0:T(8,128)S(1)}, u32[]{:S(2)}) copy-start(f32[40,768]{1,0:T(8,128)S(1)} %collective-permute-done.5.v2) | copy-start | bytes 368644
  49.1 0.7 copy-start.15
  51.6 9.1 %collective-permute-start.9 = (f32[40,768]{1,0:T(8,128)}, f32[40,768]{1,0:T(8,128)S(1)}, u32[]{:S(2)}, u32[]{:S(2)}) collective-permute-start(f32[40,768]{1,0:T(8,128)} %get-tuple-element.25.w0), channel_id=1, source_target_pairs={{0,96},{1,97},{2,98},{3,99},{4,100},{5,101},{6,102},{7,103},{8,104... | collective-permute-start | bytes 368648 | tf_op jit(solution)/shard_map/ppermute | solution.py:299
  55.4 5.5 %collective-permute-start.8 = (f32[40,768]{1,0:T(8,128)}, f32[40,768]{1,0:T(8,128)S(1)}, u32[]{:S(2)}, u32[]{:S(2)}) collective-permute-start(f32[40,768]{1,0:T(8,128)} %get-tuple-element.25.w0), channel_id=1, source_target_pairs={{0,64},{1,65},{2,66},{3,67},{4,68},{5,69},{6,70},{7,71},{8,72},{9,... | collective-permute-start | bytes 368648 | tf_op jit(solution)/shard_map/ppermute | solution.py:299
  55.4 8.6 %collective-permute-start.7 = (f32[40,768]{1,0:T(8,128)}, f32[40,768]{1,0:T(8,128)S(1)}, u32[]{:S(2)}, u32[]{:S(2)}) collective-permute-start(f32[40,768]{1,0:T(8,128)} %get-tuple-element.25.w0), channel_id=1, source_target_pairs={{0,32},{1,33},{2,34},{3,35},{4,36},{5,37},{6,38},{7,39},{8,40},{9,... | collective-permute-start | bytes 368648 | tf_op jit(solution)/shard_map/ppermute | solution.py:299
  60.7 3.3 %copy-start.16 = (f32[40,768]{1,0:T(8,128)}, f32[40,768]{1,0:T(8,128)S(1)}, u32[]{:S(2)}) copy-start(f32[40,768]{1,0:T(8,128)S(1)} %collective-permute-done.9.w3) | copy-start | bytes 368644
  60.9 3.1 %copy-start.17 = (f32[40,768]{1,0:T(8,128)}, f32[40,768]{1,0:T(8,128)S(1)}, u32[]{:S(2)}) copy-start(f32[40,768]{1,0:T(8,128)S(1)} %collective-permute-done.8.w2) | copy-start | bytes 368644
  64.0 0.6 copy-start.18
  67.1 4.9 %collective-permute-start.10 = (f32[32,768]{1,0:T(8,128)}, f32[32,768]{1,0:T(8,128)S(1)}, u32[]{:S(2)}, u32[]{:S(2)}) collective-permute-start(f32[32,768]{1,0:T(8,128)} %get-tuple-element.28), channel_id=1, source_target_pairs={{0,2},{1,3},{2,4},{3,5},{4,6},{5,7},{6,0},{7,1},{8,10},{9,11},{10,... | collective-permute-start | bytes 294920 | tf_op jit(solution)/shard_map/ppermute | solution.py:299
  68.1 6.0 %collective-permute-start.11 = (f32[32,768]{1,0:T(8,128)}, f32[32,768]{1,0:T(8,128)S(1)}, u32[]{:S(2)}, u32[]{:S(2)}) collective-permute-start(f32[32,768]{1,0:T(8,128)} %get-tuple-element.29), channel_id=1, source_target_pairs={{0,4},{1,5},{2,6},{3,7},{4,0},{5,1},{6,2},{7,3},{8,12},{9,13},{10,... | collective-permute-start | bytes 294920 | tf_op jit(solution)/shard_map/ppermute | solution.py:299
  70.4 4.7 %collective-permute-start.12 = (f32[32,768]{1,0:T(8,128)}, f32[32,768]{1,0:T(8,128)S(1)}, u32[]{:S(2)}, u32[]{:S(2)}) collective-permute-start(f32[32,768]{1,0:T(8,128)} %get-tuple-element.30), channel_id=1, source_target_pairs={{0,6},{1,7},{2,0},{3,1},{4,2},{5,3},{6,4},{7,5},{8,14},{9,15},{10,... | collective-permute-start | bytes 294920 | tf_op jit(solution)/shard_map/ppermute | solution.py:299
  72.0 3.0 %copy-start.19 = (f32[32,768]{1,0:T(8,128)}, f32[32,768]{1,0:T(8,128)S(1)}, u32[]{:S(2)}) copy-start(f32[32,768]{1,0:T(8,128)S(1)} %collective-permute-done.10.e1) | copy-start | bytes 294916
  74.1 0.9 copy-start.20
  75.1 0.6 copy-start.21
  78.1 3.4 %collective-permute-start.13 = (f32[128,768]{1,0:T(8,128)}, f32[128,768]{1,0:T(8,128)S(1)}, u32[]{:S(2)}, u32[]{:S(2)}) collective-permute-start(f32[128,768]{1,0:T(8,128)} %get-tuple-element.32), channel_id=1, source_target_pairs={{0,1},{1,0},{2,3},{3,2},{4,5},{5,4},{6,7},{7,6},{8,9},{9,8},{10,11... | collective-permute-start | bytes 1179656 | tf_op jit(solution)/shard_map/ppermute | solution.py:299
  81.5 2.8 %copy-start.1 = (bf16[2048,1536]{1,0:T(8,128)(2,1)S(1)}, bf16[2048,1536]{1,0:T(8,128)(2,1)}, u32[]{:S(2)}) copy-start(bf16[2048,1536]{1,0:T(8,128)(2,1)} %x_ref.3) | copy-start | bytes 18874372
  84.3 1.0 copy-start.8

commit v2 on v1

v2 whole, which is shorter than its diff:
```python
import functools

import jax
import jax.numpy as jnp
from jax import lax
from jax.experimental import pallas as pl
from jax.experimental.pallas import tpu as pltpu
from jax.sharding import PartitionSpec as P

HEADS = 24
HEAD = 64
STATE = 128
WIDTH = HEADS * HEAD
HALF = WIDTH // 2
SUB = 128
STEP = 256
GROUP = 256
ROWS = STATE + 8
SHIFT = 74
SHIFT_LOG = 51.29289136
OUT_STEP = 256
QUARTER = STATE // 4
FIRST_LIMIT = 60 * 1024 * 1024
LIMIT = 18 * 1024 * 1024
SMALL_LIMIT = 6 * 1024 * 1024
F32 = jnp.float32
BF16 = jnp.bfloat16


def dot(a, b, dims=((1,), (0,))):
    return lax.dot_general(a, b, (dims, ((), ())), preferred_element_type=F32)


def iota(shape, dim):
    return lax.broadcasted_iota(jnp.int32, shape, dim)


def three(v):
    high = v.astype(BF16)
    rest = v - high.astype(F32)
    middle = rest.astype(BF16)
    low = (rest - middle.astype(F32)).astype(BF16)
    return high, middle, low


def spread_parts(v):
    high, middle, low = three(v)
    lane = iota(v.shape, 1)
    picked = jnp.where(
        lane < HEADS, high.astype(F32), jnp.where(lane < 2 * HEADS, middle.astype(F32), low.astype(F32))
    )
    return picked.astype(BF16)


def decay_sums(matrix, decay):
    high, middle, low = three(decay)
    nt = ((1,), (1,))
    return dot(matrix, high, nt) + (dot(matrix, middle, nt) + dot(matrix, low, nt))


def spread_matrix(start, width):
    k, lane = iota((3 * HEADS, width), 0), start + iota((3 * HEADS, width), 1)
    return jnp.where(k % HEADS == lane // HEAD, 1.0, 0.0).astype(BF16)


def end_state_kernel(place, x_hbm, b_hbm, decay_hbm, keep_ref, send_ref, x, b, decay, scaled, factors, spread, sems):
    steps = x.shape[0] // STEP
    fetch_decay = pltpu.make_async_copy(decay_hbm, decay, sems.at[steps])
    fetch_decay.start()
    copies = []
    for i in range(steps):
        rows = pl.ds(i * STEP, STEP)
        copies.append(pltpu.make_async_copy(x_hbm.at[rows], x.at[rows], sems.at[i]))
        copies[-1].start()
    fetch_b = pltpu.make_async_copy(b_hbm, b, sems.at[steps + 1])
    fetch_b.start()
    spread[...] = spread_matrix(0, WIDTH)
    row, col = iota((STEP + 16, STEP), 0), iota((STEP + 16, STEP), 1)
    later = jnp.where((col > row) | (row >= STEP), 1.0, 0.0).astype(BF16)
    fetch_decay.wait()
    sums = []
    for i in range(steps):
        part = decay[:, i * STEP : (i + 1) * STEP]
        sums.append(decay_sums(later, jnp.concatenate([part] * 3, axis=0)))
    after = jnp.zeros((1, 3 * HEADS), F32)
    for i in reversed(range(steps)):
        factors[i * STEP : (i + 1) * STEP] = spread_parts(jnp.exp(sums[i][:STEP] + after))
        after = after + sums[i][STEP : STEP + 1]
    whole = spread_parts(jnp.exp(jnp.broadcast_to(after, (16, 3 * HEADS))))
    for i in range(steps):
        copies[i].wait()
        rows = slice(i * STEP, (i + 1) * STEP)
        scaled[rows] = (x[rows].astype(F32) * dot(factors[rows], spread[...])).astype(BF16)
    fetch_b.wait()
    mine = pl.multiple_of(place[CORE] * HALF, HALF)
    other = pl.multiple_of((1 - place[CORE]) * HALF, HALF)
    for start, out in ((other, send_ref), (mine, keep_ref)):
        lanes = pl.ds(start, HALF)
        out[:STATE] = dot(b[...], scaled[:, lanes], ((0,), (0,)))
        out[STATE:] = dot(whole, spread[:, lanes])[:8]


def end_state(place, x, b, decay):
    tokens = x.shape[0]
    half = jax.ShapeDtypeStruct((ROWS, HALF), F32)
    vmem = pl.BlockSpec(memory_space=pltpu.VMEM)
    return pl.pallas_call(
        end_state_kernel,
        in_specs=[pl.BlockSpec(memory_space=pltpu.SMEM)] + [pl.BlockSpec(memory_space=pl.ANY)] * 3,
        out_specs=[vmem, vmem],
        out_shape=[half, half],
        scratch_shapes=[
            pltpu.VMEM(x.shape, BF16),
            pltpu.VMEM(b.shape, BF16),
            pltpu.VMEM(decay.shape, F32),
            pltpu.VMEM((tokens, WIDTH), BF16),
            pltpu.VMEM((tokens, 3 * HEADS), BF16),
            pltpu.VMEM((3 * HEADS, WIDTH), BF16),
            pltpu.SemaphoreType.DMA((tokens // STEP + 2,)),
        ],
        name="end_state",
        compiler_params=pltpu.CompilerParams(vmem_limit_bytes=FIRST_LIMIT),
    )(place, x, b, decay)


def small_call(kernel, name, place, args, outs):
    vmem = pl.BlockSpec(memory_space=pltpu.VMEM)
    return pl.pallas_call(
        kernel,
        in_specs=[pl.BlockSpec(memory_space=pltpu.SMEM)] + [vmem] * len(args),
        out_specs=[vmem] * len(outs),
        out_shape=[jax.ShapeDtypeStruct(s, F32) for s in outs],
        name=name,
        compiler_params=pltpu.CompilerParams(vmem_limit_bytes=SMALL_LIMIT),
    )(place, *args)


Z, Y, X, CORE = 0, 1, 2, 3


def pair_kernel(place, keep, recv, own, *sends):
    flip = place[CORE] == 1
    kept, got = keep[STATE : STATE + 8], recv[STATE : STATE + 8]
    late = jnp.where(flip, kept, got)[:1]
    decay = kept * got
    for shift, out in enumerate((own,) + sends):
        chunk = (place[X] + shift) % 4
        rows = pl.ds(pl.multiple_of(chunk * QUARTER, QUARTER), QUARTER)
        a, b = keep[rows], recv[rows]
        out[:QUARTER] = late * jnp.where(flip, b, a) + jnp.where(flip, a, b)
        out[QUARTER:] = decay


def ordered(place, axis, refs, j):
    shift = (place[axis] - j + 4) % 4
    value = refs[0][...]
    for s in (1, 2, 3):
        value = jnp.where(shift == s, refs[s][...], value)
    return value


def line_kernel(place, u0, u1, u2, u3, total):
    state = jnp.zeros((QUARTER, HALF), F32)
    decay = jnp.ones((8, HALF), F32)
    for j in range(4):
        u = ordered(place, X, (u0, u1, u2, u3), j)
        state = u[QUARTER : QUARTER + 1] * state + u[:QUARTER]
        decay = decay * u[QUARTER:]
    total[:QUARTER] = state
    total[QUARTER:] = decay


def plane_kernel(place, v0, v1, v2, v3, total, before):
    state = jnp.zeros((QUARTER, HALF), F32)
    decay = jnp.ones((8, HALF), F32)
    for j in range(4):

        @pl.when(place[Y] == j)
        def _(state=state, decay=decay):
            before[:QUARTER] = state
            before[QUARTER:] = decay

        v = ordered(place, Y, (v0, v1, v2, v3), j)
        state = v[QUARTER : QUARTER + 1] * state + v[:QUARTER]
        decay = decay * v[QUARTER:]
    total[:QUARTER] = state
    total[QUARTER:] = decay


def enter_kernel(place, w0, w1, w2, w3, before, u0, u1, u2, u3, own, *sends):
    state = jnp.zeros((QUARTER, HALF), F32)
    for j in range(3):
        w = ordered(place, Z, (w0, w1, w2, w3), j)
        updated = w[QUARTER : QUARTER + 1] * state + w[:QUARTER]
        state = jnp.where(j < place[Z], updated, state)
    state = before[QUARTER : QUARTER + 1] * state + before[:QUARTER]
    for j in range(4):
        for shift, out in enumerate((own,) + sends):

            @pl.when((place[X] + shift) % 4 == j)
            def _(state=state, out=out):
                out[...] = state

        if j < 3:
            u = ordered(place, X, (u0, u1, u2, u3), j)
            state = u[QUARTER : QUARTER + 1] * state + u[:QUARTER]


def chip_kernel(place, e0, e1, e2, e3, keep, recv, own, send):
    flip = place[CORE] == 1
    first = jnp.where(flip, recv[STATE : STATE + 1], keep[STATE : STATE + 1])
    for shift, e in enumerate((e0, e1, e2, e3)):
        chunk = (place[X] - shift + 4) % 4
        rows = pl.ds(pl.multiple_of(chunk * QUARTER, QUARTER), QUARTER)
        at_first = e[...]
        at_second = first * at_first + jnp.where(flip, recv[rows], keep[rows])
        own[rows] = jnp.where(flip, at_second, at_first)
        send[rows] = jnp.where(flip, at_first, at_second)


FACTORS = 3 * SUB + 16


def prepare_kernel(b_ref, c_ref, decay_ref, left_ref, b_t_ref, factors_ref):
    tokens = b_ref.shape[0]
    row, col = iota((SUB, SUB), 0), iota((SUB, SUB), 1)
    causal = col <= row
    upto = jnp.where(causal, 1.0, 0.0).astype(BF16)
    before = jnp.zeros((1, 3 * HEADS), F32)
    for s in range(tokens // SUB):
        rows = slice(s * SUB, (s + 1) * SUB)
        decay = decay_ref[:, rows]
        cumul = decay_sums(upto, jnp.concatenate([decay] * 3, axis=0))
        end = cumul[SUB - 1 : SUB]
        shifted = end + SHIFT_LOG
        exponents = [shifted - cumul, jnp.broadcast_to(shifted, (16, 3 * HEADS)), cumul - shifted, cumul + before]
        factors_ref[s] = spread_parts(jnp.exp(jnp.concatenate(exponents, axis=0)))
        before = before + end
        b, c = b_ref[rows], c_ref[rows]
        scores = jnp.where(causal, dot(c, b, ((1,), (1,))), 0.0)
        left_ref[rows, :SUB] = scores.astype(BF16)
        left_ref[rows, SUB:] = c
        b_t_ref[rows] = jnp.transpose(b.astype(F32)).astype(BF16)


def prepare(b, c, decay):
    tokens = b.shape[0]
    vmem = pl.BlockSpec(memory_space=pltpu.VMEM)
    return pl.pallas_call(
        prepare_kernel,
        in_specs=[vmem] * 3,
        out_specs=[vmem] * 3,
        out_shape=[
            jax.ShapeDtypeStruct((tokens, SUB + STATE), BF16),
            jax.ShapeDtypeStruct((tokens, SUB), BF16),
            jax.ShapeDtypeStruct((tokens // SUB, FACTORS, 3 * HEADS), BF16),
        ],
        name="prepare",
        compiler_params=pltpu.CompilerParams(vmem_limit_bytes=LIMIT),
    )(b, c, decay)


def local_kernel(group, skip_ref, x_ref, gate_ref, left_ref, b_t_ref, factors_ref, sum_ref, weight_ref, scaled, carried):
    tokens = x_ref.shape[0]
    lanes = slice(group * GROUP, (group + 1) * GROUP)
    spread = spread_matrix(group * GROUP, GROUP)
    lane = iota((1, GROUP), 1)
    skip = jnp.zeros((1, GROUP), F32)
    for h in range(GROUP // HEAD):
        skip = jnp.where(lane // HEAD == h, skip_ref[group * (GROUP // HEAD) + h], skip)
    state = jnp.zeros((STATE, GROUP), F32)
    down = 2.0**-SHIFT
    for s in range(tokens // SUB):
        rows = slice(s * SUB, (s + 1) * SUB)
        wide = dot(factors_ref[s, : SUB + 16], spread)
        scaled[rows] = (x_ref[rows, lanes].astype(F32) * wide[:SUB]).astype(BF16)
        decayed = state * wide[SUB : SUB + 1]
        carried[rows] = decayed.astype(BF16)
        state = (decayed + dot(b_t_ref[rows], scaled[rows])) * down
    for s in range(tokens // SUB):
        rows = slice(s * SUB, (s + 1) * SUB)
        wide = dot(factors_ref[s, SUB + 16 :], spread)
        own = dot(left_ref[rows], jnp.concatenate([scaled[rows], carried[rows]], axis=0))
        summed = own * wide[:SUB] + skip * x_ref[rows, lanes].astype(F32)
        h = 0.5 * gate_ref[rows, lanes].astype(F32)
        silu = h + h * jnp.tanh(h)
        sum_ref[rows] = (summed * silu).astype(sum_ref.dtype)
        weight_ref[rows] = (wide[SUB:] * silu).astype(weight_ref.dtype)


def local(group, skip, x, gate, left, b_t, factors):
    tokens = x.shape[0]
    vmem = pl.BlockSpec(memory_space=pltpu.VMEM)
    return pl.pallas_call(
        functools.partial(local_kernel, group),
        in_specs=[pl.BlockSpec(memory_space=pltpu.SMEM)] + [vmem] * 5,
        out_specs=[vmem] * 2,
        out_shape=[jax.ShapeDtypeStruct((tokens, GROUP), F32), jax.ShapeDtypeStruct((tokens, GROUP), BF16)],
        scratch_shapes=[pltpu.VMEM((tokens, GROUP), BF16)] * 2,
        name="local",
        compiler_params=pltpu.CompilerParams(vmem_limit_bytes=LIMIT),
    )(skip, x, gate, left, b_t, factors)


def output_kernel(place, c_ref, gain_ref, own_ref, other_ref, *refs):
    groups = WIDTH // GROUP
    sums, weights = refs[:groups], refs[groups : 2 * groups]
    out_hbm, state, out, sems = refs[2 * groups :]
    mine = pl.multiple_of(place[CORE] * HALF, HALF)
    other = pl.multiple_of((1 - place[CORE]) * HALF, HALF)
    state[:, pl.ds(mine, HALF)] = own_ref[...].astype(BF16)
    state[:, pl.ds(other, HALF)] = other_ref[...].astype(BF16)
    same = iota((GROUP, GROUP), 0) // HEAD == iota((GROUP, GROUP), 1) // HEAD
    mean = jnp.where(same, 1.0 / HEAD, 0.0).astype(BF16)
    copies = []
    for i in range(out.shape[0] // OUT_STEP):
        rows = slice(i * OUT_STEP, (i + 1) * OUT_STEP)
        for g in range(groups):
            lanes = slice(g * GROUP, (g + 1) * GROUP)
            entering = dot(c_ref[rows], state[:, lanes])
            gated = sums[g][rows].astype(F32) + weights[g][rows].astype(F32) * entering
            square = dot((gated * gated).astype(BF16), mean)
            out[rows, lanes] = (gated * lax.rsqrt(square + 1e-5) * gain_ref[:, lanes]).astype(BF16)
        where = pl.ds(i * OUT_STEP, OUT_STEP)
        copies.append(pltpu.make_async_copy(out.at[where], out_hbm.at[where], sems.at[i]))
        copies[-1].start()
    for copy in copies:
        copy.wait()


def output(place, c, gain, own, other, sums, weights):
    tokens = c.shape[0]
    vmem = pl.BlockSpec(memory_space=pltpu.VMEM)
    return pl.pallas_call(
        output_kernel,
        in_specs=[pl.BlockSpec(memory_space=pltpu.SMEM)] + [vmem] * (4 + len(sums) + len(weights)),
        out_specs=pl.BlockSpec(memory_space=pl.ANY),
        out_shape=jax.ShapeDtypeStruct((tokens, WIDTH), BF16),
        scratch_shapes=[
            pltpu.VMEM((STATE, WIDTH), BF16),
            pltpu.VMEM((tokens, WIDTH), BF16),
            pltpu.SemaphoreType.DMA((tokens // OUT_STEP,)),
        ],
        name="output",
        compiler_params=pltpu.CompilerParams(vmem_limit_bytes=LIMIT),
    )(place, c, gain, own, other, *sums, *weights)


def device_of(z, y, x, core):
    return ((z * 4 + y) * 4 + x) * 2 + core


def moved(value, axis, shift):
    sizes = (4, 4, 4, 2)
    pairs = []
    for z in range(4):
        for y in range(4):
            for x in range(4):
                for core in range(2):
                    to = [z, y, x, core]
                    to[axis] = (to[axis] + shift) % sizes[axis]
                    pairs.append((device_of(z, y, x, core), device_of(*to)))
    return lax.ppermute(value, ("grp", "dev"), pairs)


def on_device(x, gate, b, c, decay, d_skip, norm_gain):
    z, r = lax.axis_index("grp"), lax.axis_index("dev")
    place = jnp.stack([z, r // 8, (r // 2) % 4, r % 2]).astype(jnp.int32)
    piece, chunk = (QUARTER + 8, HALF), (QUARTER, HALF)

    keep, send = end_state(place, x, b, decay)
    recv = moved(send, CORE, 1)
    left, b_t, factors = prepare(b, c, decay)
    parts = []

    def work(count, *arrived):
        for _ in range(count):
            parts.append(local(len(parts), d_skip, x, gate, left, b_t, factors))
        arrived, parts[-count:] = lax.optimization_barrier((arrived, parts[-count:]))
        return arrived

    (recv,), (left, b_t, factors) = lax.optimization_barrier(((recv,), (left, b_t, factors)))
    u0, *sends = small_call(pair_kernel, "pair", place, (keep, recv), [piece] * 4)
    lines = [u0] + list(work(1, *[moved(v, X, s + 1) for s, v in enumerate(sends)]))
    (v0,) = small_call(line_kernel, "line", place, lines, [piece])
    columns = [v0] + list(work(2, *[moved(v0, Y, s) for s in (1, 2, 3)]))
    w0, before = small_call(plane_kernel, "plane", place, columns, [piece] * 2)
    planes = [w0] + list(work(2, *[moved(w0, Z, s) for s in (1, 2, 3)]))
    e0, *sends = small_call(enter_kernel, "enter", place, planes + [before] + lines, [chunk] * 4)
    entering = [e0] + list(work(1, *[moved(v, X, s + 1) for s, v in enumerate(sends)]))
    own, send = small_call(chip_kernel, "chip", place, entering + [keep, recv], [(STATE, HALF)] * 2)
    other = moved(send, CORE, 1)
    sums, weights = zip(*parts, strict=True)
    return output(place, c, norm_gain[None], own, other, sums, weights)


def solution(mesh):
    return jax.shard_map(
        on_device,
        mesh=mesh,
        in_specs=(
            P(("grp", "dev"), None),
            P(("grp", "dev"), None),
            P(("grp", "dev"), None),
            P(("grp", "dev"), None),
            P(None, ("grp", "dev")),
            P(),
            P(),
        ),
        out_specs=P(("grp", "dev"), None),
        check_vma=False,
    )
```

time: 121 us -> 76.3 us (0.63)
  waiting for transfers between devices: 27 us -> 1.37 us
  Pallas kernels: 59.7 us -> 46.2 us
  local copies, waits for them, and re-layouts: 12.8 us -> 6.6 us
    ppermute x14, waiting for transfers between devices: 27 us -> 1.37 us  [moved(): return lax.ppermute(value, ('grp', 'dev'), pairs)]
    pallas_call x5, Pallas kernels: 10.6 us -> 3.58 us  [small_call(): pl.pallas_call(kernel, in_specs=[pl.BlockSpec(memory_space=pltpu.SMEM)] +...]
    pallas_call x2 -> x9, Pallas kernels: 49.1 us -> 42.6 us  [the longest x6 26.3 us: local(): pl.pallas_call(functools.partial(local_kernel, group), in_specs=[pl.Block...]
    unnamed x48 -> x20, local copies, waits for them, and re-layouts: 12.7 us -> 6.6 us
  transfers between devices with their start and end apart: 14 -> 14, of which waited for: 13 -> 1; matrix products, arithmetic and copies ran while one was open for 1% -> 0% of each run, Pallas kernels for 0% -> 37%
where the time goes in v2:
time: 76.3 us; the launch traced here: 76.1 us
  Pallas kernels  46.2 us (61%)
  starting transfers between devices  20.9 us (27%)
  local copies, waits for them, and re-layouts  6.6 us (9%)
  waiting for transfers between devices  1.37 us (2%)
    pallas_call x6, Pallas kernels, local(): pl.pallas_call(functools.partial(local_kernel, group), in_specs=[pl.Block...  26.3 us
    ppermute x14, starting transfers between devices, moved(): return lax.ppermute(value, ('grp', 'dev'), pairs)  20.9 us
    pallas_call x1, Pallas kernels, end_state(): pl.pallas_call(end_state_kernel, in_specs=[pl.BlockSpec(memory_space=pltp...  7.97 us
    unnamed x20, local copies, waits for them, and re-layouts  6.6 us
    pallas_call x1, Pallas kernels, output(): pl.pallas_call(output_kernel, in_specs=[pl.BlockSpec(memory_space=pltpu.S...  6.15 us
    pallas_call x5, Pallas kernels, small_call(): pl.pallas_call(kernel, in_specs=[pl.BlockSpec(memory_space=pltpu.SMEM)] +...  3.58 us
    pallas_call x1, Pallas kernels, prepare(): pl.pallas_call(prepare_kernel, in_specs=[vmem] * 3, out_specs=[vmem] * 3,...  2.17 us
  transfers between devices with their start and end apart: 14, of which 1 were waited for; matrix products, arithmetic and copies ran while one was open for 0% of the time, Pallas kernels for 37%

profile of v2, /device:TPU:1, one launch (start us, length us, event | category | flops | bytes accessed | tf_op | source)
XLA Modules:
  0.0 76.1 jit_solution(4245895350428370612)
XLA Ops:
  0.0 0.6 pad_add_fusion.place
  0.6 0.0 copy-start.2
  0.6 0.0 copy-start.3
  0.6 0.0 copy-start.6
  0.6 0.0 copy-start.7
  0.6 8.0 %end_state.1 = (f32[136,768]{1,0:T(8,128)}, f32[136,768]{1,0:T(8,128)}) custom-call(s32[4]{0:T(128)} %pad_add_fusion.place, bf16[2048,1536]{1,0:T(8,128)(2,1)} %x_ref.11, bf16[2048,128]{1,0:T(8,128)(2,1)} %b_ref.1, f32[24,2048]{1,0:T(8,128)} %decay_ref.1), custom_call_target="tpu_custom_call" | custom-call | tf_op jit(solution)/shard_map/end_state/pallas_call | solution.py:107
  8.6 0.0 copy-start.8
  8.6 1.5 %collective-permute-start = (f32[136,768]{1,0:T(8,128)}, f32[136,768]{1,0:T(8,128)S(1)}, u32[]{:S(2)}, u32[]{:S(2)}) collective-permute-start(f32[136,768]{1,0:T(8,128)} %get-tuple-element.63), channel_id=1, source_target_pairs={{0,1},{1,0},{2,3},{3,2},{4,5},{5,4},{6,7},{7,6},{8,9},{9,8},{10,11... | collective-permute-start | bytes 1253384 | tf_op jit(solution)/shard_map/ppermute | solution.py:363
  10.1 0.0 copy-done.2
  10.1 0.0 copy-done.3
  10.1 0.0 copy-done.6
  10.1 2.2 %prepare.1 = (bf16[2048,256]{1,0:T(8,128)(2,1)S(1)}, bf16[2048,128]{1,0:T(8,128)(2,1)S(1)}, bf16[16,400,72]{2,1,0:T(8,128)(2,1)S(1)}) custom-call(bf16[2048,128]{1,0:T(8,128)(2,1)S(1)} %copy-done.3, bf16[2048,128]{1,0:T(8,128)(2,1)S(1)} %copy-done.2, f32[24,2048]{1,0:T(8,128)S(1)} %copy-done.6), custom_call_target="tpu_custom_call" | custom-call | tf_op jit(solution)/shard_map/prepare/pallas_call | solution.py:249
  12.3 0.0 collective-permute-done.recv
  12.3 0.0 copy-done.7
  12.3 0.0 copy-start.4
  12.3 1.0 %copy-done.4 = f32[136,768]{1,0:T(8,128)S(1)} copy-done((f32[136,768]{1,0:T(8,128)S(1)}, f32[136,768]{1,0:T(8,128)}, u32[]{:S(2)}) %copy-start.4) | copy-done | bytes 417816
  13.3 0.6 pair.1
  13.9 1.4 %collective-permute-start.1 = (f32[40,768]{1,0:T(8,128)S(1)}, f32[40,768]{1,0:T(8,128)S(1)}, u32[]{:S(2)}, u32[]{:S(2)}) collective-permute-start(f32[40,768]{1,0:T(8,128)S(1)} %get-tuple-element.69), channel_id=1, source_target_pairs={{0,2},{1,3},{2,4},{3,5},{4,6},{5,7},{6,0},{7,1},{8,10},{9,11},{10,... | collective-permute-start | bytes 368648 | tf_op jit(solution)/shard_map/ppermute | solution.py:363
  15.3 2.5 %collective-permute-start.2 = (f32[40,768]{1,0:T(8,128)S(1)}, f32[40,768]{1,0:T(8,128)S(1)}, u32[]{:S(2)}, u32[]{:S(2)}) collective-permute-start(f32[40,768]{1,0:T(8,128)S(1)} %get-tuple-element.70), channel_id=1, source_target_pairs={{0,4},{1,5},{2,6},{3,7},{4,0},{5,1},{6,2},{7,3},{8,12},{9,13},{10,... | collective-permute-start | bytes 368648 | tf_op jit(solution)/shard_map/ppermute | solution.py:363
  17.7 1.2 %collective-permute-start.3 = (f32[40,768]{1,0:T(8,128)S(1)}, f32[40,768]{1,0:T(8,128)S(1)}, u32[]{:S(2)}, u32[]{:S(2)}) collective-permute-start(f32[40,768]{1,0:T(8,128)S(1)} %get-tuple-element.71), channel_id=1, source_target_pairs={{0,6},{1,7},{2,0},{3,1},{4,2},{5,3},{6,4},{7,5},{8,14},{9,15},{10,... | collective-permute-start | bytes 368648 | tf_op jit(solution)/shard_map/ppermute | solution.py:363
  18.9 0.0 copy-done.8
  18.9 0.0 copy-start
  18.9 2.8 %copy-done = bf16[2048,1536]{1,0:T(8,128)(2,1)S(1)} copy-done((bf16[2048,1536]{1,0:T(8,128)(2,1)S(1)}, bf16[2048,1536]{1,0:T(8,128)(2,1)}, u32[]{:S(2)}) %copy-start) | copy-done | bytes 6291480
  21.7 0.0 copy-start.1
  21.7 2.8 %copy-done.1 = bf16[2048,1536]{1,0:T(8,128)(2,1)S(1)} copy-done((bf16[2048,1536]{1,0:T(8,128)(2,1)S(1)}, bf16[2048,1536]{1,0:T(8,128)(2,1)}, u32[]{:S(2)}) %copy-start.1) | copy-done | bytes 6291480
  24.5 4.4 %local.6 = (f32[2048,256]{1,0:T(8,128)S(1)}, bf16[2048,256]{1,0:T(8,128)(2,1)S(1)}) custom-call(f32[24]{0:T(128)S(1)} %copy-done.8, bf16[2048,1536]{1,0:T(8,128)(2,1)S(1)} %copy-done, bf16[2048,1536]{1,0:T(8,128)(2,1)S(1)} %copy-done.1, bf16[2048,256]{1,0:T(8,128)(2,1)S(1)} %get-tuple-element.72.left_ref, bf16[2048,128]{1,0:T(8,128)(2,1)S(1)} %get-tuple-element.73.b_t_ref, ...), custom_call_target="tpu_custom_call" | custom-call | tf_op jit(solution)/shard_map/local/pallas_call | solution.py:294
  28.9 0.0 collective-permute-done.1.u1
  28.9 0.0 collective-permute-done.2.u2
  28.9 0.0 collective-permute-done.3.u3
  28.9 0.6 line.1.v0
  29.5 2.8 %collective-permute-start.6 = (f32[40,768]{1,0:T(8,128)S(1)}, f32[40,768]{1,0:T(8,128)S(1)}, u32[]{:S(2)}, u32[]{:S(2)}) collective-permute-start(f32[40,768]{1,0:T(8,128)S(1)} %line.1.v0), channel_id=1, source_target_pairs={{0,24},{1,25},{2,26},{3,27},{4,28},{5,29},{6,30},{7,31},{8,0},{9,1... | collective-permute-start | bytes 368648 | tf_op jit(solution)/shard_map/ppermute | solution.py:363
  32.3 0.3 collective-permute-start.5
  32.7 0.7 collective-permute-start.4
  33.4 4.4 %local.8 = (f32[2048,256]{1,0:T(8,128)S(1)}, bf16[2048,256]{1,0:T(8,128)(2,1)S(1)}) custom-call(f32[24]{0:T(128)S(1)} %copy-done.8, bf16[2048,1536]{1,0:T(8,128)(2,1)S(1)} %copy-done, bf16[2048,1536]{1,0:T(8,128)(2,1)S(1)} %copy-done.1, bf16[2048,256]{1,0:T(8,128)(2,1)S(1)} %get-tuple-element.72.left_ref, bf16[2048,128]{1,0:T(8,128)(2,1)S(1)} %get-tuple-element.73.b_t_ref, ...), custom_call_target="tpu_custom_call" | custom-call | tf_op jit(solution)/shard_map/local/pallas_call | solution.py:294
  37.8 4.4 %local.7 = (f32[2048,256]{1,0:T(8,128)S(1)}, bf16[2048,256]{1,0:T(8,128)(2,1)S(1)}) custom-call(f32[24]{0:T(128)S(1)} %copy-done.8, bf16[2048,1536]{1,0:T(8,128)(2,1)S(1)} %copy-done, bf16[2048,1536]{1,0:T(8,128)(2,1)S(1)} %copy-done.1, bf16[2048,256]{1,0:T(8,128)(2,1)S(1)} %get-tuple-element.72.left_ref, bf16[2048,128]{1,0:T(8,128)(2,1)S(1)} %get-tuple-element.73.b_t_ref, ...), custom_call_target="tpu_custom_call" | custom-call | tf_op jit(solution)/shard_map/local/pallas_call | solution.py:294
  42.2 0.0 collective-permute-done.6.v3
  42.2 0.0 collective-permute-done.5.v2
  42.2 0.0 collective-permute-done.4.v1
  42.2 0.7 plane.1
  42.9 3.8 %collective-permute-start.9 = (f32[40,768]{1,0:T(8,128)S(1)}, f32[40,768]{1,0:T(8,128)S(1)}, u32[]{:S(2)}, u32[]{:S(2)}) collective-permute-start(f32[40,768]{1,0:T(8,128)S(1)} %get-tuple-element.87.w0), channel_id=1, source_target_pairs={{0,96},{1,97},{2,98},{3,99},{4,100},{5,101},{6,102},{7,103},{8,104... | collective-permute-start | bytes 368648 | tf_op jit(solution)/shard_map/ppermute | solution.py:363
  46.8 0.0 collective-permute-start.8
  46.8 0.7 collective-permute-start.7
  47.5 4.4 %local.10 = (f32[2048,256]{1,0:T(8,128)S(1)}, bf16[2048,256]{1,0:T(8,128)(2,1)S(1)}) custom-call(f32[24]{0:T(128)S(1)} %copy-done.8, bf16[2048,1536]{1,0:T(8,128)(2,1)S(1)} %copy-done, bf16[2048,1536]{1,0:T(8,128)(2,1)S(1)} %copy-done.1, bf16[2048,256]{1,0:T(8,128)(2,1)S(1)} %get-tuple-element.72.left_ref, bf16[2048,128]{1,0:T(8,128)(2,1)S(1)} %get-tuple-element.73.b_t_ref, ...), custom_call_target="tpu_custom_call" | custom-call | tf_op jit(solution)/shard_map/local/pallas_call | solution.py:294
  51.8 4.4 %local.9 = (f32[2048,256]{1,0:T(8,128)S(1)}, bf16[2048,256]{1,0:T(8,128)(2,1)S(1)}) custom-call(f32[24]{0:T(128)S(1)} %copy-done.8, bf16[2048,1536]{1,0:T(8,128)(2,1)S(1)} %copy-done, bf16[2048,1536]{1,0:T(8,128)(2,1)S(1)} %copy-done.1, bf16[2048,256]{1,0:T(8,128)(2,1)S(1)} %get-tuple-element.72.left_ref, bf16[2048,128]{1,0:T(8,128)(2,1)S(1)} %get-tuple-element.73.b_t_ref, ...), custom_call_target="tpu_custom_call" | custom-call | tf_op jit(solution)/shard_map/local/pallas_call | solution.py:294
  56.2 0.0 collective-permute-done.9.w3
  56.2 0.0 collective-permute-done.8.w2
  56.3 0.0 collective-permute-done.7.w1
  56.3 1.0 %enter.1 = (f32[32,768]{1,0:T(8,128)S(1)}, f32[32,768]{1,0:T(8,128)S(1)}, f32[32,768]{1,0:T(8,128)S(1)}, f32[32,768]{1,0:T(8,128)S(1)}) custom-call(s32[4]{0:T(128)S(1)} %copy-done.7, f32[40,768]{1,0:T(8,128)S(1)} %get-tuple-element.87.w0, f32[40,768]{1,0:T(8,128)S(1)} %collective-permute-done.7.w1, f32[40,768]{1,0:T(8,128)S(1)} %collective-permute-done.8.w2, ...), custom_call_target="tpu_custom_call" | custom-call | tf_op jit(solution)/shard_map/enter/pallas_call | solution.py:128
  57.2 0.4 collective-permute-start.10
  57.6 0.9 %collective-permute-start.11 = (f32[32,768]{1,0:T(8,128)S(1)}, f32[32,768]{1,0:T(8,128)S(1)}, u32[]{:S(2)}, u32[]{:S(2)}) collective-permute-start(f32[32,768]{1,0:T(8,128)S(1)} %get-tuple-element.98), channel_id=1, source_target_pairs={{0,4},{1,5},{2,6},{3,7},{4,0},{5,1},{6,2},{7,3},{8,12},{9,13},{10,... | collective-permute-start | bytes 294920 | tf_op jit(solution)/shard_map/ppermute | solution.py:363
  58.5 0.0 copy-start.5
  58.5 0.0 copy-start.9
  58.5 1.6 %collective-permute-start.12 = (f32[32,768]{1,0:T(8,128)S(1)}, f32[32,768]{1,0:T(8,128)S(1)}, u32[]{:S(2)}, u32[]{:S(2)}) collective-permute-start(f32[32,768]{1,0:T(8,128)S(1)} %get-tuple-element.99), channel_id=1, source_target_pairs={{0,6},{1,7},{2,0},{3,1},{4,2},{5,3},{6,4},{7,5},{8,14},{9,15},{10,... | collective-permute-start | bytes 294920 | tf_op jit(solution)/shard_map/ppermute | solution.py:363
  60.1 4.4 %local.11 = (f32[2048,256]{1,0:T(8,128)S(1)}, bf16[2048,256]{1,0:T(8,128)(2,1)S(1)}) custom-call(f32[24]{0:T(128)S(1)} %copy-done.8, bf16[2048,1536]{1,0:T(8,128)(2,1)S(1)} %copy-done, bf16[2048,1536]{1,0:T(8,128)(2,1)S(1)} %copy-done.1, bf16[2048,256]{1,0:T(8,128)(2,1)S(1)} %get-tuple-element.72.left_ref, bf16[2048,128]{1,0:T(8,128)(2,1)S(1)} %get-tuple-element.73.b_t_ref, ...), custom_call_target="tpu_custom_call" | custom-call | tf_op jit(solution)/shard_map/local/pallas_call | solution.py:294
  64.5 0.0 collective-permute-done.10.e1
  64.5 0.0 collective-permute-done.11.e2
  64.5 0.0 collective-permute-done.12.e3
  64.5 0.0 copy-done.5
  64.5 0.7 chip.1
  65.2 3.2 %collective-permute-start.13 = (f32[128,768]{1,0:T(8,128)S(1)}, f32[128,768]{1,0:T(8,128)S(1)}, u32[]{:S(2)}, u32[]{:S(2)}) collective-permute-start(f32[128,768]{1,0:T(8,128)S(1)} %get-tuple-element.106), channel_id=1, source_target_pairs={{0,1},{1,0},{2,3},{3,2},{4,5},{5,4},{6,7},{7,6},{8,9},{9,8},{10,11... | collective-permute-start | bytes 1179656 | tf_op jit(solution)/shard_map/ppermute | solution.py:363
  68.4 0.0 copy-done.9
  68.4 1.3 %collective-permute-done.13.other_ref = f32[128,768]{1,0:T(8,128)S(1)} collective-permute-done((f32[128,768]{1,0:T(8,128)S(1)}, f32[128,768]{1,0:T(8,128)S(1)}, u32[]{:S(2)}, u32[]{:S(2)}) %collective-permute-start.13) | collective-permute-done | bytes 393248 | tf_op jit(solution)/shard_map/ppermute | solution.py:363
  69.8 6.2 %output.1 = bf16[2048,1536]{1,0:T(8,128)(2,1)} custom-call(s32[4]{0:T(128)S(1)} %copy-done.7, bf16[2048,128]{1,0:T(8,128)(2,1)S(1)} %copy-done.2, f32[1,1536]{1,0:T(1,128)S(1)} %broadcast_in_dim.3.gain_ref, f32[128,768]{1,0:T(8,128)S(1)} %get-tuple-element.105.own_ref, f32[128,768]{1,0:T(8,128)S(1)} %collective-permute-done.13.other_ref, ...), custom_call_target="tpu_custom_call" | custom-call | tf_op jit(solution)/shard_map/output/pallas_call | solution.py:334
  (1 shorter events, 0.0 us)
Async XLA Ops:
  0.6 9.5 %copy-start.2 = (bf16[2048,128]{1,0:T(8,128)(2,1)S(1)}, bf16[2048,128]{1,0:T(8,128)(2,1)}, u32[]{:S(2)}) copy-start(bf16[2048,128]{1,0:T(8,128)(2,1)} %c_ref.3) | copy-start | bytes 1572868
  0.6 9.5 %copy-start.3 = (bf16[2048,128]{1,0:T(8,128)(2,1)S(1)}, bf16[2048,128]{1,0:T(8,128)(2,1)}, u32[]{:S(2)}) copy-start(bf16[2048,128]{1,0:T(8,128)(2,1)} %b_ref.1) | copy-start | bytes 1572868
  0.6 9.5 %copy-start.6 = (f32[24,2048]{1,0:T(8,128)S(1)}, f32[24,2048]{1,0:T(8,128)}, u32[]{:S(2)}) copy-start(f32[24,2048]{1,0:T(8,128)} %decay_ref.1) | copy-start | bytes 589828
  0.6 11.7 %copy-start.7 = (s32[4]{0:T(128)S(1)}, s32[4]{0:T(128)}, u32[]{:S(2)}) copy-start(s32[4]{0:T(128)} %pad_add_fusion.place) | copy-start | bytes 52
  8.6 10.3 %copy-start.8 = (f32[24]{0:T(128)S(1)}, f32[24]{0:T(128)}, u32[]{:S(2)}) copy-start(f32[24]{0:T(128)} %skip_ref.11) | copy-start | bytes 292
  8.6 3.7 %collective-permute-start = (f32[136,768]{1,0:T(8,128)}, f32[136,768]{1,0:T(8,128)S(1)}, u32[]{:S(2)}, u32[]{:S(2)}) collective-permute-start(f32[136,768]{1,0:T(8,128)} %get-tuple-element.63), channel_id=1, source_target_pairs={{0,1},{1,0},{2,3},{3,2},{4,5},{5,4},{6,7},{7,6},{8,9},{9,8},{10,11... | collective-permute-start | bytes 1253384 | tf_op jit(solution)/shard_map/ppermute | solution.py:363
  12.3 1.0 %copy-start.4 = (f32[136,768]{1,0:T(8,128)S(1)}, f32[136,768]{1,0:T(8,128)}, u32[]{:S(2)}) copy-start(f32[136,768]{1,0:T(8,128)} %get-tuple-element.62.keep) | copy-start | bytes 1253380
  13.9 14.9 %collective-permute-start.1 = (f32[40,768]{1,0:T(8,128)S(1)}, f32[40,768]{1,0:T(8,128)S(1)}, u32[]{:S(2)}, u32[]{:S(2)}) collective-permute-start(f32[40,768]{1,0:T(8,128)S(1)} %get-tuple-element.69), channel_id=1, source_target_pairs={{0,2},{1,3},{2,4},{3,5},{4,6},{5,7},{6,0},{7,1},{8,10},{9,11},{10,... | collective-permute-start | bytes 368648 | tf_op jit(solution)/shard_map/ppermute | solution.py:363
  15.3 13.6 %collective-permute-start.2 = (f32[40,768]{1,0:T(8,128)S(1)}, f32[40,768]{1,0:T(8,128)S(1)}, u32[]{:S(2)}, u32[]{:S(2)}) collective-permute-start(f32[40,768]{1,0:T(8,128)S(1)} %get-tuple-element.70), channel_id=1, source_target_pairs={{0,4},{1,5},{2,6},{3,7},{4,0},{5,1},{6,2},{7,3},{8,12},{9,13},{10,... | collective-permute-start | bytes 368648 | tf_op jit(solution)/shard_map/ppermute | solution.py:363
  17.7 11.1 %collective-permute-start.3 = (f32[40,768]{1,0:T(8,128)S(1)}, f32[40,768]{1,0:T(8,128)S(1)}, u32[]{:S(2)}, u32[]{:S(2)}) collective-permute-start(f32[40,768]{1,0:T(8,128)S(1)} %get-tuple-element.71), channel_id=1, source_target_pairs={{0,6},{1,7},{2,0},{3,1},{4,2},{5,3},{6,4},{7,5},{8,14},{9,15},{10,... | collective-permute-start | bytes 368648 | tf_op jit(solution)/shard_map/ppermute | solution.py:363
  18.9 2.8 %copy-start = (bf16[2048,1536]{1,0:T(8,128)(2,1)S(1)}, bf16[2048,1536]{1,0:T(8,128)(2,1)}, u32[]{:S(2)}) copy-start(bf16[2048,1536]{1,0:T(8,128)(2,1)} %x_ref.11) | copy-start | bytes 18874372
  21.7 2.8 %copy-start.1 = (bf16[2048,1536]{1,0:T(8,128)(2,1)S(1)}, bf16[2048,1536]{1,0:T(8,128)(2,1)}, u32[]{:S(2)}) copy-start(bf16[2048,1536]{1,0:T(8,128)(2,1)} %gate_ref.11) | copy-start | bytes 18874372
  29.5 12.6 %collective-permute-start.6 = (f32[40,768]{1,0:T(8,128)S(1)}, f32[40,768]{1,0:T(8,128)S(1)}, u32[]{:S(2)}, u32[]{:S(2)}) collective-permute-start(f32[40,768]{1,0:T(8,128)S(1)} %line.1.v0), channel_id=1, source_target_pairs={{0,24},{1,25},{2,26},{3,27},{4,28},{5,29},{6,30},{7,31},{8,0},{9,1... | collective-permute-start | bytes 368648 | tf_op jit(solution)/shard_map/ppermute | solution.py:363
  32.3 9.8 %collective-permute-start.5 = (f32[40,768]{1,0:T(8,128)S(1)}, f32[40,768]{1,0:T(8,128)S(1)}, u32[]{:S(2)}, u32[]{:S(2)}) collective-permute-start(f32[40,768]{1,0:T(8,128)S(1)} %line.1.v0), channel_id=1, source_target_pairs={{0,16},{1,17},{2,18},{3,19},{4,20},{5,21},{6,22},{7,23},{8,24},{9,... | collective-permute-start | bytes 368648 | tf_op jit(solution)/shard_map/ppermute | solution.py:363
  32.7 9.5 %collective-permute-start.4 = (f32[40,768]{1,0:T(8,128)S(1)}, f32[40,768]{1,0:T(8,128)S(1)}, u32[]{:S(2)}, u32[]{:S(2)}) collective-permute-start(f32[40,768]{1,0:T(8,128)S(1)} %line.1.v0), channel_id=1, source_target_pairs={{0,8},{1,9},{2,10},{3,11},{4,12},{5,13},{6,14},{7,15},{8,16},{9,17... | collective-permute-start | bytes 368648 | tf_op jit(solution)/shard_map/ppermute | solution.py:363
  42.9 13.3 %collective-permute-start.9 = (f32[40,768]{1,0:T(8,128)S(1)}, f32[40,768]{1,0:T(8,128)S(1)}, u32[]{:S(2)}, u32[]{:S(2)}) collective-permute-start(f32[40,768]{1,0:T(8,128)S(1)} %get-tuple-element.87.w0), channel_id=1, source_target_pairs={{0,96},{1,97},{2,98},{3,99},{4,100},{5,101},{6,102},{7,103},{8,104... | collective-permute-start | bytes 368648 | tf_op jit(solution)/shard_map/ppermute | solution.py:363
  46.8 9.5 %collective-permute-start.8 = (f32[40,768]{1,0:T(8,128)S(1)}, f32[40,768]{1,0:T(8,128)S(1)}, u32[]{:S(2)}, u32[]{:S(2)}) collective-permute-start(f32[40,768]{1,0:T(8,128)S(1)} %get-tuple-element.87.w0), channel_id=1, source_target_pairs={{0,64},{1,65},{2,66},{3,67},{4,68},{5,69},{6,70},{7,71},{8,72},{9,... | collective-permute-start | bytes 368648 | tf_op jit(solution)/shard_map/ppermute | solution.py:363
  46.8 9.5 %collective-permute-start.7 = (f32[40,768]{1,0:T(8,128)S(1)}, f32[40,768]{1,0:T(8,128)S(1)}, u32[]{:S(2)}, u32[]{:S(2)}) collective-permute-start(f32[40,768]{1,0:T(8,128)S(1)} %get-tuple-element.87.w0), channel_id=1, source_target_pairs={{0,32},{1,33},{2,34},{3,35},{4,36},{5,37},{6,38},{7,39},{8,40},{9,... | collective-permute-start | bytes 368648 | tf_op jit(solution)/shard_map/ppermute | solution.py:363
  57.2 7.3 %collective-permute-start.10 = (f32[32,768]{1,0:T(8,128)S(1)}, f32[32,768]{1,0:T(8,128)S(1)}, u32[]{:S(2)}, u32[]{:S(2)}) collective-permute-start(f32[32,768]{1,0:T(8,128)S(1)} %get-tuple-element.97), channel_id=1, source_target_pairs={{0,2},{1,3},{2,4},{3,5},{4,6},{5,7},{6,0},{7,1},{8,10},{9,11},{10,... | collective-permute-start | bytes 294920 | tf_op jit(solution)/shard_map/ppermute | solution.py:363
  57.6 6.9 %collective-permute-start.11 = (f32[32,768]{1,0:T(8,128)S(1)}, f32[32,768]{1,0:T(8,128)S(1)}, u32[]{:S(2)}, u32[]{:S(2)}) collective-permute-start(f32[32,768]{1,0:T(8,128)S(1)} %get-tuple-element.98), channel_id=1, source_target_pairs={{0,4},{1,5},{2,6},{3,7},{4,0},{5,1},{6,2},{7,3},{8,12},{9,13},{10,... | collective-permute-start | bytes 294920 | tf_op jit(solution)/shard_map/ppermute | solution.py:363
  58.5 6.0 %copy-start.5 = (f32[136,768]{1,0:T(8,128)S(1)}, f32[136,768]{1,0:T(8,128)}, u32[]{:S(2)}) copy-start(f32[136,768]{1,0:T(8,128)} %get-tuple-element.62.keep) | copy-start | bytes 1253380
  58.5 9.9 %copy-start.9 = (f32[1536]{0:T(1024)S(1)}, f32[1536]{0:T(1024)}, u32[]{:S(2)}) copy-start(f32[1536]{0:T(1024)} %param.13) | copy-start | bytes 18436
  58.5 6.0 %collective-permute-start.12 = (f32[32,768]{1,0:T(8,128)S(1)}, f32[32,768]{1,0:T(8,128)S(1)}, u32[]{:S(2)}, u32[]{:S(2)}) collective-permute-start(f32[32,768]{1,0:T(8,128)S(1)} %get-tuple-element.99), channel_id=1, source_target_pairs={{0,6},{1,7},{2,0},{3,1},{4,2},{5,3},{6,4},{7,5},{8,14},{9,15},{10,... | collective-permute-start | bytes 294920 | tf_op jit(solution)/shard_map/ppermute | solution.py:363
  65.2 4.5 %collective-permute-start.13 = (f32[128,768]{1,0:T(8,128)S(1)}, f32[128,768]{1,0:T(8,128)S(1)}, u32[]{:S(2)}, u32[]{:S(2)}) collective-permute-start(f32[128,768]{1,0:T(8,128)S(1)} %get-tuple-element.106), channel_id=1, source_target_pairs={{0,1},{1,0},{2,3},{3,2},{4,5},{5,4},{6,7},{7,6},{8,9},{9,8},{10,11... | collective-permute-start | bytes 1179656 | tf_op jit(solution)/shard_map/ppermute | solution.py:363

commit v3 on v2

--- a/solution.py
+++ b/solution.py
@@ -20,7 +20,8 @@
 SHIFT_LOG = 51.29289136
 OUT_STEP = 256
 QUARTER = STATE // 4
-FIRST_LIMIT = 60 * 1024 * 1024
+FIRST_LIMIT = 42 * 1024 * 1024
+PREPARE_LIMIT = 40 * 1024 * 1024
 LIMIT = 18 * 1024 * 1024
 SMALL_LIMIT = 6 * 1024 * 1024
 F32 = jnp.float32
@@ -63,18 +64,31 @@
     return jnp.where(k % HEADS == lane // HEAD, 1.0, 0.0).astype(BF16)
 
 
-def end_state_kernel(place, x_hbm, b_hbm, decay_hbm, keep_ref, send_ref, x, b, decay, scaled, factors, spread, sems):
-    steps = x.shape[0] // STEP
-    fetch_decay = pltpu.make_async_copy(decay_hbm, decay, sems.at[steps])
+def half_state(x, b, factors, scaled, start, out, fetched):
+    lanes = pl.ds(pl.multiple_of(start, HALF), HALF)
+    spread = spread_matrix(start, HALF)
+    tokens = x.shape[0]
+    for i in range(tokens // STEP):
+        fetched(i)
+        rows = slice(i * STEP, (i + 1) * STEP)
+        scaled[rows] = (x[rows, lanes].astype(F32) * dot(factors[rows], spread)).astype(BF16)
+    fetched(tokens // STEP)
+    out[:STATE] = dot(b[...], scaled[...], ((0,), (0,)))
+    out[STATE:] = dot(factors[tokens:], spread)[:8]
+
+
+def send_state_kernel(place, x_hbm, b_hbm, decay_hbm, send_ref, x, b, factors, decay, scaled, sems):
+    tokens = x.shape[0]
+    steps = tokens // STEP
+    fetch_decay = pltpu.make_async_copy(decay_hbm, decay, sems.at[steps + 1])
     fetch_decay.start()
     copies = []
     for i in range(steps):
         rows = pl.ds(i * STEP, STEP)
         copies.append(pltpu.make_async_copy(x_hbm.at[rows], x.at[rows], sems.at[i]))
-        copies[-1].start()
-    fetch_b = pltpu.make_async_copy(b_hbm, b, sems.at[steps + 1])
-    fetch_b.start()
-    spread[...] = spread_matrix(0, WIDTH)
+    copies.append(pltpu.make_async_copy(b_hbm, b, sems.at[steps]))
+    for copy in copies:
+        copy.start()
     row, col = iota((STEP + 16, STEP), 0), iota((STEP + 16, STEP), 1)
     later = jnp.where((col > row) | (row >= STEP), 1.0, 0.0).astype(BF16)
     fetch_decay.wait()
@@ -86,41 +100,48 @@
     for i in reversed(range(steps)):
         factors[i * STEP : (i + 1) * STEP] = spread_parts(jnp.exp(sums[i][:STEP] + after))
         after = after + sums[i][STEP : STEP + 1]
-    whole = spread_parts(jnp.exp(jnp.broadcast_to(after, (16, 3 * HEADS))))
-    for i in range(steps):
-        copies[i].wait()
-        rows = slice(i * STEP, (i + 1) * STEP)
-        scaled[rows] = (x[rows].astype(F32) * dot(factors[rows], spread[...])).astype(BF16)
-    fetch_b.wait()
-    mine = pl.multiple_of(place[CORE] * HALF, HALF)
-    other = pl.multiple_of((1 - place[CORE]) * HALF, HALF)
-    for start, out in ((other, send_ref), (mine, keep_ref)):
-        lanes = pl.ds(start, HALF)
-        out[:STATE] = dot(b[...], scaled[:, lanes], ((0,), (0,)))
-        out[STATE:] = dot(whole, spread[:, lanes])[:8]
-
-
-def end_state(place, x, b, decay):
+    factors[tokens:] = spread_parts(jnp.exp(jnp.broadcast_to(after, (16, 3 * HEADS))))
+    half_state(x, b, factors, scaled, (1 - place[CORE]) * HALF, send_ref, lambda i: copies[i].wait())
+
+
+def send_state(place, x, b, decay):
     tokens = x.shape[0]
-    half = jax.ShapeDtypeStruct((ROWS, HALF), F32)
-    vmem = pl.BlockSpec(memory_space=pltpu.VMEM)
-    return pl.pallas_call(
-        end_state_kernel,
-        in_specs=[pl.BlockSpec(memory_space=pltpu.SMEM)] + [pl.BlockSpec(memory_space=pl.ANY)] * 3,
-        out_specs=[vmem, vmem],
-        out_shape=[half, half],
+    vmem = pl.BlockSpec(memory_space=pltpu.VMEM)
+    return pl.pallas_call(
+        send_state_kernel,
+        in_specs=[pl.BlockSpec(memory_space=pltpu.SMEM)] + [pl.BlockSpec(memory_space=pltpu.HBM)] * 3,
+        out_specs=[vmem] * 4,
+        out_shape=[
+            jax.ShapeDtypeStruct((ROWS, HALF), F32),
+            jax.ShapeDtypeStruct(x.shape, BF16),
+            jax.ShapeDtypeStruct(b.shape, BF16),
+            jax.ShapeDtypeStruct((tokens + 16, 3 * HEADS), BF16),
+        ],
         scratch_shapes=[
-            pltpu.VMEM(x.shape, BF16),
-            pltpu.VMEM(b.shape, BF16),
             pltpu.VMEM(decay.shape, F32),
-            pltpu.VMEM((tokens, WIDTH), BF16),
-            pltpu.VMEM((tokens, 3 * HEADS), BF16),
-            pltpu.VMEM((3 * HEADS, WIDTH), BF16),
+            pltpu.VMEM((tokens, HALF), BF16),
             pltpu.SemaphoreType.DMA((tokens // STEP + 2,)),
         ],
-        name="end_state",
+        name="send_state",
         compiler_params=pltpu.CompilerParams(vmem_limit_bytes=FIRST_LIMIT),
     )(place, x, b, decay)
+
+
+def keep_state_kernel(place, x, b, factors, keep_ref, scaled):
+    half_state(x, b, factors, scaled, place[CORE] * HALF, keep_ref, lambda i: None)
+
+
+def keep_state(place, x, b, factors):
+    vmem = pl.BlockSpec(memory_space=pltpu.VMEM)
+    return pl.pallas_call(
+        keep_state_kernel,
+        in_specs=[pl.BlockSpec(memory_space=pltpu.SMEM)] + [vmem] * 3,
+        out_specs=vmem,
+        out_shape=jax.ShapeDtypeStruct((ROWS, HALF), F32),
+        scratch_shapes=[pltpu.VMEM((x.shape[0], HALF), BF16)],
+        name="keep_state",
+        compiler_params=pltpu.CompilerParams(vmem_limit_bytes=LIMIT),
+    )(place, x, b, factors)
 
 
 def small_call(kernel, name, place, args, outs):
@@ -218,98 +239,113 @@
         send[rows] = jnp.where(flip, at_first, at_second)
 
 
-FACTORS = 3 * SUB + 16
-
-
-def prepare_kernel(b_ref, c_ref, decay_ref, left_ref, b_t_ref, factors_ref):
+BEFORE = SUB + 16
+AFTER = 2 * SUB
+
+
+def prepare_kernel(gate_hbm, b_ref, c_ref, decay_ref, gate, left_ref, b_t_ref, before_ref, after_ref, sem):
+    fetch = pltpu.make_async_copy(gate_hbm, gate, sem)
+    fetch.start()
     tokens = b_ref.shape[0]
     row, col = iota((SUB, SUB), 0), iota((SUB, SUB), 1)
     causal = col <= row
     upto = jnp.where(causal, 1.0, 0.0).astype(BF16)
-    before = jnp.zeros((1, 3 * HEADS), F32)
+    start = jnp.zeros((1, 3 * HEADS), F32)
     for s in range(tokens // SUB):
         rows = slice(s * SUB, (s + 1) * SUB)
         decay = decay_ref[:, rows]
         cumul = decay_sums(upto, jnp.concatenate([decay] * 3, axis=0))
         end = cumul[SUB - 1 : SUB]
         shifted = end + SHIFT_LOG
-        exponents = [shifted - cumul, jnp.broadcast_to(shifted, (16, 3 * HEADS)), cumul - shifted, cumul + before]
-        factors_ref[s] = spread_parts(jnp.exp(jnp.concatenate(exponents, axis=0)))
-        before = before + end
+        exponents = [shifted - cumul, jnp.broadcast_to(shifted, (16, 3 * HEADS)), cumul - shifted, cumul + start]
+        factors = spread_parts(jnp.exp(jnp.concatenate(exponents, axis=0)))
+        before_ref[s * BEFORE : (s + 1) * BEFORE] = factors[:BEFORE]
+        after_ref[s * AFTER : (s + 1) * AFTER] = factors[BEFORE:]
+        start = start + end
         b, c = b_ref[rows], c_ref[rows]
         scores = jnp.where(causal, dot(c, b, ((1,), (1,))), 0.0)
         left_ref[rows, :SUB] = scores.astype(BF16)
         left_ref[rows, SUB:] = c
         b_t_ref[rows] = jnp.transpose(b.astype(F32)).astype(BF16)
-
-
-def prepare(b, c, decay):
+    fetch.wait()
+
+
+def prepare(gate, b, c, decay):
     tokens = b.shape[0]
+    subs = tokens // SUB
     vmem = pl.BlockSpec(memory_space=pltpu.VMEM)
     return pl.pallas_call(
         prepare_kernel,
-        in_specs=[vmem] * 3,
-        out_specs=[vmem] * 3,
+        in_specs=[pl.BlockSpec(memory_space=pltpu.HBM)] + [vmem] * 3,
+        out_specs=[vmem] * 5,
         out_shape=[
+            jax.ShapeDtypeStruct(gate.shape, BF16),
             jax.ShapeDtypeStruct((tokens, SUB + STATE), BF16),
             jax.ShapeDtypeStruct((tokens, SUB), BF16),
-            jax.ShapeDtypeStruct((tokens // SUB, FACTORS, 3 * HEADS), BF16),
+            jax.ShapeDtypeStruct((subs * BEFORE, 3 * HEADS), BF16),
+            jax.ShapeDtypeStruct((subs * AFTER, 3 * HEADS), BF16),
         ],
+        scratch_shapes=[pltpu.SemaphoreType.DMA],
         name="prepare",
-        compiler_params=pltpu.CompilerParams(vmem_limit_bytes=LIMIT),
-    )(b, c, decay)
-
-
-def local_kernel(group, skip_ref, x_ref, gate_ref, left_ref, b_t_ref, factors_ref, sum_ref, weight_ref, scaled, carried):
+        compiler_params=pltpu.CompilerParams(vmem_limit_bytes=PREPARE_LIMIT),
+    )(gate, b, c, decay)
+
+
+def local_kernel(
+    part, place, skip_ref, x_ref, gate_ref, left_ref, b_t_ref, before_ref, after_ref, sum_ref, weight_ref,
+    scaled, carried,
+):
     tokens = x_ref.shape[0]
-    lanes = slice(group * GROUP, (group + 1) * GROUP)
-    spread = spread_matrix(group * GROUP, GROUP)
+    group = lax.rem(place[CORE] * (HALF // GROUP) + part, WIDTH // GROUP)
+    start = pl.multiple_of(group * GROUP, GROUP)
+    lanes = pl.ds(start, GROUP)
+    spread = spread_matrix(start, GROUP)
     lane = iota((1, GROUP), 1)
     skip = jnp.zeros((1, GROUP), F32)
     for h in range(GROUP // HEAD):
         skip = jnp.where(lane // HEAD == h, skip_ref[group * (GROUP // HEAD) + h], skip)
     state = jnp.zeros((STATE, GROUP), F32)
     down = 2.0**-SHIFT
+    before = dot(before_ref[...], spread)
     for s in range(tokens // SUB):
         rows = slice(s * SUB, (s + 1) * SUB)
-        wide = dot(factors_ref[s, : SUB + 16], spread)
+        wide = before[s * BEFORE : (s + 1) * BEFORE]
         scaled[rows] = (x_ref[rows, lanes].astype(F32) * wide[:SUB]).astype(BF16)
         decayed = state * wide[SUB : SUB + 1]
         carried[rows] = decayed.astype(BF16)
         state = (decayed + dot(b_t_ref[rows], scaled[rows])) * down
+    after = dot(after_ref[...], spread)
     for s in range(tokens // SUB):
         rows = slice(s * SUB, (s + 1) * SUB)
-        wide = dot(factors_ref[s, SUB + 16 :], spread)
+        wide = after[s * AFTER : (s + 1) * AFTER]
         own = dot(left_ref[rows], jnp.concatenate([scaled[rows], carried[rows]], axis=0))
         summed = own * wide[:SUB] + skip * x_ref[rows, lanes].astype(F32)
         h = 0.5 * gate_ref[rows, lanes].astype(F32)
         silu = h + h * jnp.tanh(h)
-        sum_ref[rows] = (summed * silu).astype(sum_ref.dtype)
-        weight_ref[rows] = (wide[SUB:] * silu).astype(weight_ref.dtype)
-
-
-def local(group, skip, x, gate, left, b_t, factors):
+        sum_ref[rows] = summed * silu
+        weight_ref[rows] = (wide[SUB:] * silu).astype(BF16)
+
+
+def local(part, place, skip, x, gate, left, b_t, before, after):
     tokens = x.shape[0]
     vmem = pl.BlockSpec(memory_space=pltpu.VMEM)
     return pl.pallas_call(
-        functools.partial(local_kernel, group),
-        in_specs=[pl.BlockSpec(memory_space=pltpu.SMEM)] + [vmem] * 5,
+        functools.partial(local_kernel, part),
+        in_specs=[pl.BlockSpec(memory_space=pltpu.SMEM)] * 2 + [vmem] * 6,
         out_specs=[vmem] * 2,
         out_shape=[jax.ShapeDtypeStruct((tokens, GROUP), F32), jax.ShapeDtypeStruct((tokens, GROUP), BF16)],
         scratch_shapes=[pltpu.VMEM((tokens, GROUP), BF16)] * 2,
         name="local",
         compiler_params=pltpu.CompilerParams(vmem_limit_bytes=LIMIT),
-    )(skip, x, gate, left, b_t, factors)
-
-
-def output_kernel(place, c_ref, gain_ref, own_ref, other_ref, *refs):
-    groups = WIDTH // GROUP
+    )(place, skip, x, gate, left, b_t, before, after)
+
+
+def output_kernel(mine, place, c_ref, gain_ref, state_ref, *refs):
+    groups = HALF // GROUP
     sums, weights = refs[:groups], refs[groups : 2 * groups]
-    out_hbm, state, out, sems = refs[2 * groups :]
-    mine = pl.multiple_of(place[CORE] * HALF, HALF)
-    other = pl.multiple_of((1 - place[CORE]) * HALF, HALF)
-    state[:, pl.ds(mine, HALF)] = own_ref[...].astype(BF16)
-    state[:, pl.ds(other, HALF)] = other_ref[...].astype(BF16)
+    out_hbm, state, out, sems = refs[-4:]
+    state[...] = state_ref[...].astype(BF16)
+    half = pl.multiple_of((place[CORE] if mine else 1 - place[CORE]) * HALF, HALF)
     same = iota((GROUP, GROUP), 0) // HEAD == iota((GROUP, GROUP), 1) // HEAD
     mean = jnp.where(same, 1.0 / HEAD, 0.0).astype(BF16)
     copies = []
@@ -317,33 +353,38 @@
         rows = slice(i * OUT_STEP, (i + 1) * OUT_STEP)
         for g in range(groups):
             lanes = slice(g * GROUP, (g + 1) * GROUP)
+            gain = gain_ref[:, pl.ds(pl.multiple_of(half + g * GROUP, GROUP), GROUP)]
             entering = dot(c_ref[rows], state[:, lanes])
-            gated = sums[g][rows].astype(F32) + weights[g][rows].astype(F32) * entering
+            gated = sums[g][rows] + weights[g][rows].astype(F32) * entering
             square = dot((gated * gated).astype(BF16), mean)
-            out[rows, lanes] = (gated * lax.rsqrt(square + 1e-5) * gain_ref[:, lanes]).astype(BF16)
+            out[rows, lanes] = (gated * lax.rsqrt(square + 1e-5) * gain).astype(BF16)
         where = pl.ds(i * OUT_STEP, OUT_STEP)
-        copies.append(pltpu.make_async_copy(out.at[where], out_hbm.at[where], sems.at[i]))
+        copies.append(pltpu.make_async_copy(out.at[where], out_hbm.at[where, pl.ds(half, HALF)], sems.at[i]))
         copies[-1].start()
     for copy in copies:
         copy.wait()
 
 
-def output(place, c, gain, own, other, sums, weights):
+def output(mine, place, c, gain, state, parts, *half_done):
     tokens = c.shape[0]
-    vmem = pl.BlockSpec(memory_space=pltpu.VMEM)
-    return pl.pallas_call(
-        output_kernel,
-        in_specs=[pl.BlockSpec(memory_space=pltpu.SMEM)] + [vmem] * (4 + len(sums) + len(weights)),
-        out_specs=pl.BlockSpec(memory_space=pl.ANY),
+    sums, weights = zip(*parts, strict=True)
+    args = (place, c, gain, state, *sums, *weights)
+    vmem = pl.BlockSpec(memory_space=pltpu.VMEM)
+    hbm = pl.BlockSpec(memory_space=pl.ANY)
+    return pl.pallas_call(
+        functools.partial(output_kernel, mine),
+        in_specs=[pl.BlockSpec(memory_space=pltpu.SMEM)] + [vmem] * (len(args) - 1) + [hbm] * len(half_done),
+        out_specs=hbm,
         out_shape=jax.ShapeDtypeStruct((tokens, WIDTH), BF16),
+        input_output_aliases={len(args): 0} if half_done else {},
         scratch_shapes=[
-            pltpu.VMEM((STATE, WIDTH), BF16),
-            pltpu.VMEM((tokens, WIDTH), BF16),
+            pltpu.VMEM((STATE, HALF), BF16),
+            pltpu.VMEM((tokens, HALF), BF16),
             pltpu.SemaphoreType.DMA((tokens // OUT_STEP,)),
         ],
         name="output",
         compiler_params=pltpu.CompilerParams(vmem_limit_bytes=LIMIT),
-    )(place, c, gain, own, other, *sums, *weights)
+    )(*args, *half_done)
 
 
 def device_of(z, y, x, core):
@@ -368,19 +409,20 @@
     place = jnp.stack([z, r // 8, (r // 2) % 4, r % 2]).astype(jnp.int32)
     piece, chunk = (QUARTER + 8, HALF), (QUARTER, HALF)
 
-    keep, send = end_state(place, x, b, decay)
+    send, x, b, factors = send_state(place, x, b, decay)
     recv = moved(send, CORE, 1)
-    left, b_t, factors = prepare(b, c, decay)
+    keep = keep_state(place, x, b, factors)
+    keep, recv = lax.optimization_barrier((keep, recv))
     parts = []
 
     def work(count, *arrived):
         for _ in range(count):
-            parts.append(local(len(parts), d_skip, x, gate, left, b_t, factors))
+            parts.append(local(len(parts), place, d_skip, x, *shared))
         arrived, parts[-count:] = lax.optimization_barrier((arrived, parts[-count:]))
         return arrived
 
-    (recv,), (left, b_t, factors) = lax.optimization_barrier(((recv,), (left, b_t, factors)))
     u0, *sends = small_call(pair_kernel, "pair", place, (keep, recv), [piece] * 4)
+    shared = prepare(gate, b, c, decay)
     lines = [u0] + list(work(1, *[moved(v, X, s + 1) for s, v in enumerate(sends)]))
     (v0,) = small_call(line_kernel, "line", place, lines, [piece])
     columns = [v0] + list(work(2, *[moved(v0, Y, s) for s in (1, 2, 3)]))
@@ -390,8 +432,11 @@
     entering = [e0] + list(work(1, *[moved(v, X, s + 1) for s, v in enumerate(sends)]))
     own, send = small_call(chip_kernel, "chip", place, entering + [keep, recv], [(STATE, HALF)] * 2)
     other = moved(send, CORE, 1)
-    sums, weights = zip(*parts, strict=True)
-    return output(place, c, norm_gain[None], own, other, sums, weights)
+    half = len(parts) // 2
+    gain = norm_gain[None]
+    out = output(True, place, c, gain, own, parts[:half])
+    out, other = lax.optimization_barrier((out, other))
+    return output(False, place, c, gain, other, parts[half:], out)
 
 
 def solution(mesh):

time: 76.3 us -> 64.6 us (0.85)
  Pallas kernels: 46.2 us -> 36.2 us
  starting transfers between devices: 20.9 us -> 25.6 us
  local copies, waits for them, and re-layouts: 6.6 us -> 1.99 us
  waiting for transfers between devices: 1.37 us -> 0.09 us
    pallas_call x9 -> x11, Pallas kernels: 42.6 us -> 32.6 us  [the longest x6 14.7 us: local(): pl.pallas_call(functools.partial(local_kernel, part), in_specs=[pl.BlockS...]
    ppermute x14, starting transfers between devices: 20.9 us -> 25.6 us  [moved(): return lax.ppermute(value, ('grp', 'dev'), pairs)]
    unnamed x20 -> x12, local copies, waits for them, and re-layouts: 6.6 us -> 1.98 us
    ppermute x14, waiting for transfers between devices: 1.37 us -> 0.09 us  [moved(): return lax.ppermute(value, ('grp', 'dev'), pairs)]
  transfers between devices with their start and end apart: 14 -> 14, of which waited for: 1 -> 1; matrix products, arithmetic and copies ran while one was open for 0% -> 0% of each run, Pallas kernels for 37% -> 36%
where the time goes in v3:
time: 64.6 us; the launch traced here: 64.4 us
  Pallas kernels  36.2 us (56%)
  starting transfers between devices  25.6 us (40%)
  local copies, waits for them, and re-layouts  1.99 us (3%)
    ppermute x14, starting transfers between devices, moved(): return lax.ppermute(value, ('grp', 'dev'), pairs)  25.6 us
    pallas_call x6, Pallas kernels, local(): pl.pallas_call(functools.partial(local_kernel, part), in_specs=[pl.BlockS...  14.7 us
    pallas_call x2, Pallas kernels, output(): pl.pallas_call(functools.partial(output_kernel, mine), in_specs=[pl.Block...  7.51 us
    pallas_call x1, Pallas kernels, send_state(): pl.pallas_call(send_state_kernel, in_specs=[pl.BlockSpec(memory_space=plt...  5.6 us
    pallas_call x5, Pallas kernels, small_call(): pl.pallas_call(kernel, in_specs=[pl.BlockSpec(memory_space=pltpu.SMEM)] +...  3.59 us
    pallas_call x1, Pallas kernels, prepare(): pl.pallas_call(prepare_kernel, in_specs=[pl.BlockSpec(memory_space=pltpu....  2.8 us
    pallas_call x1, Pallas kernels, keep_state(): pl.pallas_call(keep_state_kernel, in_specs=[pl.BlockSpec(memory_space=plt...  2.05 us
    unnamed x12, local copies, waits for them, and re-layouts  1.98 us
  transfers between devices with their start and end apart: 14, of which 1 were waited for; matrix products, arithmetic and copies ran while one was open for 0% of the time, Pallas kernels for 36%

profile of v3, /device:TPU:1, one launch (start us, length us, event | category | flops | bytes accessed | tf_op | source)
XLA Modules:
  0.0 64.4 jit_solution(8370741733583436608)
XLA Ops:
  0.0 0.1 pad_add_fusion.place
  0.1 0.0 copy-start.1
  0.1 0.9 %copy-done.1 = f32[24,2048]{1,0:T(8,128)S(1)} copy-done((f32[24,2048]{1,0:T(8,128)S(1)}, f32[24,2048]{1,0:T(8,128)}, u32[]{:S(2)}) %copy-start.1) | copy-done | bytes 196632
  1.0 0.0 copy-start.3
  1.0 1.0 %copy-done.3 = bf16[2048,128]{1,0:T(8,128)(2,1)S(1)} copy-done((bf16[2048,128]{1,0:T(8,128)(2,1)S(1)}, bf16[2048,128]{1,0:T(8,128)(2,1)}, u32[]{:S(2)}) %copy-start.3) | copy-done | bytes 524312
  2.0 0.0 copy-start
  2.1 0.0 copy-start.2
  2.1 5.6 %send_state.1 = (f32[136,768]{1,0:T(8,128)S(1)}, bf16[2048,1536]{1,0:T(8,128)(2,1)S(1)}, bf16[2048,128]{1,0:T(8,128)(2,1)S(1)}, bf16[2064,72]{1,0:T(8,128)(2,1)S(1)}) custom-call(s32[4]{0:T(128)S(1)} %pad_add_fusion.place, bf16[2048,1536]{1,0:T(8,128)(2,1)} %x_hbm.1, bf16[2048,128]{1,0:T(8,128)(2,1)S(1)} %copy-done.3, f32[24,2048]{1,0:T(8,128)S(1)} %copy-done.1), custom_call_target="tpu_custom_call" | custom-call | tf_op jit(solution)/shard_map/send_state/pallas_call | solution.py:110
  7.7 1.5 %collective-permute-start = (f32[136,768]{1,0:T(8,128)S(1)}, f32[136,768]{1,0:T(8,128)S(1)}, u32[]{:S(2)}, u32[]{:S(2)}) collective-permute-start(f32[136,768]{1,0:T(8,128)S(1)} %get-tuple-element.69), channel_id=1, source_target_pairs={{0,1},{1,0},{2,3},{3,2},{4,5},{5,4},{6,7},{7,6},{8,9},{9,8},{10,11... | collective-permute-start | bytes 1253384 | tf_op jit(solution)/shard_map/ppermute | solution.py:404
  9.2 0.0 copy-start.4
  9.2 2.0 %keep_state.1.keep = f32[136,768]{1,0:T(8,128)S(1)} custom-call(s32[4]{0:T(128)S(1)} %pad_add_fusion.place, bf16[2048,1536]{1,0:T(8,128)(2,1)S(1)} %get-tuple-element.66.x.x_ref, bf16[2048,128]{1,0:T(8,128)(2,1)S(1)} %get-tuple-element.67.b.b_ref, bf16[2064,72]{1,0:T(8,128)(2,1)S(1)} %get-tuple-element.68.factors), custom_call_target="tpu_custom_call" | custom-call | tf_op jit(solution)/shard_map/keep_state/pallas_call | solution.py:136
  11.2 0.0 collective-permute-done.recv
  11.2 0.6 pair.1
  11.8 1.4 %collective-permute-start.1 = (f32[40,768]{1,0:T(8,128)S(1)}, f32[40,768]{1,0:T(8,128)S(1)}, u32[]{:S(2)}, u32[]{:S(2)}) collective-permute-start(f32[40,768]{1,0:T(8,128)S(1)} %get-tuple-element.73), channel_id=1, source_target_pairs={{0,2},{1,3},{2,4},{3,5},{4,6},{5,7},{6,0},{7,1},{8,10},{9,11},{10,... | collective-permute-start | bytes 368648 | tf_op jit(solution)/shard_map/ppermute | solution.py:404
  13.2 2.5 %collective-permute-start.2 = (f32[40,768]{1,0:T(8,128)S(1)}, f32[40,768]{1,0:T(8,128)S(1)}, u32[]{:S(2)}, u32[]{:S(2)}) collective-permute-start(f32[40,768]{1,0:T(8,128)S(1)} %get-tuple-element.74), channel_id=1, source_target_pairs={{0,4},{1,5},{2,6},{3,7},{4,0},{5,1},{6,2},{7,3},{8,12},{9,13},{10,... | collective-permute-start | bytes 368648 | tf_op jit(solution)/shard_map/ppermute | solution.py:404
  15.7 1.1 %collective-permute-start.3 = (f32[40,768]{1,0:T(8,128)S(1)}, f32[40,768]{1,0:T(8,128)S(1)}, u32[]{:S(2)}, u32[]{:S(2)}) collective-permute-start(f32[40,768]{1,0:T(8,128)S(1)} %get-tuple-element.75), channel_id=1, source_target_pairs={{0,6},{1,7},{2,0},{3,1},{4,2},{5,3},{6,4},{7,5},{8,14},{9,15},{10,... | collective-permute-start | bytes 368648 | tf_op jit(solution)/shard_map/ppermute | solution.py:404
  16.8 0.0 copy-done
  16.8 0.0 copy-done.2
  16.8 2.8 %prepare.1 = (bf16[2048,1536]{1,0:T(8,128)(2,1)S(1)}, bf16[2048,256]{1,0:T(8,128)(2,1)S(1)}, bf16[2048,128]{1,0:T(8,128)(2,1)S(1)}, bf16[2304,72]{1,0:T(8,128)(2,1)S(1)}, bf16[4096,72]{1,0:T(8,128)(2,1)S(1)}) custom-call(bf16[2048,1536]{1,0:T(8,128)(2,1)} %gate_hbm.1, bf16[2048,128]{1,0:T(8,128)(2,1)S(1)} %get-tuple-element.67.b.b_ref, ...), custom_call_target="tpu_custom_call" | custom-call | tf_op jit(solution)/shard_map/prepare/pallas_call | solution.py:277
  19.6 0.0 copy-done.4
  19.6 2.5 %local.6 = (f32[2048,256]{1,0:T(8,128)S(1)}, bf16[2048,256]{1,0:T(8,128)(2,1)S(1)}) custom-call(s32[4]{0:T(128)S(1)} %pad_add_fusion.place, f32[24]{0:T(128)S(1)} %copy-done.4, bf16[2048,1536]{1,0:T(8,128)(2,1)S(1)} %get-tuple-element.66.x.x_ref, bf16[2048,1536]{1,0:T(8,128)(2,1)S(1)} %get-tuple-element.76.gate_ref, ...), custom_call_target="tpu_custom_call" | custom-call | tf_op jit(solution)/shard_map/local/pallas_call | solution.py:332
  22.1 0.0 collective-permute-done.1.u1
  22.1 0.0 collective-permute-done.2.u2
  22.1 0.0 collective-permute-done.3.u3
  22.1 0.6 line.1.v0
  22.8 1.4 %collective-permute-start.4 = (f32[40,768]{1,0:T(8,128)S(1)}, f32[40,768]{1,0:T(8,128)S(1)}, u32[]{:S(2)}, u32[]{:S(2)}) collective-permute-start(f32[40,768]{1,0:T(8,128)S(1)} %line.1.v0), channel_id=1, source_target_pairs={{0,8},{1,9},{2,10},{3,11},{4,12},{5,13},{6,14},{7,15},{8,16},{9,17... | collective-permute-start | bytes 368648 | tf_op jit(solution)/shard_map/ppermute | solution.py:404
  24.2 2.6 %collective-permute-start.5 = (f32[40,768]{1,0:T(8,128)S(1)}, f32[40,768]{1,0:T(8,128)S(1)}, u32[]{:S(2)}, u32[]{:S(2)}) collective-permute-start(f32[40,768]{1,0:T(8,128)S(1)} %line.1.v0), channel_id=1, source_target_pairs={{0,16},{1,17},{2,18},{3,19},{4,20},{5,21},{6,22},{7,23},{8,24},{9,... | collective-permute-start | bytes 368648 | tf_op jit(solution)/shard_map/ppermute | solution.py:404
  26.8 1.1 %collective-permute-start.6 = (f32[40,768]{1,0:T(8,128)S(1)}, f32[40,768]{1,0:T(8,128)S(1)}, u32[]{:S(2)}, u32[]{:S(2)}) collective-permute-start(f32[40,768]{1,0:T(8,128)S(1)} %line.1.v0), channel_id=1, source_target_pairs={{0,24},{1,25},{2,26},{3,27},{4,28},{5,29},{6,30},{7,31},{8,0},{9,1... | collective-permute-start | bytes 368648 | tf_op jit(solution)/shard_map/ppermute | solution.py:404
  27.9 2.4 %local.7 = (f32[2048,256]{1,0:T(8,128)S(1)}, bf16[2048,256]{1,0:T(8,128)(2,1)S(1)}) custom-call(s32[4]{0:T(128)S(1)} %pad_add_fusion.place, f32[24]{0:T(128)S(1)} %copy-done.4, bf16[2048,1536]{1,0:T(8,128)(2,1)S(1)} %get-tuple-element.66.x.x_ref, bf16[2048,1536]{1,0:T(8,128)(2,1)S(1)} %get-tuple-element.76.gate_ref, ...), custom_call_target="tpu_custom_call" | custom-call | tf_op jit(solution)/shard_map/local/pallas_call | solution.py:332
  30.2 2.5 %local.8 = (f32[2048,256]{1,0:T(8,128)S(1)}, bf16[2048,256]{1,0:T(8,128)(2,1)S(1)}) custom-call(s32[4]{0:T(128)S(1)} %pad_add_fusion.place, f32[24]{0:T(128)S(1)} %copy-done.4, bf16[2048,1536]{1,0:T(8,128)(2,1)S(1)} %get-tuple-element.66.x.x_ref, bf16[2048,1536]{1,0:T(8,128)(2,1)S(1)} %get-tuple-element.76.gate_ref, ...), custom_call_target="tpu_custom_call" | custom-call | tf_op jit(solution)/shard_map/local/pallas_call | solution.py:332
  32.7 0.0 collective-permute-done.4.v1
  32.7 0.0 collective-permute-done.5.v2
  32.7 0.0 collective-permute-done.6.v3
  32.8 0.7 %plane.1 = (f32[40,768]{1,0:T(8,128)S(1)}, f32[40,768]{1,0:T(8,128)S(1)}) custom-call(s32[4]{0:T(128)S(1)} %pad_add_fusion.place, f32[40,768]{1,0:T(8,128)S(1)} %line.1.v0, f32[40,768]{1,0:T(8,128)S(1)} %collective-permute-done.4.v1, f32[40,768]{1,0:T(8,128)S(1)} %collective-permute-done.5.v2, f32[40,768]{1,0:T(8,128)S(1)} %collective-permute-done.6.v3), custom_call_target="tpu_custom_call" | custom-call | tf_op jit(solution)/shard_map/plane/pallas_call | solution.py:149
  33.5 1.7 %collective-permute-start.7 = (f32[40,768]{1,0:T(8,128)S(1)}, f32[40,768]{1,0:T(8,128)S(1)}, u32[]{:S(2)}, u32[]{:S(2)}) collective-permute-start(f32[40,768]{1,0:T(8,128)S(1)} %get-tuple-element.93.w0), channel_id=1, source_target_pairs={{0,32},{1,33},{2,34},{3,35},{4,36},{5,37},{6,38},{7,39},{8,40},{9,... | collective-permute-start | bytes 368648 | tf_op jit(solution)/shard_map/ppermute | solution.py:404
  35.2 3.3 %collective-permute-start.8 = (f32[40,768]{1,0:T(8,128)S(1)}, f32[40,768]{1,0:T(8,128)S(1)}, u32[]{:S(2)}, u32[]{:S(2)}) collective-permute-start(f32[40,768]{1,0:T(8,128)S(1)} %get-tuple-element.93.w0), channel_id=1, source_target_pairs={{0,64},{1,65},{2,66},{3,67},{4,68},{5,69},{6,70},{7,71},{8,72},{9,... | collective-permute-start | bytes 368648 | tf_op jit(solution)/shard_map/ppermute | solution.py:404
  38.5 0.7 %collective-permute-start.9 = (f32[40,768]{1,0:T(8,128)S(1)}, f32[40,768]{1,0:T(8,128)S(1)}, u32[]{:S(2)}, u32[]{:S(2)}) collective-permute-start(f32[40,768]{1,0:T(8,128)S(1)} %get-tuple-element.93.w0), channel_id=1, source_target_pairs={{0,96},{1,97},{2,98},{3,99},{4,100},{5,101},{6,102},{7,103},{8,104... | collective-permute-start | bytes 368648 | tf_op jit(solution)/shard_map/ppermute | solution.py:404
  39.2 2.4 %local.9 = (f32[2048,256]{1,0:T(8,128)S(1)}, bf16[2048,256]{1,0:T(8,128)(2,1)S(1)}) custom-call(s32[4]{0:T(128)S(1)} %pad_add_fusion.place, f32[24]{0:T(128)S(1)} %copy-done.4, bf16[2048,1536]{1,0:T(8,128)(2,1)S(1)} %get-tuple-element.66.x.x_ref, bf16[2048,1536]{1,0:T(8,128)(2,1)S(1)} %get-tuple-element.76.gate_ref, ...), custom_call_target="tpu_custom_call" | custom-call | tf_op jit(solution)/shard_map/local/pallas_call | solution.py:332
  41.6 2.5 %local.10 = (f32[2048,256]{1,0:T(8,128)S(1)}, bf16[2048,256]{1,0:T(8,128)(2,1)S(1)}) custom-call(s32[4]{0:T(128)S(1)} %pad_add_fusion.place, f32[24]{0:T(128)S(1)} %copy-done.4, bf16[2048,1536]{1,0:T(8,128)(2,1)S(1)} %get-tuple-element.66.x.x_ref, bf16[2048,1536]{1,0:T(8,128)(2,1)S(1)} %get-tuple-element.76.gate_ref, ...), custom_call_target="tpu_custom_call" | custom-call | tf_op jit(solution)/shard_map/local/pallas_call | solution.py:332
  44.1 0.0 collective-permute-done.7.w1
  44.1 0.0 collective-permute-done.8.w2
  44.1 0.0 collective-permute-done.9.w3
  44.1 1.0 %enter.1 = (f32[32,768]{1,0:T(8,128)S(1)}, f32[32,768]{1,0:T(8,128)S(1)}, f32[32,768]{1,0:T(8,128)S(1)}, f32[32,768]{1,0:T(8,128)S(1)}) custom-call(s32[4]{0:T(128)S(1)} %pad_add_fusion.place, f32[40,768]{1,0:T(8,128)S(1)} %get-tuple-element.93.w0, f32[40,768]{1,0:T(8,128)S(1)} %collective-permute-done.7.w1, f32[40,768]{1,0:T(8,128)S(1)} %collective-permute-done.8.w2, ...), custom_call_target="tpu_custom_call" | custom-call | tf_op jit(solution)/shard_map/enter/pallas_call | solution.py:149
  45.1 0.4 collective-permute-start.10
  45.5 2.4 %collective-permute-start.11 = (f32[32,768]{1,0:T(8,128)S(1)}, f32[32,768]{1,0:T(8,128)S(1)}, u32[]{:S(2)}, u32[]{:S(2)}) collective-permute-start(f32[32,768]{1,0:T(8,128)S(1)} %get-tuple-element.104), channel_id=1, source_target_pairs={{0,4},{1,5},{2,6},{3,7},{4,0},{5,1},{6,2},{7,3},{8,12},{9,13},{10,... | collective-permute-start | bytes 294920 | tf_op jit(solution)/shard_map/ppermute | solution.py:404
  47.9 0.0 copy-start.5
  47.9 1.1 %collective-permute-start.12 = (f32[32,768]{1,0:T(8,128)S(1)}, f32[32,768]{1,0:T(8,128)S(1)}, u32[]{:S(2)}, u32[]{:S(2)}) collective-permute-start(f32[32,768]{1,0:T(8,128)S(1)} %get-tuple-element.105), channel_id=1, source_target_pairs={{0,6},{1,7},{2,0},{3,1},{4,2},{5,3},{6,4},{7,5},{8,14},{9,15},{10,... | collective-permute-start | bytes 294920 | tf_op jit(solution)/shard_map/ppermute | solution.py:404
  48.9 2.5 %local.11 = (f32[2048,256]{1,0:T(8,128)S(1)}, bf16[2048,256]{1,0:T(8,128)(2,1)S(1)}) custom-call(s32[4]{0:T(128)S(1)} %pad_add_fusion.place, f32[24]{0:T(128)S(1)} %copy-done.4, bf16[2048,1536]{1,0:T(8,128)(2,1)S(1)} %get-tuple-element.66.x.x_ref, bf16[2048,1536]{1,0:T(8,128)(2,1)S(1)} %get-tuple-element.76.gate_ref, ...), custom_call_target="tpu_custom_call" | custom-call | tf_op jit(solution)/shard_map/local/pallas_call | solution.py:332
  51.4 0.0 collective-permute-done.10.e1
  51.4 0.0 collective-permute-done.11.e2
  51.4 0.1 collective-permute-done.12.e3
  51.5 0.7 %chip.1 = (f32[128,768]{1,0:T(8,128)S(1)}, f32[128,768]{1,0:T(8,128)S(1)}) custom-call(s32[4]{0:T(128)S(1)} %pad_add_fusion.place, f32[32,768]{1,0:T(8,128)S(1)} %get-tuple-element.102.e0, f32[32,768]{1,0:T(8,128)S(1)} %collective-permute-done.10.e1, f32[32,768]{1,0:T(8,128)S(1)} %collective-permute-done.11.e2, f32[32,768]{1,0:T(8,128)S(1)} %collective-permute-done.12.e3, ...), custom_call_target="tpu_custom_call" | custom-call | tf_op jit(solution)/shard_map/chip/pallas_call | solution.py:149
  52.1 4.5 %collective-permute-start.13 = (f32[128,768]{1,0:T(8,128)S(1)}, f32[128,768]{1,0:T(8,128)S(1)}, u32[]{:S(2)}, u32[]{:S(2)}) collective-permute-start(f32[128,768]{1,0:T(8,128)S(1)} %get-tuple-element.118), channel_id=1, source_target_pairs={{0,1},{1,0},{2,3},{3,2},{4,5},{5,4},{6,7},{7,6},{8,9},{9,8},{10,11... | collective-permute-start | bytes 1179656 | tf_op jit(solution)/shard_map/ppermute | solution.py:404
  56.6 0.0 copy-done.5
  56.7 3.7 %output.2.refs_6_ = bf16[2048,1536]{1,0:T(8,128)(2,1)} custom-call(s32[4]{0:T(128)S(1)} %pad_add_fusion.place, bf16[2048,128]{1,0:T(8,128)(2,1)S(1)} %copy-done, f32[1,1536]{1,0:T(1,128)S(1)} %broadcast_in_dim.3.gain_ref, f32[128,768]{1,0:T(8,128)S(1)} %get-tuple-element.111.state_ref, f32[2048,256]{1,0:T(8,128)S(1)} %get-tuple-element.112.refs_0_, ...), custom_call_target="tpu_custom_call" | custom-call | tf_op jit(solution)/shard_map/output/pallas_call | solution.py:374
  60.4 0.0 collective-permute-done.13.state_ref
  60.4 3.8 %output.3 = bf16[2048,1536]{1,0:T(8,128)(2,1)} custom-call(s32[4]{0:T(128)S(1)} %pad_add_fusion.place, bf16[2048,128]{1,0:T(8,128)(2,1)S(1)} %copy-done, f32[1,1536]{1,0:T(1,128)S(1)} %broadcast_in_dim.3.gain_ref, f32[128,768]{1,0:T(8,128)S(1)} %collective-permute-done.13.state_ref, ...), custom_call_target="tpu_custom_call", output_to_operand_aliasing={{}: (10, {})} | custom-call | tf_op jit(solution)/shard_map/output/pallas_call | solution.py:374
  (1 shorter events, 0.0 us)
Async XLA Ops:
  0.1 0.9 %copy-start.1 = (f32[24,2048]{1,0:T(8,128)S(1)}, f32[24,2048]{1,0:T(8,128)}, u32[]{:S(2)}) copy-start(f32[24,2048]{1,0:T(8,128)} %decay_ref.1) | copy-start | bytes 589828
  1.0 1.0 %copy-start.3 = (bf16[2048,128]{1,0:T(8,128)(2,1)S(1)}, bf16[2048,128]{1,0:T(8,128)(2,1)}, u32[]{:S(2)}) copy-start(bf16[2048,128]{1,0:T(8,128)(2,1)} %b_hbm.1) | copy-start | bytes 1572868
  2.0 14.8 %copy-start = (bf16[2048,128]{1,0:T(8,128)(2,1)S(1)}, bf16[2048,128]{1,0:T(8,128)(2,1)}, u32[]{:S(2)}) copy-start(bf16[2048,128]{1,0:T(8,128)(2,1)} %c_ref.5) | copy-start | bytes 1572868
  2.1 14.8 %copy-start.2 = (f32[24,2048]{1,0:T(8,128)S(1)}, f32[24,2048]{1,0:T(8,128)}, u32[]{:S(2)}) copy-start(f32[24,2048]{1,0:T(8,128)} %decay_ref.1) | copy-start | bytes 589828
  7.7 3.6 %collective-permute-start = (f32[136,768]{1,0:T(8,128)S(1)}, f32[136,768]{1,0:T(8,128)S(1)}, u32[]{:S(2)}, u32[]{:S(2)}) collective-permute-start(f32[136,768]{1,0:T(8,128)S(1)} %get-tuple-element.69), channel_id=1, source_target_pairs={{0,1},{1,0},{2,3},{3,2},{4,5},{5,4},{6,7},{7,6},{8,9},{9,8},{10,11... | collective-permute-start | bytes 1253384 | tf_op jit(solution)/shard_map/ppermute | solution.py:404
  9.2 10.5 %copy-start.4 = (f32[24]{0:T(128)S(1)}, f32[24]{0:T(128)}, u32[]{:S(2)}) copy-start(f32[24]{0:T(128)} %skip_ref.11) | copy-start | bytes 292
  11.8 10.3 %collective-permute-start.1 = (f32[40,768]{1,0:T(8,128)S(1)}, f32[40,768]{1,0:T(8,128)S(1)}, u32[]{:S(2)}, u32[]{:S(2)}) collective-permute-start(f32[40,768]{1,0:T(8,128)S(1)} %get-tuple-element.73), channel_id=1, source_target_pairs={{0,2},{1,3},{2,4},{3,5},{4,6},{5,7},{6,0},{7,1},{8,10},{9,11},{10,... | collective-permute-start | bytes 368648 | tf_op jit(solution)/shard_map/ppermute | solution.py:404
  13.2 8.9 %collective-permute-start.2 = (f32[40,768]{1,0:T(8,128)S(1)}, f32[40,768]{1,0:T(8,128)S(1)}, u32[]{:S(2)}, u32[]{:S(2)}) collective-permute-start(f32[40,768]{1,0:T(8,128)S(1)} %get-tuple-element.74), channel_id=1, source_target_pairs={{0,4},{1,5},{2,6},{3,7},{4,0},{5,1},{6,2},{7,3},{8,12},{9,13},{10,... | collective-permute-start | bytes 368648 | tf_op jit(solution)/shard_map/ppermute | solution.py:404
  15.7 6.5 %collective-permute-start.3 = (f32[40,768]{1,0:T(8,128)S(1)}, f32[40,768]{1,0:T(8,128)S(1)}, u32[]{:S(2)}, u32[]{:S(2)}) collective-permute-start(f32[40,768]{1,0:T(8,128)S(1)} %get-tuple-element.75), channel_id=1, source_target_pairs={{0,6},{1,7},{2,0},{3,1},{4,2},{5,3},{6,4},{7,5},{8,14},{9,15},{10,... | collective-permute-start | bytes 368648 | tf_op jit(solution)/shard_map/ppermute | solution.py:404
  22.8 9.9 %collective-permute-start.4 = (f32[40,768]{1,0:T(8,128)S(1)}, f32[40,768]{1,0:T(8,128)S(1)}, u32[]{:S(2)}, u32[]{:S(2)}) collective-permute-start(f32[40,768]{1,0:T(8,128)S(1)} %line.1.v0), channel_id=1, source_target_pairs={{0,8},{1,9},{2,10},{3,11},{4,12},{5,13},{6,14},{7,15},{8,16},{9,17... | collective-permute-start | bytes 368648 | tf_op jit(solution)/shard_map/ppermute | solution.py:404
  24.2 8.6 %collective-permute-start.5 = (f32[40,768]{1,0:T(8,128)S(1)}, f32[40,768]{1,0:T(8,128)S(1)}, u32[]{:S(2)}, u32[]{:S(2)}) collective-permute-start(f32[40,768]{1,0:T(8,128)S(1)} %line.1.v0), channel_id=1, source_target_pairs={{0,16},{1,17},{2,18},{3,19},{4,20},{5,21},{6,22},{7,23},{8,24},{9,... | collective-permute-start | bytes 368648 | tf_op jit(solution)/shard_map/ppermute | solution.py:404
  26.8 6.0 %collective-permute-start.6 = (f32[40,768]{1,0:T(8,128)S(1)}, f32[40,768]{1,0:T(8,128)S(1)}, u32[]{:S(2)}, u32[]{:S(2)}) collective-permute-start(f32[40,768]{1,0:T(8,128)S(1)} %line.1.v0), channel_id=1, source_target_pairs={{0,24},{1,25},{2,26},{3,27},{4,28},{5,29},{6,30},{7,31},{8,0},{9,1... | collective-permute-start | bytes 368648 | tf_op jit(solution)/shard_map/ppermute | solution.py:404
  33.5 10.6 %collective-permute-start.7 = (f32[40,768]{1,0:T(8,128)S(1)}, f32[40,768]{1,0:T(8,128)S(1)}, u32[]{:S(2)}, u32[]{:S(2)}) collective-permute-start(f32[40,768]{1,0:T(8,128)S(1)} %get-tuple-element.93.w0), channel_id=1, source_target_pairs={{0,32},{1,33},{2,34},{3,35},{4,36},{5,37},{6,38},{7,39},{8,40},{9,... | collective-permute-start | bytes 368648 | tf_op jit(solution)/shard_map/ppermute | solution.py:404
  35.2 8.9 %collective-permute-start.8 = (f32[40,768]{1,0:T(8,128)S(1)}, f32[40,768]{1,0:T(8,128)S(1)}, u32[]{:S(2)}, u32[]{:S(2)}) collective-permute-start(f32[40,768]{1,0:T(8,128)S(1)} %get-tuple-element.93.w0), channel_id=1, source_target_pairs={{0,64},{1,65},{2,66},{3,67},{4,68},{5,69},{6,70},{7,71},{8,72},{9,... | collective-permute-start | bytes 368648 | tf_op jit(solution)/shard_map/ppermute | solution.py:404
  38.5 5.6 %collective-permute-start.9 = (f32[40,768]{1,0:T(8,128)S(1)}, f32[40,768]{1,0:T(8,128)S(1)}, u32[]{:S(2)}, u32[]{:S(2)}) collective-permute-start(f32[40,768]{1,0:T(8,128)S(1)} %get-tuple-element.93.w0), channel_id=1, source_target_pairs={{0,96},{1,97},{2,98},{3,99},{4,100},{5,101},{6,102},{7,103},{8,104... | collective-permute-start | bytes 368648 | tf_op jit(solution)/shard_map/ppermute | solution.py:404
  45.1 6.3 %collective-permute-start.10 = (f32[32,768]{1,0:T(8,128)S(1)}, f32[32,768]{1,0:T(8,128)S(1)}, u32[]{:S(2)}, u32[]{:S(2)}) collective-permute-start(f32[32,768]{1,0:T(8,128)S(1)} %get-tuple-element.103), channel_id=1, source_target_pairs={{0,2},{1,3},{2,4},{3,5},{4,6},{5,7},{6,0},{7,1},{8,10},{9,11},{10,... | collective-permute-start | bytes 294920 | tf_op jit(solution)/shard_map/ppermute | solution.py:404
  45.5 5.9 %collective-permute-start.11 = (f32[32,768]{1,0:T(8,128)S(1)}, f32[32,768]{1,0:T(8,128)S(1)}, u32[]{:S(2)}, u32[]{:S(2)}) collective-permute-start(f32[32,768]{1,0:T(8,128)S(1)} %get-tuple-element.104), channel_id=1, source_target_pairs={{0,4},{1,5},{2,6},{3,7},{4,0},{5,1},{6,2},{7,3},{8,12},{9,13},{10,... | collective-permute-start | bytes 294920 | tf_op jit(solution)/shard_map/ppermute | solution.py:404
  47.9 8.8 %copy-start.5 = (f32[1536]{0:T(1024)S(1)}, f32[1536]{0:T(1024)}, u32[]{:S(2)}) copy-start(f32[1536]{0:T(1024)} %param.13) | copy-start | bytes 18436
  47.9 3.6 %collective-permute-start.12 = (f32[32,768]{1,0:T(8,128)S(1)}, f32[32,768]{1,0:T(8,128)S(1)}, u32[]{:S(2)}, u32[]{:S(2)}) collective-permute-start(f32[32,768]{1,0:T(8,128)S(1)} %get-tuple-element.105), channel_id=1, source_target_pairs={{0,6},{1,7},{2,0},{3,1},{4,2},{5,3},{6,4},{7,5},{8,14},{9,15},{10,... | collective-permute-start | bytes 294920 | tf_op jit(solution)/shard_map/ppermute | solution.py:404
  52.1 8.3 %collective-permute-start.13 = (f32[128,768]{1,0:T(8,128)S(1)}, f32[128,768]{1,0:T(8,128)S(1)}, u32[]{:S(2)}, u32[]{:S(2)}) collective-permute-start(f32[128,768]{1,0:T(8,128)S(1)} %get-tuple-element.118), channel_id=1, source_target_pairs={{0,1},{1,0},{2,3},{3,2},{4,5},{5,4},{6,7},{7,6},{8,9},{9,8},{10,11... | collective-permute-start | bytes 1179656 | tf_op jit(solution)/shard_map/ppermute | solution.py:404

commit v4 on v3

--- a/solution.py
+++ b/solution.py
@@ -19,8 +19,9 @@
 SHIFT = 74
 SHIFT_LOG = 51.29289136
 OUT_STEP = 256
+FETCH = 512
 QUARTER = STATE // 4
-FIRST_LIMIT = 42 * 1024 * 1024
+FETCH_LIMIT = 42 * 1024 * 1024
 PREPARE_LIMIT = 40 * 1024 * 1024
 LIMIT = 18 * 1024 * 1024
 SMALL_LIMIT = 6 * 1024 * 1024
@@ -64,34 +65,23 @@
     return jnp.where(k % HEADS == lane // HEAD, 1.0, 0.0).astype(BF16)
 
 
-def half_state(x, b, factors, scaled, start, out, fetched):
-    lanes = pl.ds(pl.multiple_of(start, HALF), HALF)
-    spread = spread_matrix(start, HALF)
-    tokens = x.shape[0]
-    for i in range(tokens // STEP):
-        fetched(i)
-        rows = slice(i * STEP, (i + 1) * STEP)
-        scaled[rows] = (x[rows, lanes].astype(F32) * dot(factors[rows], spread)).astype(BF16)
-    fetched(tokens // STEP)
-    out[:STATE] = dot(b[...], scaled[...], ((0,), (0,)))
-    out[STATE:] = dot(factors[tokens:], spread)[:8]
-
-
-def send_state_kernel(place, x_hbm, b_hbm, decay_hbm, send_ref, x, b, factors, decay, scaled, sems):
-    tokens = x.shape[0]
-    steps = tokens // STEP
-    fetch_decay = pltpu.make_async_copy(decay_hbm, decay, sems.at[steps + 1])
-    fetch_decay.start()
+def half_copies(place, mine, source, target, sems):
+    start = pl.multiple_of((place[CORE] if mine else 1 - place[CORE]) * HALF, HALF)
     copies = []
-    for i in range(steps):
-        rows = pl.ds(i * STEP, STEP)
-        copies.append(pltpu.make_async_copy(x_hbm.at[rows], x.at[rows], sems.at[i]))
-    copies.append(pltpu.make_async_copy(b_hbm, b, sems.at[steps]))
+    for i in range(target.shape[0] // FETCH):
+        rows = pl.ds(i * FETCH, FETCH)
+        copies.append(pltpu.make_async_copy(source.at[rows, pl.ds(start, HALF)], target.at[rows], sems.at[i]))
+    return copies
+
+
+def factors_kernel(place, x_hbm, decay, x_send, x_keep, factors, sems):
+    copies = half_copies(place, False, x_hbm, x_send, sems.at[0]) + half_copies(place, True, x_hbm, x_keep, sems.at[1])
     for copy in copies:
         copy.start()
+    tokens = decay.shape[1]
+    steps = tokens // STEP
     row, col = iota((STEP + 16, STEP), 0), iota((STEP + 16, STEP), 1)
     later = jnp.where((col > row) | (row >= STEP), 1.0, 0.0).astype(BF16)
-    fetch_decay.wait()
     sums = []
     for i in range(steps):
         part = decay[:, i * STEP : (i + 1) * STEP]
@@ -101,45 +91,51 @@
         factors[i * STEP : (i + 1) * STEP] = spread_parts(jnp.exp(sums[i][:STEP] + after))
         after = after + sums[i][STEP : STEP + 1]
     factors[tokens:] = spread_parts(jnp.exp(jnp.broadcast_to(after, (16, 3 * HEADS))))
-    half_state(x, b, factors, scaled, (1 - place[CORE]) * HALF, send_ref, lambda i: copies[i].wait())
-
-
-def send_state(place, x, b, decay):
+    for copy in copies:
+        copy.wait()
+
+
+def decay_factors(place, x, decay):
     tokens = x.shape[0]
     vmem = pl.BlockSpec(memory_space=pltpu.VMEM)
     return pl.pallas_call(
-        send_state_kernel,
-        in_specs=[pl.BlockSpec(memory_space=pltpu.SMEM)] + [pl.BlockSpec(memory_space=pltpu.HBM)] * 3,
-        out_specs=[vmem] * 4,
+        factors_kernel,
+        in_specs=[pl.BlockSpec(memory_space=pltpu.SMEM), pl.BlockSpec(memory_space=pl.ANY), vmem],
+        out_specs=[vmem] * 3,
         out_shape=[
-            jax.ShapeDtypeStruct((ROWS, HALF), F32),
-            jax.ShapeDtypeStruct(x.shape, BF16),
-            jax.ShapeDtypeStruct(b.shape, BF16),
+            jax.ShapeDtypeStruct((tokens, HALF), BF16),
+            jax.ShapeDtypeStruct((tokens, HALF), BF16),
             jax.ShapeDtypeStruct((tokens + 16, 3 * HEADS), BF16),
         ],
-        scratch_shapes=[
-            pltpu.VMEM(decay.shape, F32),
-            pltpu.VMEM((tokens, HALF), BF16),
-            pltpu.SemaphoreType.DMA((tokens // STEP + 2,)),
-        ],
-        name="send_state",
-        compiler_params=pltpu.CompilerParams(vmem_limit_bytes=FIRST_LIMIT),
-    )(place, x, b, decay)
-
-
-def keep_state_kernel(place, x, b, factors, keep_ref, scaled):
-    half_state(x, b, factors, scaled, place[CORE] * HALF, keep_ref, lambda i: None)
-
-
-def keep_state(place, x, b, factors):
-    vmem = pl.BlockSpec(memory_space=pltpu.VMEM)
-    return pl.pallas_call(
-        keep_state_kernel,
+        scratch_shapes=[pltpu.SemaphoreType.DMA((2, tokens // FETCH))],
+        name="decay_factors",
+        compiler_params=pltpu.CompilerParams(vmem_limit_bytes=FETCH_LIMIT),
+    )(place, x, decay)
+
+
+def half_state(x, b, factors, scaled, start, out):
+    spread = spread_matrix(start, HALF)
+    tokens = x.shape[0]
+    for i in range(tokens // STEP):
+        rows = slice(i * STEP, (i + 1) * STEP)
+        scaled[rows] = (x[rows].astype(F32) * dot(factors[rows], spread)).astype(BF16)
+    out[:STATE] = dot(b[...], scaled[...], ((0,), (0,)))
+    out[STATE:] = dot(factors[tokens:], spread)[:8]
+
+
+def state_kernel(mine, place, x, b, factors, out, scaled):
+    half_state(x, b, factors, scaled, (place[CORE] if mine else 1 - place[CORE]) * HALF, out)
+
+
+def end_state(mine, place, x, b, factors):
+    vmem = pl.BlockSpec(memory_space=pltpu.VMEM)
+    return pl.pallas_call(
+        functools.partial(state_kernel, mine),
         in_specs=[pl.BlockSpec(memory_space=pltpu.SMEM)] + [vmem] * 3,
         out_specs=vmem,
         out_shape=jax.ShapeDtypeStruct((ROWS, HALF), F32),
-        scratch_shapes=[pltpu.VMEM((x.shape[0], HALF), BF16)],
-        name="keep_state",
+        scratch_shapes=[pltpu.VMEM(x.shape, BF16)],
+        name="end_state",
         compiler_params=pltpu.CompilerParams(vmem_limit_bytes=LIMIT),
     )(place, x, b, factors)
 
@@ -240,7 +236,6 @@
 
 
 BEFORE = SUB + 16
-AFTER = 2 * SUB
 
 
 def prepare_kernel(gate_hbm, b_ref, c_ref, decay_ref, gate, left_ref, b_t_ref, before_ref, after_ref, sem):
@@ -257,10 +252,11 @@
         cumul = decay_sums(upto, jnp.concatenate([decay] * 3, axis=0))
         end = cumul[SUB - 1 : SUB]
         shifted = end + SHIFT_LOG
-        exponents = [shifted - cumul, jnp.broadcast_to(shifted, (16, 3 * HEADS)), cumul - shifted, cumul + start]
+        ends = [jnp.broadcast_to(v, (8, 3 * HEADS)) for v in (shifted, shifted + start)]
+        exponents = [shifted - cumul, *ends, cumul - shifted]
         factors = spread_parts(jnp.exp(jnp.concatenate(exponents, axis=0)))
         before_ref[s * BEFORE : (s + 1) * BEFORE] = factors[:BEFORE]
-        after_ref[s * AFTER : (s + 1) * AFTER] = factors[BEFORE:]
+        after_ref[rows] = factors[BEFORE:]
         start = start + end
         b, c = b_ref[rows], c_ref[rows]
         scores = jnp.where(causal, dot(c, b, ((1,), (1,))), 0.0)
@@ -283,7 +279,7 @@
             jax.ShapeDtypeStruct((tokens, SUB + STATE), BF16),
             jax.ShapeDtypeStruct((tokens, SUB), BF16),
             jax.ShapeDtypeStruct((subs * BEFORE, 3 * HEADS), BF16),
-            jax.ShapeDtypeStruct((subs * AFTER, 3 * HEADS), BF16),
+            jax.ShapeDtypeStruct((tokens, 3 * HEADS), BF16),
         ],
         scratch_shapes=[pltpu.SemaphoreType.DMA],
         name="prepare",
@@ -299,6 +295,8 @@
     group = lax.rem(place[CORE] * (HALF // GROUP) + part, WIDTH // GROUP)
     start = pl.multiple_of(group * GROUP, GROUP)
     lanes = pl.ds(start, GROUP)
+    at = part % (HALF // GROUP) * GROUP
+    x_lanes = slice(at, at + GROUP)
     spread = spread_matrix(start, GROUP)
     lane = iota((1, GROUP), 1)
     skip = jnp.zeros((1, GROUP), F32)
@@ -310,20 +308,20 @@
     for s in range(tokens // SUB):
         rows = slice(s * SUB, (s + 1) * SUB)
         wide = before[s * BEFORE : (s + 1) * BEFORE]
-        scaled[rows] = (x_ref[rows, lanes].astype(F32) * wide[:SUB]).astype(BF16)
+        scaled[rows] = (x_ref[rows, x_lanes].astype(F32) * wide[:SUB]).astype(BF16)
         decayed = state * wide[SUB : SUB + 1]
         carried[rows] = decayed.astype(BF16)
         state = (decayed + dot(b_t_ref[rows], scaled[rows])) * down
     after = dot(after_ref[...], spread)
     for s in range(tokens // SUB):
         rows = slice(s * SUB, (s + 1) * SUB)
-        wide = after[s * AFTER : (s + 1) * AFTER]
         own = dot(left_ref[rows], jnp.concatenate([scaled[rows], carried[rows]], axis=0))
-        summed = own * wide[:SUB] + skip * x_ref[rows, lanes].astype(F32)
         h = 0.5 * gate_ref[rows, lanes].astype(F32)
         silu = h + h * jnp.tanh(h)
-        sum_ref[rows] = summed * silu
-        weight_ref[rows] = (wide[SUB:] * silu).astype(BF16)
+        factor = after[rows] * silu
+        sum_ref[rows] = own * factor + (skip * x_ref[rows, x_lanes].astype(F32)) * silu
+        entering = s * BEFORE + SUB + 8
+        weight_ref[rows] = (factor * before[entering : entering + 1]).astype(BF16)
 
 
 def local(part, place, skip, x, gate, left, b_t, before, after):
@@ -340,51 +338,77 @@
     )(place, skip, x, gate, left, b_t, before, after)
 
 
-def output_kernel(mine, place, c_ref, gain_ref, state_ref, *refs):
-    groups = HALF // GROUP
-    sums, weights = refs[:groups], refs[groups : 2 * groups]
-    out_hbm, state, out, sems = refs[-4:]
-    state[...] = state_ref[...].astype(BF16)
-    half = pl.multiple_of((place[CORE] if mine else 1 - place[CORE]) * HALF, HALF)
+def finish(start, c_ref, gain_ref, state_ref, sums, weights, out, rows):
     same = iota((GROUP, GROUP), 0) // HEAD == iota((GROUP, GROUP), 1) // HEAD
     mean = jnp.where(same, 1.0 / HEAD, 0.0).astype(BF16)
-    copies = []
+    for g in range(HALF // GROUP):
+        lanes = slice(g * GROUP, (g + 1) * GROUP)
+        gain = gain_ref[:, pl.ds(pl.multiple_of(start + g * GROUP, GROUP), GROUP)]
+        entering = dot(c_ref[rows], state_ref[:, lanes].astype(BF16))
+        gated = sums[g][rows] + weights[g][rows].astype(F32) * entering
+        square = dot((gated * gated).astype(BF16), mean)
+        out[rows, lanes] = (gated * lax.rsqrt(square + 1e-5) * gain).astype(BF16)
+
+
+def own_output_kernel(place, c_ref, gain_ref, state_ref, *refs):
+    groups = HALF // GROUP
+    out = refs[-1]
+    start = place[CORE] * HALF
     for i in range(out.shape[0] // OUT_STEP):
         rows = slice(i * OUT_STEP, (i + 1) * OUT_STEP)
-        for g in range(groups):
-            lanes = slice(g * GROUP, (g + 1) * GROUP)
-            gain = gain_ref[:, pl.ds(pl.multiple_of(half + g * GROUP, GROUP), GROUP)]
-            entering = dot(c_ref[rows], state[:, lanes])
-            gated = sums[g][rows] + weights[g][rows].astype(F32) * entering
-            square = dot((gated * gated).astype(BF16), mean)
-            out[rows, lanes] = (gated * lax.rsqrt(square + 1e-5) * gain).astype(BF16)
+        finish(start, c_ref, gain_ref, state_ref, refs[:groups], refs[groups : 2 * groups], out, rows)
+
+
+def own_output(place, c, gain, state, parts):
+    sums, weights = zip(*parts, strict=True)
+    args = (place, c, gain, state, *sums, *weights)
+    vmem = pl.BlockSpec(memory_space=pltpu.VMEM)
+    return pl.pallas_call(
+        own_output_kernel,
+        in_specs=[pl.BlockSpec(memory_space=pltpu.SMEM)] + [vmem] * (len(args) - 1),
+        out_specs=vmem,
+        out_shape=jax.ShapeDtypeStruct((c.shape[0], HALF), BF16),
+        name="own_output",
+        compiler_params=pltpu.CompilerParams(vmem_limit_bytes=LIMIT),
+    )(*args)
+
+
+def output_kernel(place, c_ref, gain_ref, state_ref, own, *refs):
+    groups = HALF // GROUP
+    out_hbm, out, own_sem, sems = refs[-4:]
+    start = (1 - place[CORE]) * HALF
+    own_lanes = pl.ds(pl.multiple_of(place[CORE] * HALF, HALF), HALF)
+    lanes = pl.ds(pl.multiple_of(start, HALF), HALF)
+    copies = [pltpu.make_async_copy(own, out_hbm.at[:, own_lanes], own_sem)]
+    copies[0].start()
+    for i in range(out.shape[0] // OUT_STEP):
+        rows = slice(i * OUT_STEP, (i + 1) * OUT_STEP)
+        finish(start, c_ref, gain_ref, state_ref, refs[:groups], refs[groups : 2 * groups], out, rows)
         where = pl.ds(i * OUT_STEP, OUT_STEP)
-        copies.append(pltpu.make_async_copy(out.at[where], out_hbm.at[where, pl.ds(half, HALF)], sems.at[i]))
+        copies.append(pltpu.make_async_copy(out.at[where], out_hbm.at[where, lanes], sems.at[i]))
         copies[-1].start()
     for copy in copies:
         copy.wait()
 
 
-def output(mine, place, c, gain, state, parts, *half_done):
+def output(place, c, gain, state, own, parts):
     tokens = c.shape[0]
     sums, weights = zip(*parts, strict=True)
-    args = (place, c, gain, state, *sums, *weights)
-    vmem = pl.BlockSpec(memory_space=pltpu.VMEM)
-    hbm = pl.BlockSpec(memory_space=pl.ANY)
-    return pl.pallas_call(
-        functools.partial(output_kernel, mine),
-        in_specs=[pl.BlockSpec(memory_space=pltpu.SMEM)] + [vmem] * (len(args) - 1) + [hbm] * len(half_done),
-        out_specs=hbm,
+    args = (place, c, gain, state, own, *sums, *weights)
+    vmem = pl.BlockSpec(memory_space=pltpu.VMEM)
+    return pl.pallas_call(
+        output_kernel,
+        in_specs=[pl.BlockSpec(memory_space=pltpu.SMEM)] + [vmem] * (len(args) - 1),
+        out_specs=pl.BlockSpec(memory_space=pl.ANY),
         out_shape=jax.ShapeDtypeStruct((tokens, WIDTH), BF16),
-        input_output_aliases={len(args): 0} if half_done else {},
         scratch_shapes=[
-            pltpu.VMEM((STATE, HALF), BF16),
             pltpu.VMEM((tokens, HALF), BF16),
+            pltpu.SemaphoreType.DMA,
             pltpu.SemaphoreType.DMA((tokens // OUT_STEP,)),
         ],
         name="output",
         compiler_params=pltpu.CompilerParams(vmem_limit_bytes=LIMIT),
-    )(*args, *half_done)
+    )(*args)
 
 
 def device_of(z, y, x, core):
@@ -409,15 +433,18 @@
     place = jnp.stack([z, r // 8, (r // 2) % 4, r % 2]).astype(jnp.int32)
     piece, chunk = (QUARTER + 8, HALF), (QUARTER, HALF)
 
-    send, x, b, factors = send_state(place, x, b, decay)
+    x_send, x_keep, factors = decay_factors(place, x, decay)
+    send = end_state(False, place, x_send, b, factors)
     recv = moved(send, CORE, 1)
-    keep = keep_state(place, x, b, factors)
+    keep = end_state(True, place, x_keep, b, factors)
     keep, recv = lax.optimization_barrier((keep, recv))
     parts = []
 
     def work(count, *arrived):
         for _ in range(count):
-            parts.append(local(len(parts), place, d_skip, x, *shared))
+            part = len(parts)
+            half = x_keep if part < HALF // GROUP else x_send
+            parts.append(local(part, place, d_skip, half, *shared))
         arrived, parts[-count:] = lax.optimization_barrier((arrived, parts[-count:]))
         return arrived
 
@@ -434,9 +461,9 @@
     other = moved(send, CORE, 1)
     half = len(parts) // 2
     gain = norm_gain[None]
-    out = output(True, place, c, gain, own, parts[:half])
-    out, other = lax.optimization_barrier((out, other))
-    return output(False, place, c, gain, other, parts[half:], out)
+    own = own_output(place, c, gain, own, parts[:half])
+    own, other = lax.optimization_barrier((own, other))
+    return output(place, c, gain, other, own, parts[half:])
 
 
 def solution(mesh):

time: 64.6 us -> 61.5 us (0.952)
  Pallas kernels: 36.2 us -> 33.5 us
  local copies, waits for them, and re-layouts: 1.99 us -> 0.96 us
    pallas_call x6, Pallas kernels: 14.7 us -> 12.6 us  [local(): pl.pallas_call(functools.partial(local_kernel, part), in_specs=[pl.BlockS...]
    unnamed x12, local copies, waits for them, and re-layouts: 1.98 us -> 0.95 us
    pallas_call x4 -> x5, Pallas kernels: 15.2 us -> 14.5 us  [the longest x2 4.07 us: end_state(): pl.pallas_call(functools.partial(state_kernel, mine), in_specs=[pl.BlockS...]
  transfers between devices with their start and end apart: 14 -> 14, of which waited for: 1 -> 1; matrix products, arithmetic and copies ran while one was open for 0% -> 0% of each run, Pallas kernels for 36% -> 33%
where the time goes in v4:
time: 61.5 us; the launch traced here: 61.3 us
  Pallas kernels  33.5 us (54%)
  starting transfers between devices  26 us (42%)
  local copies, waits for them, and re-layouts  0.96 us (2%)
    ppermute x14, starting transfers between devices, moved(): return lax.ppermute(value, ('grp', 'dev'), pairs)  26 us
    pallas_call x6, Pallas kernels, local(): pl.pallas_call(functools.partial(local_kernel, part), in_specs=[pl.BlockS...  12.6 us
    pallas_call x2, Pallas kernels, end_state(): pl.pallas_call(functools.partial(state_kernel, mine), in_specs=[pl.BlockS...  4.07 us
    pallas_call x1, Pallas kernels, output(): pl.pallas_call(output_kernel, in_specs=[pl.BlockSpec(memory_space=pltpu.S...  3.8 us
    pallas_call x1, Pallas kernels, decay_factors(): pl.pallas_call(factors_kernel, in_specs=[pl.BlockSpec(memory_space=pltpu....  3.66 us
    pallas_call x5, Pallas kernels, small_call(): pl.pallas_call(kernel, in_specs=[pl.BlockSpec(memory_space=pltpu.SMEM)] +...  3.59 us
    pallas_call x1, Pallas kernels, own_output(): pl.pallas_call(own_output_kernel, in_specs=[pl.BlockSpec(memory_space=plt...  2.95 us
    pallas_call x1, Pallas kernels, prepare(): pl.pallas_call(prepare_kernel, in_specs=[pl.BlockSpec(memory_space=pltpu....  2.8 us
  transfers between devices with their start and end apart: 14, of which 1 were waited for; matrix products, arithmetic and copies ran while one was open for 0% of the time, Pallas kernels for 33%

profile of v4, /device:TPU:1, one launch (start us, length us, event | category | flops | bytes accessed | tf_op | source)
XLA Modules:
  0.0 61.3 jit_solution(8973265514966206902)
XLA Ops:
  0.0 0.1 pad_add_fusion.place
  0.1 0.0 copy-start.2
  0.1 0.9 %copy-done.2 = f32[24,2048]{1,0:T(8,128)S(1)} copy-done((f32[24,2048]{1,0:T(8,128)S(1)}, f32[24,2048]{1,0:T(8,128)}, u32[]{:S(2)}) %copy-start.2) | copy-done | bytes 196632
  1.0 0.0 copy-start.1
  1.0 3.7 %decay_factors.1 = (bf16[2048,768]{1,0:T(8,128)(2,1)S(1)}, bf16[2048,768]{1,0:T(8,128)(2,1)S(1)}, bf16[2064,72]{1,0:T(8,128)(2,1)S(1)}) custom-call(s32[4]{0:T(128)S(1)} %pad_add_fusion.place, bf16[2048,1536]{1,0:T(8,128)(2,1)} %x_hbm.1, f32[24,2048]{1,0:T(8,128)S(1)} %copy-done.2), custom_call_target="tpu_custom_call" | custom-call | tf_op jit(solution)/shard_map/decay_factors/pallas_call | solution.py:101
  4.7 0.0 copy-done.1
  4.7 2.0 %end_state.3 = f32[136,768]{1,0:T(8,128)S(1)} custom-call(s32[4]{0:T(128)S(1)} %pad_add_fusion.place, bf16[2048,768]{1,0:T(8,128)(2,1)S(1)} %get-tuple-element.67.x.x_ref, bf16[2048,128]{1,0:T(8,128)(2,1)S(1)} %copy-done.1, bf16[2064,72]{1,0:T(8,128)(2,1)S(1)} %get-tuple-element.66.factors), custom_call_target="tpu_custom_call" | custom-call | tf_op jit(solution)/shard_map/end_state/pallas_call | solution.py:132
  6.7 0.0 copy-start
  6.7 0.0 copy-start.3
  6.8 1.5 %collective-permute-start = (f32[136,768]{1,0:T(8,128)S(1)}, f32[136,768]{1,0:T(8,128)S(1)}, u32[]{:S(2)}, u32[]{:S(2)}) collective-permute-start(f32[136,768]{1,0:T(8,128)S(1)} %end_state.3), channel_id=1, source_target_pairs={{0,1},{1,0},{2,3},{3,2},{4,5},{5,4},{6,7},{7,6},{8,9},{9,8},{10,11... | collective-permute-start | bytes 1253384 | tf_op jit(solution)/shard_map/ppermute | solution.py:428
  8.3 2.0 %end_state.2.keep = f32[136,768]{1,0:T(8,128)S(1)} custom-call(s32[4]{0:T(128)S(1)} %pad_add_fusion.place, bf16[2048,768]{1,0:T(8,128)(2,1)S(1)} %get-tuple-element.65.x.x_ref, bf16[2048,128]{1,0:T(8,128)(2,1)S(1)} %copy-done.1, bf16[2064,72]{1,0:T(8,128)(2,1)S(1)} %get-tuple-element.66.factors), custom_call_target="tpu_custom_call" | custom-call | tf_op jit(solution)/shard_map/end_state/pallas_call | solution.py:132
  10.3 0.0 collective-permute-done.recv
  10.3 0.6 pair.1
  10.9 1.4 %collective-permute-start.1 = (f32[40,768]{1,0:T(8,128)S(1)}, f32[40,768]{1,0:T(8,128)S(1)}, u32[]{:S(2)}, u32[]{:S(2)}) collective-permute-start(f32[40,768]{1,0:T(8,128)S(1)} %get-tuple-element.71), channel_id=1, source_target_pairs={{0,2},{1,3},{2,4},{3,5},{4,6},{5,7},{6,0},{7,1},{8,10},{9,11},{10,... | collective-permute-start | bytes 368648 | tf_op jit(solution)/shard_map/ppermute | solution.py:428
  12.3 2.4 %collective-permute-start.2 = (f32[40,768]{1,0:T(8,128)S(1)}, f32[40,768]{1,0:T(8,128)S(1)}, u32[]{:S(2)}, u32[]{:S(2)}) collective-permute-start(f32[40,768]{1,0:T(8,128)S(1)} %get-tuple-element.72), channel_id=1, source_target_pairs={{0,4},{1,5},{2,6},{3,7},{4,0},{5,1},{6,2},{7,3},{8,12},{9,13},{10,... | collective-permute-start | bytes 368648 | tf_op jit(solution)/shard_map/ppermute | solution.py:428
  14.7 0.0 copy-start.4
  14.7 1.2 %collective-permute-start.3 = (f32[40,768]{1,0:T(8,128)S(1)}, f32[40,768]{1,0:T(8,128)S(1)}, u32[]{:S(2)}, u32[]{:S(2)}) collective-permute-start(f32[40,768]{1,0:T(8,128)S(1)} %get-tuple-element.73), channel_id=1, source_target_pairs={{0,6},{1,7},{2,0},{3,1},{4,2},{5,3},{6,4},{7,5},{8,14},{9,15},{10,... | collective-permute-start | bytes 368648 | tf_op jit(solution)/shard_map/ppermute | solution.py:428
  15.9 0.0 copy-done
  15.9 0.0 copy-done.3
  15.9 2.8 %prepare.1 = (bf16[2048,1536]{1,0:T(8,128)(2,1)S(1)}, bf16[2048,256]{1,0:T(8,128)(2,1)S(1)}, bf16[2048,128]{1,0:T(8,128)(2,1)S(1)}, bf16[2304,72]{1,0:T(8,128)(2,1)S(1)}, bf16[2048,72]{1,0:T(8,128)(2,1)S(1)}) custom-call(bf16[2048,1536]{1,0:T(8,128)(2,1)} %gate_hbm.1, bf16[2048,128]{1,0:T(8,128)(2,1)S(1)} %copy-done.1, bf16[2048,128]{1,0:T(8,128)(2,1)S(1)} %copy-done, ...), custom_call_target="tpu_custom_call" | custom-call | tf_op jit(solution)/shard_map/prepare/pallas_call | solution.py:273
  18.7 0.0 copy-done.4
  18.7 2.1 %local.6 = (f32[2048,256]{1,0:T(8,128)S(1)}, bf16[2048,256]{1,0:T(8,128)(2,1)S(1)}) custom-call(s32[4]{0:T(128)S(1)} %pad_add_fusion.place, f32[24]{0:T(128)S(1)} %copy-done.4, bf16[2048,768]{1,0:T(8,128)(2,1)S(1)} %get-tuple-element.65.x.x_ref, bf16[2048,1536]{1,0:T(8,128)(2,1)S(1)} %get-tuple-element.74.gate_ref, ...), custom_call_target="tpu_custom_call" | custom-call | tf_op jit(solution)/shard_map/local/pallas_call | solution.py:330
  20.8 0.0 collective-permute-done.1.u1
  20.9 0.0 collective-permute-done.2.u2
  20.9 0.0 collective-permute-done.3.u3
  20.9 0.6 %line.1.v0 = f32[40,768]{1,0:T(8,128)S(1)} custom-call(s32[4]{0:T(128)S(1)} %pad_add_fusion.place, f32[40,768]{1,0:T(8,128)S(1)} %get-tuple-element.70.u0, f32[40,768]{1,0:T(8,128)S(1)} %collective-permute-done.1.u1, f32[40,768]{1,0:T(8,128)S(1)} %collective-permute-done.2.u2, f32[40,768]{1,0:T(8,128)S(1)} %collective-permute-done.3.u3), custom_call_target="tpu_custom_call" | custom-call | tf_op jit(solution)/shard_map/line/pallas_call | solution.py:145
  21.5 1.4 %collective-permute-start.4 = (f32[40,768]{1,0:T(8,128)S(1)}, f32[40,768]{1,0:T(8,128)S(1)}, u32[]{:S(2)}, u32[]{:S(2)}) collective-permute-start(f32[40,768]{1,0:T(8,128)S(1)} %line.1.v0), channel_id=1, source_target_pairs={{0,8},{1,9},{2,10},{3,11},{4,12},{5,13},{6,14},{7,15},{8,16},{9,17... | collective-permute-start | bytes 368648 | tf_op jit(solution)/shard_map/ppermute | solution.py:428
  22.9 2.6 %collective-permute-start.5 = (f32[40,768]{1,0:T(8,128)S(1)}, f32[40,768]{1,0:T(8,128)S(1)}, u32[]{:S(2)}, u32[]{:S(2)}) collective-permute-start(f32[40,768]{1,0:T(8,128)S(1)} %line.1.v0), channel_id=1, source_target_pairs={{0,16},{1,17},{2,18},{3,19},{4,20},{5,21},{6,22},{7,23},{8,24},{9,... | collective-permute-start | bytes 368648 | tf_op jit(solution)/shard_map/ppermute | solution.py:428
  25.5 1.1 %collective-permute-start.6 = (f32[40,768]{1,0:T(8,128)S(1)}, f32[40,768]{1,0:T(8,128)S(1)}, u32[]{:S(2)}, u32[]{:S(2)}) collective-permute-start(f32[40,768]{1,0:T(8,128)S(1)} %line.1.v0), channel_id=1, source_target_pairs={{0,24},{1,25},{2,26},{3,27},{4,28},{5,29},{6,30},{7,31},{8,0},{9,1... | collective-permute-start | bytes 368648 | tf_op jit(solution)/shard_map/ppermute | solution.py:428
  26.6 2.1 %local.7 = (f32[2048,256]{1,0:T(8,128)S(1)}, bf16[2048,256]{1,0:T(8,128)(2,1)S(1)}) custom-call(s32[4]{0:T(128)S(1)} %pad_add_fusion.place, f32[24]{0:T(128)S(1)} %copy-done.4, bf16[2048,768]{1,0:T(8,128)(2,1)S(1)} %get-tuple-element.65.x.x_ref, bf16[2048,1536]{1,0:T(8,128)(2,1)S(1)} %get-tuple-element.74.gate_ref, ...), custom_call_target="tpu_custom_call" | custom-call | tf_op jit(solution)/shard_map/local/pallas_call | solution.py:330
  28.7 2.1 %local.8 = (f32[2048,256]{1,0:T(8,128)S(1)}, bf16[2048,256]{1,0:T(8,128)(2,1)S(1)}) custom-call(s32[4]{0:T(128)S(1)} %pad_add_fusion.place, f32[24]{0:T(128)S(1)} %copy-done.4, bf16[2048,768]{1,0:T(8,128)(2,1)S(1)} %get-tuple-element.65.x.x_ref, bf16[2048,1536]{1,0:T(8,128)(2,1)S(1)} %get-tuple-element.74.gate_ref, ...), custom_call_target="tpu_custom_call" | custom-call | tf_op jit(solution)/shard_map/local/pallas_call | solution.py:330
  30.8 0.0 collective-permute-done.4.v1
  30.8 0.0 collective-permute-done.5.v2
  30.8 0.0 collective-permute-done.6.v3
  30.8 0.7 %plane.1 = (f32[40,768]{1,0:T(8,128)S(1)}, f32[40,768]{1,0:T(8,128)S(1)}) custom-call(s32[4]{0:T(128)S(1)} %pad_add_fusion.place, f32[40,768]{1,0:T(8,128)S(1)} %line.1.v0, f32[40,768]{1,0:T(8,128)S(1)} %collective-permute-done.4.v1, f32[40,768]{1,0:T(8,128)S(1)} %collective-permute-done.5.v2, f32[40,768]{1,0:T(8,128)S(1)} %collective-permute-done.6.v3), custom_call_target="tpu_custom_call" | custom-call | tf_op jit(solution)/shard_map/plane/pallas_call | solution.py:145
  31.6 1.7 %collective-permute-start.7 = (f32[40,768]{1,0:T(8,128)S(1)}, f32[40,768]{1,0:T(8,128)S(1)}, u32[]{:S(2)}, u32[]{:S(2)}) collective-permute-start(f32[40,768]{1,0:T(8,128)S(1)} %get-tuple-element.91.w0), channel_id=1, source_target_pairs={{0,32},{1,33},{2,34},{3,35},{4,36},{5,37},{6,38},{7,39},{8,40},{9,... | collective-permute-start | bytes 368648 | tf_op jit(solution)/shard_map/ppermute | solution.py:428
  33.3 3.3 %collective-permute-start.8 = (f32[40,768]{1,0:T(8,128)S(1)}, f32[40,768]{1,0:T(8,128)S(1)}, u32[]{:S(2)}, u32[]{:S(2)}) collective-permute-start(f32[40,768]{1,0:T(8,128)S(1)} %get-tuple-element.91.w0), channel_id=1, source_target_pairs={{0,64},{1,65},{2,66},{3,67},{4,68},{5,69},{6,70},{7,71},{8,72},{9,... | collective-permute-start | bytes 368648 | tf_op jit(solution)/shard_map/ppermute | solution.py:428
  36.6 0.7 %collective-permute-start.9 = (f32[40,768]{1,0:T(8,128)S(1)}, f32[40,768]{1,0:T(8,128)S(1)}, u32[]{:S(2)}, u32[]{:S(2)}) collective-permute-start(f32[40,768]{1,0:T(8,128)S(1)} %get-tuple-element.91.w0), channel_id=1, source_target_pairs={{0,96},{1,97},{2,98},{3,99},{4,100},{5,101},{6,102},{7,103},{8,104... | collective-permute-start | bytes 368648 | tf_op jit(solution)/shard_map/ppermute | solution.py:428
  37.3 2.1 %local.9 = (f32[2048,256]{1,0:T(8,128)S(1)}, bf16[2048,256]{1,0:T(8,128)(2,1)S(1)}) custom-call(s32[4]{0:T(128)S(1)} %pad_add_fusion.place, f32[24]{0:T(128)S(1)} %copy-done.4, bf16[2048,768]{1,0:T(8,128)(2,1)S(1)} %get-tuple-element.67.x.x_ref, bf16[2048,1536]{1,0:T(8,128)(2,1)S(1)} %get-tuple-element.74.gate_ref, ...), custom_call_target="tpu_custom_call" | custom-call | tf_op jit(solution)/shard_map/local/pallas_call | solution.py:330
  39.4 2.1 %local.10 = (f32[2048,256]{1,0:T(8,128)S(1)}, bf16[2048,256]{1,0:T(8,128)(2,1)S(1)}) custom-call(s32[4]{0:T(128)S(1)} %pad_add_fusion.place, f32[24]{0:T(128)S(1)} %copy-done.4, bf16[2048,768]{1,0:T(8,128)(2,1)S(1)} %get-tuple-element.67.x.x_ref, bf16[2048,1536]{1,0:T(8,128)(2,1)S(1)} %get-tuple-element.74.gate_ref, ...), custom_call_target="tpu_custom_call" | custom-call | tf_op jit(solution)/shard_map/local/pallas_call | solution.py:330
  41.5 0.0 collective-permute-done.7.w1
  41.5 0.0 collective-permute-done.8.w2
  41.5 0.0 collective-permute-done.9.w3
  41.5 1.0 %enter.1 = (f32[32,768]{1,0:T(8,128)S(1)}, f32[32,768]{1,0:T(8,128)S(1)}, f32[32,768]{1,0:T(8,128)S(1)}, f32[32,768]{1,0:T(8,128)S(1)}) custom-call(s32[4]{0:T(128)S(1)} %pad_add_fusion.place, f32[40,768]{1,0:T(8,128)S(1)} %get-tuple-element.91.w0, f32[40,768]{1,0:T(8,128)S(1)} %collective-permute-done.7.w1, f32[40,768]{1,0:T(8,128)S(1)} %collective-permute-done.8.w2, ...), custom_call_target="tpu_custom_call" | custom-call | tf_op jit(solution)/shard_map/enter/pallas_call | solution.py:145
  42.5 0.7 %collective-permute-start.10 = (f32[32,768]{1,0:T(8,128)S(1)}, f32[32,768]{1,0:T(8,128)S(1)}, u32[]{:S(2)}, u32[]{:S(2)}) collective-permute-start(f32[32,768]{1,0:T(8,128)S(1)} %get-tuple-element.101), channel_id=1, source_target_pairs={{0,2},{1,3},{2,4},{3,5},{4,6},{5,7},{6,0},{7,1},{8,10},{9,11},{10,... | collective-permute-start | bytes 294920 | tf_op jit(solution)/shard_map/ppermute | solution.py:428
  43.2 2.4 %collective-permute-start.11 = (f32[32,768]{1,0:T(8,128)S(1)}, f32[32,768]{1,0:T(8,128)S(1)}, u32[]{:S(2)}, u32[]{:S(2)}) collective-permute-start(f32[32,768]{1,0:T(8,128)S(1)} %get-tuple-element.102), channel_id=1, source_target_pairs={{0,4},{1,5},{2,6},{3,7},{4,0},{5,1},{6,2},{7,3},{8,12},{9,13},{10,... | collective-permute-start | bytes 294920 | tf_op jit(solution)/shard_map/ppermute | solution.py:428
  45.6 0.0 copy-start.5
  45.6 1.1 %collective-permute-start.12 = (f32[32,768]{1,0:T(8,128)S(1)}, f32[32,768]{1,0:T(8,128)S(1)}, u32[]{:S(2)}, u32[]{:S(2)}) collective-permute-start(f32[32,768]{1,0:T(8,128)S(1)} %get-tuple-element.103), channel_id=1, source_target_pairs={{0,6},{1,7},{2,0},{3,1},{4,2},{5,3},{6,4},{7,5},{8,14},{9,15},{10,... | collective-permute-start | bytes 294920 | tf_op jit(solution)/shard_map/ppermute | solution.py:428
  46.7 2.1 %local.11 = (f32[2048,256]{1,0:T(8,128)S(1)}, bf16[2048,256]{1,0:T(8,128)(2,1)S(1)}) custom-call(s32[4]{0:T(128)S(1)} %pad_add_fusion.place, f32[24]{0:T(128)S(1)} %copy-done.4, bf16[2048,768]{1,0:T(8,128)(2,1)S(1)} %get-tuple-element.67.x.x_ref, bf16[2048,1536]{1,0:T(8,128)(2,1)S(1)} %get-tuple-element.74.gate_ref, ...), custom_call_target="tpu_custom_call" | custom-call | tf_op jit(solution)/shard_map/local/pallas_call | solution.py:330
  48.8 0.0 collective-permute-done.10.e1
  48.8 0.0 collective-permute-done.11.e2
  48.8 0.3 collective-permute-done.12.e3
  49.1 0.7 %chip.1 = (f32[128,768]{1,0:T(8,128)S(1)}, f32[128,768]{1,0:T(8,128)S(1)}) custom-call(s32[4]{0:T(128)S(1)} %pad_add_fusion.place, f32[32,768]{1,0:T(8,128)S(1)} %get-tuple-element.100.e0, f32[32,768]{1,0:T(8,128)S(1)} %collective-permute-done.10.e1, f32[32,768]{1,0:T(8,128)S(1)} %collective-permute-done.11.e2, f32[32,768]{1,0:T(8,128)S(1)} %collective-permute-done.12.e3, ...), custom_call_target="tpu_custom_call" | custom-call | tf_op jit(solution)/shard_map/chip/pallas_call | solution.py:145
  49.8 4.6 %collective-permute-start.13 = (f32[128,768]{1,0:T(8,128)S(1)}, f32[128,768]{1,0:T(8,128)S(1)}, u32[]{:S(2)}, u32[]{:S(2)}) collective-permute-start(f32[128,768]{1,0:T(8,128)S(1)} %get-tuple-element.116), channel_id=1, source_target_pairs={{0,1},{1,0},{2,3},{3,2},{4,5},{5,4},{6,7},{7,6},{8,9},{9,8},{10,11... | collective-permute-start | bytes 1179656 | tf_op jit(solution)/shard_map/ppermute | solution.py:428
  54.4 0.0 copy-done.5
  54.4 3.0 %own_output.1.own = bf16[2048,768]{1,0:T(8,128)(2,1)S(1)} custom-call(s32[4]{0:T(128)S(1)} %pad_add_fusion.place, bf16[2048,128]{1,0:T(8,128)(2,1)S(1)} %copy-done, f32[1,1536]{1,0:T(1,128)S(1)} %broadcast_in_dim.3.gain_ref, f32[128,768]{1,0:T(8,128)S(1)} %get-tuple-element.109.state_ref, f32[2048,256]{1,0:T(8,128)S(1)} %get-tuple-element.110.refs_0_, ...), custom_call_target="tpu_custom_call" | custom-call | tf_op jit(solution)/shard_map/own_output/pallas_call | solution.py:366
  57.3 0.0 collective-permute-done.13.state_ref
  57.3 3.8 %output.1 = bf16[2048,1536]{1,0:T(8,128)(2,1)} custom-call(s32[4]{0:T(128)S(1)} %pad_add_fusion.place, bf16[2048,128]{1,0:T(8,128)(2,1)S(1)} %copy-done, f32[1,1536]{1,0:T(1,128)S(1)} %broadcast_in_dim.3.gain_ref, f32[128,768]{1,0:T(8,128)S(1)} %collective-permute-done.13.state_ref, bf16[2048,768]{1,0:T(8,128)(2,1)S(1)} %own_output.1.own, ...), custom_call_target="tpu_custom_call" | custom-call | tf_op jit(solution)/shard_map/output/pallas_call | solution.py:399
  (1 shorter events, 0.0 us)
Async XLA Ops:
  0.1 0.9 %copy-start.2 = (f32[24,2048]{1,0:T(8,128)S(1)}, f32[24,2048]{1,0:T(8,128)}, u32[]{:S(2)}) copy-start(f32[24,2048]{1,0:T(8,128)} %decay_ref.1) | copy-start | bytes 589828
  1.0 3.7 %copy-start.1 = (bf16[2048,128]{1,0:T(8,128)(2,1)S(1)}, bf16[2048,128]{1,0:T(8,128)(2,1)}, u32[]{:S(2)}) copy-start(bf16[2048,128]{1,0:T(8,128)(2,1)} %b_ref.1) | copy-start | bytes 1572868
  6.7 9.2 %copy-start = (bf16[2048,128]{1,0:T(8,128)(2,1)S(1)}, bf16[2048,128]{1,0:T(8,128)(2,1)}, u32[]{:S(2)}) copy-start(bf16[2048,128]{1,0:T(8,128)(2,1)} %c_ref.5) | copy-start | bytes 1572868
  6.7 9.2 %copy-start.3 = (f32[24,2048]{1,0:T(8,128)S(1)}, f32[24,2048]{1,0:T(8,128)}, u32[]{:S(2)}) copy-start(f32[24,2048]{1,0:T(8,128)} %decay_ref.1) | copy-start | bytes 589828
  6.8 3.5 %collective-permute-start = (f32[136,768]{1,0:T(8,128)S(1)}, f32[136,768]{1,0:T(8,128)S(1)}, u32[]{:S(2)}, u32[]{:S(2)}) collective-permute-start(f32[136,768]{1,0:T(8,128)S(1)} %end_state.3), channel_id=1, source_target_pairs={{0,1},{1,0},{2,3},{3,2},{4,5},{5,4},{6,7},{7,6},{8,9},{9,8},{10,11... | collective-permute-start | bytes 1253384 | tf_op jit(solution)/shard_map/ppermute | solution.py:428
  10.9 9.9 %collective-permute-start.1 = (f32[40,768]{1,0:T(8,128)S(1)}, f32[40,768]{1,0:T(8,128)S(1)}, u32[]{:S(2)}, u32[]{:S(2)}) collective-permute-start(f32[40,768]{1,0:T(8,128)S(1)} %get-tuple-element.71), channel_id=1, source_target_pairs={{0,2},{1,3},{2,4},{3,5},{4,6},{5,7},{6,0},{7,1},{8,10},{9,11},{10,... | collective-permute-start | bytes 368648 | tf_op jit(solution)/shard_map/ppermute | solution.py:428
  12.3 8.6 %collective-permute-start.2 = (f32[40,768]{1,0:T(8,128)S(1)}, f32[40,768]{1,0:T(8,128)S(1)}, u32[]{:S(2)}, u32[]{:S(2)}) collective-permute-start(f32[40,768]{1,0:T(8,128)S(1)} %get-tuple-element.72), channel_id=1, source_target_pairs={{0,4},{1,5},{2,6},{3,7},{4,0},{5,1},{6,2},{7,3},{8,12},{9,13},{10,... | collective-permute-start | bytes 368648 | tf_op jit(solution)/shard_map/ppermute | solution.py:428
  14.7 4.0 %copy-start.4 = (f32[24]{0:T(128)S(1)}, f32[24]{0:T(128)}, u32[]{:S(2)}) copy-start(f32[24]{0:T(128)} %skip_ref.11) | copy-start | bytes 292
  14.7 6.1 %collective-permute-start.3 = (f32[40,768]{1,0:T(8,128)S(1)}, f32[40,768]{1,0:T(8,128)S(1)}, u32[]{:S(2)}, u32[]{:S(2)}) collective-permute-start(f32[40,768]{1,0:T(8,128)S(1)} %get-tuple-element.73), channel_id=1, source_target_pairs={{0,6},{1,7},{2,0},{3,1},{4,2},{5,3},{6,4},{7,5},{8,14},{9,15},{10,... | collective-permute-start | bytes 368648 | tf_op jit(solution)/shard_map/ppermute | solution.py:428
  21.5 9.3 %collective-permute-start.4 = (f32[40,768]{1,0:T(8,128)S(1)}, f32[40,768]{1,0:T(8,128)S(1)}, u32[]{:S(2)}, u32[]{:S(2)}) collective-permute-start(f32[40,768]{1,0:T(8,128)S(1)} %line.1.v0), channel_id=1, source_target_pairs={{0,8},{1,9},{2,10},{3,11},{4,12},{5,13},{6,14},{7,15},{8,16},{9,17... | collective-permute-start | bytes 368648 | tf_op jit(solution)/shard_map/ppermute | solution.py:428
  22.9 7.9 %collective-permute-start.5 = (f32[40,768]{1,0:T(8,128)S(1)}, f32[40,768]{1,0:T(8,128)S(1)}, u32[]{:S(2)}, u32[]{:S(2)}) collective-permute-start(f32[40,768]{1,0:T(8,128)S(1)} %line.1.v0), channel_id=1, source_target_pairs={{0,16},{1,17},{2,18},{3,19},{4,20},{5,21},{6,22},{7,23},{8,24},{9,... | collective-permute-start | bytes 368648 | tf_op jit(solution)/shard_map/ppermute | solution.py:428
  25.5 5.3 %collective-permute-start.6 = (f32[40,768]{1,0:T(8,128)S(1)}, f32[40,768]{1,0:T(8,128)S(1)}, u32[]{:S(2)}, u32[]{:S(2)}) collective-permute-start(f32[40,768]{1,0:T(8,128)S(1)} %line.1.v0), channel_id=1, source_target_pairs={{0,24},{1,25},{2,26},{3,27},{4,28},{5,29},{6,30},{7,31},{8,0},{9,1... | collective-permute-start | bytes 368648 | tf_op jit(solution)/shard_map/ppermute | solution.py:428
  31.6 10.0 %collective-permute-start.7 = (f32[40,768]{1,0:T(8,128)S(1)}, f32[40,768]{1,0:T(8,128)S(1)}, u32[]{:S(2)}, u32[]{:S(2)}) collective-permute-start(f32[40,768]{1,0:T(8,128)S(1)} %get-tuple-element.91.w0), channel_id=1, source_target_pairs={{0,32},{1,33},{2,34},{3,35},{4,36},{5,37},{6,38},{7,39},{8,40},{9,... | collective-permute-start | bytes 368648 | tf_op jit(solution)/shard_map/ppermute | solution.py:428
  33.3 8.3 %collective-permute-start.8 = (f32[40,768]{1,0:T(8,128)S(1)}, f32[40,768]{1,0:T(8,128)S(1)}, u32[]{:S(2)}, u32[]{:S(2)}) collective-permute-start(f32[40,768]{1,0:T(8,128)S(1)} %get-tuple-element.91.w0), channel_id=1, source_target_pairs={{0,64},{1,65},{2,66},{3,67},{4,68},{5,69},{6,70},{7,71},{8,72},{9,... | collective-permute-start | bytes 368648 | tf_op jit(solution)/shard_map/ppermute | solution.py:428
  36.6 5.0 %collective-permute-start.9 = (f32[40,768]{1,0:T(8,128)S(1)}, f32[40,768]{1,0:T(8,128)S(1)}, u32[]{:S(2)}, u32[]{:S(2)}) collective-permute-start(f32[40,768]{1,0:T(8,128)S(1)} %get-tuple-element.91.w0), channel_id=1, source_target_pairs={{0,96},{1,97},{2,98},{3,99},{4,100},{5,101},{6,102},{7,103},{8,104... | collective-permute-start | bytes 368648 | tf_op jit(solution)/shard_map/ppermute | solution.py:428
  42.5 6.3 %collective-permute-start.10 = (f32[32,768]{1,0:T(8,128)S(1)}, f32[32,768]{1,0:T(8,128)S(1)}, u32[]{:S(2)}, u32[]{:S(2)}) collective-permute-start(f32[32,768]{1,0:T(8,128)S(1)} %get-tuple-element.101), channel_id=1, source_target_pairs={{0,2},{1,3},{2,4},{3,5},{4,6},{5,7},{6,0},{7,1},{8,10},{9,11},{10,... | collective-permute-start | bytes 294920 | tf_op jit(solution)/shard_map/ppermute | solution.py:428
  43.2 5.6 %collective-permute-start.11 = (f32[32,768]{1,0:T(8,128)S(1)}, f32[32,768]{1,0:T(8,128)S(1)}, u32[]{:S(2)}, u32[]{:S(2)}) collective-permute-start(f32[32,768]{1,0:T(8,128)S(1)} %get-tuple-element.102), channel_id=1, source_target_pairs={{0,4},{1,5},{2,6},{3,7},{4,0},{5,1},{6,2},{7,3},{8,12},{9,13},{10,... | collective-permute-start | bytes 294920 | tf_op jit(solution)/shard_map/ppermute | solution.py:428
  45.6 8.8 %copy-start.5 = (f32[1536]{0:T(1024)S(1)}, f32[1536]{0:T(1024)}, u32[]{:S(2)}) copy-start(f32[1536]{0:T(1024)} %param.13) | copy-start | bytes 18436
  45.6 3.5 %collective-permute-start.12 = (f32[32,768]{1,0:T(8,128)S(1)}, f32[32,768]{1,0:T(8,128)S(1)}, u32[]{:S(2)}, u32[]{:S(2)}) collective-permute-start(f32[32,768]{1,0:T(8,128)S(1)} %get-tuple-element.103), channel_id=1, source_target_pairs={{0,6},{1,7},{2,0},{3,1},{4,2},{5,3},{6,4},{7,5},{8,14},{9,15},{10,... | collective-permute-start | bytes 294920 | tf_op jit(solution)/shard_map/ppermute | solution.py:428
  49.8 7.6 %collective-permute-start.13 = (f32[128,768]{1,0:T(8,128)S(1)}, f32[128,768]{1,0:T(8,128)S(1)}, u32[]{:S(2)}, u32[]{:S(2)}) collective-permute-start(f32[128,768]{1,0:T(8,128)S(1)} %get-tuple-element.116), channel_id=1, source_target_pairs={{0,1},{1,0},{2,3},{3,2},{4,5},{5,4},{6,7},{7,6},{8,9},{9,8},{10,11... | collective-permute-start | bytes 1179656 | tf_op jit(solution)/shard_map/ppermute | solution.py:428

commit v5 on v4

--- a/solution.py
+++ b/solution.py
@@ -21,6 +21,7 @@
 OUT_STEP = 256
 FETCH = 512
 QUARTER = STATE // 4
+TILES = QUARTER // 8 * (HALF // 128)
 FETCH_LIMIT = 42 * 1024 * 1024
 PREPARE_LIMIT = 40 * 1024 * 1024
 LIMIT = 18 * 1024 * 1024
@@ -155,6 +156,23 @@
 Z, Y, X, CORE = 0, 1, 2, 3
 
 
+def parts_of(piece):
+    state = piece[:TILES].reshape(QUARTER // 8, HALF // 128, 8, 128)
+    decay = [jnp.broadcast_to(piece[TILES, j : j + 1], (8, 128)) for j in range(HALF // 128)]
+    return state, jnp.stack(decay)
+
+
+def set_piece(out, state, decay):
+    out[:TILES] = state.reshape(TILES, 8, 128)
+    out[TILES] = jnp.zeros((8, 128), F32)
+    for j in range(HALF // 128):
+        out[TILES, j : j + 1] = decay[j, :1]
+
+
+def nothing():
+    return jnp.zeros((QUARTER // 8, HALF // 128, 8, 128), F32), jnp.ones((HALF // 128, 8, 128), F32)
+
+
 def pair_kernel(place, keep, recv, own, *sends):
     flip = place[CORE] == 1
     kept, got = keep[STATE : STATE + 8], recv[STATE : STATE + 8]
@@ -164,8 +182,13 @@
         chunk = (place[X] + shift) % 4
         rows = pl.ds(pl.multiple_of(chunk * QUARTER, QUARTER), QUARTER)
         a, b = keep[rows], recv[rows]
-        out[:QUARTER] = late * jnp.where(flip, b, a) + jnp.where(flip, a, b)
-        out[QUARTER:] = decay
+        total = late * jnp.where(flip, b, a) + jnp.where(flip, a, b)
+        out[TILES] = jnp.zeros((8, 128), F32)
+        for j in range(HALF // 128):
+            lanes = slice(128 * j, 128 * (j + 1))
+            out[TILES, j : j + 1] = decay[:1, lanes]
+            for i in range(QUARTER // 8):
+                out[i * (HALF // 128) + j] = total[8 * i : 8 * (i + 1), lanes]
 
 
 def ordered(place, axis, refs, j):
@@ -173,54 +196,51 @@
     value = refs[0][...]
     for s in (1, 2, 3):
         value = jnp.where(shift == s, refs[s][...], value)
-    return value
+    return parts_of(value)
 
 
 def line_kernel(place, u0, u1, u2, u3, total):
-    state = jnp.zeros((QUARTER, HALF), F32)
-    decay = jnp.ones((8, HALF), F32)
+    state, decay = nothing()
     for j in range(4):
-        u = ordered(place, X, (u0, u1, u2, u3), j)
-        state = u[QUARTER : QUARTER + 1] * state + u[:QUARTER]
-        decay = decay * u[QUARTER:]
-    total[:QUARTER] = state
-    total[QUARTER:] = decay
+        u, u_decay = ordered(place, X, (u0, u1, u2, u3), j)
+        state = u_decay * state + u
+        decay = decay * u_decay
+    set_piece(total, state, decay)
 
 
 def plane_kernel(place, v0, v1, v2, v3, total, before):
-    state = jnp.zeros((QUARTER, HALF), F32)
-    decay = jnp.ones((8, HALF), F32)
+    state, decay = nothing()
     for j in range(4):
 
         @pl.when(place[Y] == j)
         def _(state=state, decay=decay):
-            before[:QUARTER] = state
-            before[QUARTER:] = decay
-
-        v = ordered(place, Y, (v0, v1, v2, v3), j)
-        state = v[QUARTER : QUARTER + 1] * state + v[:QUARTER]
-        decay = decay * v[QUARTER:]
-    total[:QUARTER] = state
-    total[QUARTER:] = decay
+            set_piece(before, state, decay)
+
+        v, v_decay = ordered(place, Y, (v0, v1, v2, v3), j)
+        state = v_decay * state + v
+        decay = decay * v_decay
+    set_piece(total, state, decay)
 
 
 def enter_kernel(place, w0, w1, w2, w3, before, u0, u1, u2, u3, own, *sends):
-    state = jnp.zeros((QUARTER, HALF), F32)
+    state, _ = nothing()
     for j in range(3):
-        w = ordered(place, Z, (w0, w1, w2, w3), j)
-        updated = w[QUARTER : QUARTER + 1] * state + w[:QUARTER]
-        state = jnp.where(j < place[Z], updated, state)
-    state = before[QUARTER : QUARTER + 1] * state + before[:QUARTER]
+        w, w_decay = ordered(place, Z, (w0, w1, w2, w3), j)
+        state = jnp.where(j < place[Z], w_decay * state + w, state)
+    earlier, decay = parts_of(before[...])
+    state = decay * state + earlier
     for j in range(4):
         for shift, out in enumerate((own,) + sends):
 
             @pl.when((place[X] + shift) % 4 == j)
             def _(state=state, out=out):
-                out[...] = state
+                for a in range(QUARTER // 8):
+                    for b in range(HALF // 128):
+                        out[8 * a : 8 * (a + 1), 128 * b : 128 * (b + 1)] = state[a, b]
 
         if j < 3:
-            u = ordered(place, X, (u0, u1, u2, u3), j)
-            state = u[QUARTER : QUARTER + 1] * state + u[:QUARTER]
+            u, u_decay = ordered(place, X, (u0, u1, u2, u3), j)
+            state = u_decay * state + u
 
 
 def chip_kernel(place, e0, e1, e2, e3, keep, recv, own, send):
@@ -431,7 +451,7 @@
 def on_device(x, gate, b, c, decay, d_skip, norm_gain):
     z, r = lax.axis_index("grp"), lax.axis_index("dev")
     place = jnp.stack([z, r // 8, (r // 2) % 4, r % 2]).astype(jnp.int32)
-    piece, chunk = (QUARTER + 8, HALF), (QUARTER, HALF)
+    piece, chunk = (TILES + 1, 8, 128), (QUARTER, HALF)
 
     x_send, x_keep, factors = decay_factors(place, x, decay)
     send = end_state(False, place, x_send, b, factors)
@@ -439,24 +459,26 @@
     keep = end_state(True, place, x_keep, b, factors)
     keep, recv = lax.optimization_barrier((keep, recv))
     parts = []
-
-    def work(count, *arrived):
+    far_last = (0, 2, 1)
+
+    def work(count, order, *arrived):
         for _ in range(count):
             part = len(parts)
             half = x_keep if part < HALF // GROUP else x_send
             parts.append(local(part, place, d_skip, half, *shared))
-        arrived, parts[-count:] = lax.optimization_barrier((arrived, parts[-count:]))
-        return arrived
+        begun = [arrived[i] for i in order]
+        begun, parts[-count:] = lax.optimization_barrier((begun, parts[-count:]))
+        return [begun[order.index(i)] for i in range(3)]
 
     u0, *sends = small_call(pair_kernel, "pair", place, (keep, recv), [piece] * 4)
     shared = prepare(gate, b, c, decay)
-    lines = [u0] + list(work(1, *[moved(v, X, s + 1) for s, v in enumerate(sends)]))
+    lines = [u0] + list(work(1, far_last, *[moved(v, X, s + 1) for s, v in enumerate(sends)]))
     (v0,) = small_call(line_kernel, "line", place, lines, [piece])
-    columns = [v0] + list(work(2, *[moved(v0, Y, s) for s in (1, 2, 3)]))
+    columns = [v0] + list(work(2, far_last, *[moved(v0, Y, s) for s in (1, 2, 3)]))
     w0, before = small_call(plane_kernel, "plane", place, columns, [piece] * 2)
-    planes = [w0] + list(work(2, *[moved(w0, Z, s) for s in (1, 2, 3)]))
+    planes = [w0] + list(work(2, far_last, *[moved(w0, Z, s) for s in (1, 2, 3)]))
     e0, *sends = small_call(enter_kernel, "enter", place, planes + [before] + lines, [chunk] * 4)
-    entering = [e0] + list(work(1, *[moved(v, X, s + 1) for s, v in enumerate(sends)]))
+    entering = [e0] + list(work(1, (0, 1, 2), *[moved(v, X, s + 1) for s, v in enumerate(sends)]))
     own, send = small_call(chip_kernel, "chip", place, entering + [keep, recv], [(STATE, HALF)] * 2)
     other = moved(send, CORE, 1)
     half = len(parts) // 2

time: 61.5 us -> 59.2 us (0.963)
  starting transfers between devices: 26 us -> 23 us
  waiting for transfers between devices: 0.31 us -> 1.08 us
    ppermute x14, starting transfers between devices: 26 us -> 23 us  [moved(): return lax.ppermute(value, ('grp', 'dev'), pairs)]
    ppermute x14, waiting for transfers between devices: 0.31 us -> 1.08 us  [moved(): return lax.ppermute(value, ('grp', 'dev'), pairs)]
  transfers between devices with their start and end apart: 14 -> 14, of which waited for: 1 -> 3; matrix products, arithmetic and copies ran while one was open for 0% -> 0% of each run, Pallas kernels for 33% -> 35%
where the time goes in v5:
time: 59.2 us; the launch traced here: 59 us
  Pallas kernels  33.4 us (56%)
  starting transfers between devices  23 us (39%)
  waiting for transfers between devices  1.08 us (2%)
  local copies, waits for them, and re-layouts  0.96 us (2%)
    ppermute x14, starting transfers between devices, moved(): return lax.ppermute(value, ('grp', 'dev'), pairs)  23 us
    pallas_call x6, Pallas kernels, local(): pl.pallas_call(functools.partial(local_kernel, part), in_specs=[pl.BlockS...  12.6 us
    pallas_call x2, Pallas kernels, end_state(): pl.pallas_call(functools.partial(state_kernel, mine), in_specs=[pl.BlockS...  4.07 us
    pallas_call x1, Pallas kernels, output(): pl.pallas_call(output_kernel, in_specs=[pl.BlockSpec(memory_space=pltpu.S...  3.8 us
    pallas_call x1, Pallas kernels, decay_factors(): pl.pallas_call(factors_kernel, in_specs=[pl.BlockSpec(memory_space=pltpu....  3.66 us
    pallas_call x5, Pallas kernels, small_call(): pl.pallas_call(kernel, in_specs=[pl.BlockSpec(memory_space=pltpu.SMEM)] +...  3.49 us
    pallas_call x1, Pallas kernels, own_output(): pl.pallas_call(own_output_kernel, in_specs=[pl.BlockSpec(memory_space=plt...  2.95 us
    pallas_call x1, Pallas kernels, prepare(): pl.pallas_call(prepare_kernel, in_specs=[pl.BlockSpec(memory_space=pltpu....  2.8 us
  transfers between devices with their start and end apart: 14, of which 3 were waited for; matrix products, arithmetic and copies ran while one was open for 0% of the time, Pallas kernels for 35%

profile of v5, /device:TPU:1, one launch (start us, length us, event | category | flops | bytes accessed | tf_op | source)
XLA Modules:
  0.0 59.0 jit_solution(13481140632672359528)
XLA Ops:
  0.0 0.1 pad_add_fusion.place
  0.1 0.0 copy-start.2
  0.1 0.9 %copy-done.2 = f32[24,2048]{1,0:T(8,128)S(1)} copy-done((f32[24,2048]{1,0:T(8,128)S(1)}, f32[24,2048]{1,0:T(8,128)}, u32[]{:S(2)}) %copy-start.2) | copy-done | bytes 196632
  1.0 0.0 copy-start.1
  1.0 3.7 %decay_factors.1 = (bf16[2048,768]{1,0:T(8,128)(2,1)S(1)}, bf16[2048,768]{1,0:T(8,128)(2,1)S(1)}, bf16[2064,72]{1,0:T(8,128)(2,1)S(1)}) custom-call(s32[4]{0:T(128)S(1)} %pad_add_fusion.place, bf16[2048,1536]{1,0:T(8,128)(2,1)} %x_hbm.1, f32[24,2048]{1,0:T(8,128)S(1)} %copy-done.2), custom_call_target="tpu_custom_call" | custom-call | tf_op jit(solution)/shard_map/decay_factors/pallas_call | solution.py:102
  4.7 0.0 copy-done.1
  4.7 2.0 %end_state.3 = f32[136,768]{1,0:T(8,128)S(1)} custom-call(s32[4]{0:T(128)S(1)} %pad_add_fusion.place, bf16[2048,768]{1,0:T(8,128)(2,1)S(1)} %get-tuple-element.67.x.x_ref, bf16[2048,128]{1,0:T(8,128)(2,1)S(1)} %copy-done.1, bf16[2064,72]{1,0:T(8,128)(2,1)S(1)} %get-tuple-element.66.factors), custom_call_target="tpu_custom_call" | custom-call | tf_op jit(solution)/shard_map/end_state/pallas_call | solution.py:133
  6.7 0.0 copy-start
  6.7 0.0 copy-start.3
  6.8 1.5 %collective-permute-start = (f32[136,768]{1,0:T(8,128)S(1)}, f32[136,768]{1,0:T(8,128)S(1)}, u32[]{:S(2)}, u32[]{:S(2)}) collective-permute-start(f32[136,768]{1,0:T(8,128)S(1)} %end_state.3), channel_id=1, source_target_pairs={{0,1},{1,0},{2,3},{3,2},{4,5},{5,4},{6,7},{7,6},{8,9},{9,8},{10,11... | collective-permute-start | bytes 1253384 | tf_op jit(solution)/shard_map/ppermute | solution.py:448
  8.3 2.0 %end_state.2.keep = f32[136,768]{1,0:T(8,128)S(1)} custom-call(s32[4]{0:T(128)S(1)} %pad_add_fusion.place, bf16[2048,768]{1,0:T(8,128)(2,1)S(1)} %get-tuple-element.65.x.x_ref, bf16[2048,128]{1,0:T(8,128)(2,1)S(1)} %copy-done.1, bf16[2064,72]{1,0:T(8,128)(2,1)S(1)} %get-tuple-element.66.factors), custom_call_target="tpu_custom_call" | custom-call | tf_op jit(solution)/shard_map/end_state/pallas_call | solution.py:133
  10.3 0.0 collective-permute-done.recv
  10.3 0.6 %pair.1 = (f32[25,8,128]{2,1,0:T(8,128)S(1)}, f32[25,8,128]{2,1,0:T(8,128)S(1)}, f32[25,8,128]{2,1,0:T(8,128)S(1)}, f32[25,8,128]{2,1,0:T(8,128)S(1)}) custom-call(s32[4]{0:T(128)S(1)} %pad_add_fusion.place, f32[136,768]{1,0:T(8,128)S(1)} %end_state.2.keep, f32[136,768]{1,0:T(8,128)S(1)} %collective-permute-done.recv), custom_call_target="tpu_custom_call" | custom-call | tf_op jit(solution)/shard_map/pair/pallas_call | solution.py:146
  10.9 1.4 %collective-permute-start.1 = (f32[25,8,128]{2,1,0:T(8,128)S(1)}, f32[25,8,128]{2,1,0:T(8,128)S(1)}, u32[]{:S(2)}, u32[]{:S(2)}) collective-permute-start(f32[25,8,128]{2,1,0:T(8,128)S(1)} %get-tuple-element.71), channel_id=1, source_target_pairs={{0,2},{1,3},{2,4},{3,5},{4,6},{5,7},{6,0},{7,1},{8,10},{9,11},{10,... | collective-permute-start | bytes 307208 | tf_op jit(solution)/shard_map/ppermute | solution.py:448
  12.3 1.4 %collective-permute-start.2 = (f32[25,8,128]{2,1,0:T(8,128)S(1)}, f32[25,8,128]{2,1,0:T(8,128)S(1)}, u32[]{:S(2)}, u32[]{:S(2)}) collective-permute-start(f32[25,8,128]{2,1,0:T(8,128)S(1)} %get-tuple-element.72), channel_id=1, source_target_pairs={{0,6},{1,7},{2,0},{3,1},{4,2},{5,3},{6,4},{7,5},{8,14},{9,15},{10,... | collective-permute-start | bytes 307208 | tf_op jit(solution)/shard_map/ppermute | solution.py:448
  13.7 0.0 copy-start.4
  13.7 1.6 %collective-permute-start.3 = (f32[25,8,128]{2,1,0:T(8,128)S(1)}, f32[25,8,128]{2,1,0:T(8,128)S(1)}, u32[]{:S(2)}, u32[]{:S(2)}) collective-permute-start(f32[25,8,128]{2,1,0:T(8,128)S(1)} %get-tuple-element.73), channel_id=1, source_target_pairs={{0,4},{1,5},{2,6},{3,7},{4,0},{5,1},{6,2},{7,3},{8,12},{9,13},{10,... | collective-permute-start | bytes 307208 | tf_op jit(solution)/shard_map/ppermute | solution.py:448
  15.3 0.0 copy-done
  15.3 0.0 copy-done.3
  15.3 2.8 %prepare.1 = (bf16[2048,1536]{1,0:T(8,128)(2,1)S(1)}, bf16[2048,256]{1,0:T(8,128)(2,1)S(1)}, bf16[2048,128]{1,0:T(8,128)(2,1)S(1)}, bf16[2304,72]{1,0:T(8,128)(2,1)S(1)}, bf16[2048,72]{1,0:T(8,128)(2,1)S(1)}) custom-call(bf16[2048,1536]{1,0:T(8,128)(2,1)} %gate_hbm.1, bf16[2048,128]{1,0:T(8,128)(2,1)S(1)} %copy-done.1, bf16[2048,128]{1,0:T(8,128)(2,1)S(1)} %copy-done, ...), custom_call_target="tpu_custom_call" | custom-call | tf_op jit(solution)/shard_map/prepare/pallas_call | solution.py:293
  18.1 0.0 copy-done.4
  18.1 2.1 %local.6 = (f32[2048,256]{1,0:T(8,128)S(1)}, bf16[2048,256]{1,0:T(8,128)(2,1)S(1)}) custom-call(s32[4]{0:T(128)S(1)} %pad_add_fusion.place, f32[24]{0:T(128)S(1)} %copy-done.4, bf16[2048,768]{1,0:T(8,128)(2,1)S(1)} %get-tuple-element.65.x.x_ref, bf16[2048,1536]{1,0:T(8,128)(2,1)S(1)} %get-tuple-element.74.gate_ref, ...), custom_call_target="tpu_custom_call" | custom-call | tf_op jit(solution)/shard_map/local/pallas_call | solution.py:350
  20.2 0.0 collective-permute-done.1.u1
  20.3 0.0 collective-permute-done.2.u3
  20.3 0.0 collective-permute-done.3.u2
  20.3 0.6 %line.1.v0 = f32[25,8,128]{2,1,0:T(8,128)S(1)} custom-call(s32[4]{0:T(128)S(1)} %pad_add_fusion.place, f32[25,8,128]{2,1,0:T(8,128)S(1)} %get-tuple-element.70.u0, f32[25,8,128]{2,1,0:T(8,128)S(1)} %collective-permute-done.1.u1, f32[25,8,128]{2,1,0:T(8,128)S(1)} %collective-permute-done.3.u2, f32[25,8,128]{2,1,0:T(8,128)S(1)} %collective-permute-done.2.u3), custom_call_target="tpu_custom_call" | custom-call | tf_op jit(solution)/shard_map/line/pallas_call | solution.py:146
  20.9 1.4 %collective-permute-start.4 = (f32[25,8,128]{2,1,0:T(8,128)S(1)}, f32[25,8,128]{2,1,0:T(8,128)S(1)}, u32[]{:S(2)}, u32[]{:S(2)}) collective-permute-start(f32[25,8,128]{2,1,0:T(8,128)S(1)} %line.1.v0), channel_id=1, source_target_pairs={{0,8},{1,9},{2,10},{3,11},{4,12},{5,13},{6,14},{7,15},{8,16},{9,17... | collective-permute-start | bytes 307208 | tf_op jit(solution)/shard_map/ppermute | solution.py:448
  22.3 1.5 %collective-permute-start.5 = (f32[25,8,128]{2,1,0:T(8,128)S(1)}, f32[25,8,128]{2,1,0:T(8,128)S(1)}, u32[]{:S(2)}, u32[]{:S(2)}) collective-permute-start(f32[25,8,128]{2,1,0:T(8,128)S(1)} %line.1.v0), channel_id=1, source_target_pairs={{0,24},{1,25},{2,26},{3,27},{4,28},{5,29},{6,30},{7,31},{8,0},{9,1... | collective-permute-start | bytes 307208 | tf_op jit(solution)/shard_map/ppermute | solution.py:448
  23.8 1.6 %collective-permute-start.6 = (f32[25,8,128]{2,1,0:T(8,128)S(1)}, f32[25,8,128]{2,1,0:T(8,128)S(1)}, u32[]{:S(2)}, u32[]{:S(2)}) collective-permute-start(f32[25,8,128]{2,1,0:T(8,128)S(1)} %line.1.v0), channel_id=1, source_target_pairs={{0,16},{1,17},{2,18},{3,19},{4,20},{5,21},{6,22},{7,23},{8,24},{9,... | collective-permute-start | bytes 307208 | tf_op jit(solution)/shard_map/ppermute | solution.py:448
  25.4 2.1 %local.7 = (f32[2048,256]{1,0:T(8,128)S(1)}, bf16[2048,256]{1,0:T(8,128)(2,1)S(1)}) custom-call(s32[4]{0:T(128)S(1)} %pad_add_fusion.place, f32[24]{0:T(128)S(1)} %copy-done.4, bf16[2048,768]{1,0:T(8,128)(2,1)S(1)} %get-tuple-element.65.x.x_ref, bf16[2048,1536]{1,0:T(8,128)(2,1)S(1)} %get-tuple-element.74.gate_ref, ...), custom_call_target="tpu_custom_call" | custom-call | tf_op jit(solution)/shard_map/local/pallas_call | solution.py:350
  27.5 2.1 %local.8 = (f32[2048,256]{1,0:T(8,128)S(1)}, bf16[2048,256]{1,0:T(8,128)(2,1)S(1)}) custom-call(s32[4]{0:T(128)S(1)} %pad_add_fusion.place, f32[24]{0:T(128)S(1)} %copy-done.4, bf16[2048,768]{1,0:T(8,128)(2,1)S(1)} %get-tuple-element.65.x.x_ref, bf16[2048,1536]{1,0:T(8,128)(2,1)S(1)} %get-tuple-element.74.gate_ref, ...), custom_call_target="tpu_custom_call" | custom-call | tf_op jit(solution)/shard_map/local/pallas_call | solution.py:350
  29.6 0.0 collective-permute-done.4.v1
  29.6 0.0 collective-permute-done.5.v3
  29.6 0.0 collective-permute-done.6.v2
  29.6 0.7 %plane.1 = (f32[25,8,128]{2,1,0:T(8,128)S(1)}, f32[25,8,128]{2,1,0:T(8,128)S(1)}) custom-call(s32[4]{0:T(128)S(1)} %pad_add_fusion.place, f32[25,8,128]{2,1,0:T(8,128)S(1)} %line.1.v0, f32[25,8,128]{2,1,0:T(8,128)S(1)} %collective-permute-done.4.v1, f32[25,8,128]{2,1,0:T(8,128)S(1)} %collective-permute-done.6.v2, f32[25,8,128]{2,1,0:T(8,128)S(1)} %collective-permute-done.5.v3), custom_call_target="tpu_custom_call" | custom-call | tf_op jit(solution)/shard_map/plane/pallas_call | solution.py:146
  30.3 1.7 %collective-permute-start.7 = (f32[25,8,128]{2,1,0:T(8,128)S(1)}, f32[25,8,128]{2,1,0:T(8,128)S(1)}, u32[]{:S(2)}, u32[]{:S(2)}) collective-permute-start(f32[25,8,128]{2,1,0:T(8,128)S(1)} %get-tuple-element.91.w0), channel_id=1, source_target_pairs={{0,32},{1,33},{2,34},{3,35},{4,36},{5,37},{6,38},{7,39},{8,40},{9,... | collective-permute-start | bytes 307208 | tf_op jit(solution)/shard_map/ppermute | solution.py:448
  32.0 2.2 %collective-permute-start.8 = (f32[25,8,128]{2,1,0:T(8,128)S(1)}, f32[25,8,128]{2,1,0:T(8,128)S(1)}, u32[]{:S(2)}, u32[]{:S(2)}) collective-permute-start(f32[25,8,128]{2,1,0:T(8,128)S(1)} %get-tuple-element.91.w0), channel_id=1, source_target_pairs={{0,96},{1,97},{2,98},{3,99},{4,100},{5,101},{6,102},{7,103},{8,104... | collective-permute-start | bytes 307208 | tf_op jit(solution)/shard_map/ppermute | solution.py:448
  34.2 1.2 %collective-permute-start.9 = (f32[25,8,128]{2,1,0:T(8,128)S(1)}, f32[25,8,128]{2,1,0:T(8,128)S(1)}, u32[]{:S(2)}, u32[]{:S(2)}) collective-permute-start(f32[25,8,128]{2,1,0:T(8,128)S(1)} %get-tuple-element.91.w0), channel_id=1, source_target_pairs={{0,64},{1,65},{2,66},{3,67},{4,68},{5,69},{6,70},{7,71},{8,72},{9,... | collective-permute-start | bytes 307208 | tf_op jit(solution)/shard_map/ppermute | solution.py:448
  35.4 2.1 %local.9 = (f32[2048,256]{1,0:T(8,128)S(1)}, bf16[2048,256]{1,0:T(8,128)(2,1)S(1)}) custom-call(s32[4]{0:T(128)S(1)} %pad_add_fusion.place, f32[24]{0:T(128)S(1)} %copy-done.4, bf16[2048,768]{1,0:T(8,128)(2,1)S(1)} %get-tuple-element.67.x.x_ref, bf16[2048,1536]{1,0:T(8,128)(2,1)S(1)} %get-tuple-element.74.gate_ref, ...), custom_call_target="tpu_custom_call" | custom-call | tf_op jit(solution)/shard_map/local/pallas_call | solution.py:350
  37.5 2.1 %local.10 = (f32[2048,256]{1,0:T(8,128)S(1)}, bf16[2048,256]{1,0:T(8,128)(2,1)S(1)}) custom-call(s32[4]{0:T(128)S(1)} %pad_add_fusion.place, f32[24]{0:T(128)S(1)} %copy-done.4, bf16[2048,768]{1,0:T(8,128)(2,1)S(1)} %get-tuple-element.67.x.x_ref, bf16[2048,1536]{1,0:T(8,128)(2,1)S(1)} %get-tuple-element.74.gate_ref, ...), custom_call_target="tpu_custom_call" | custom-call | tf_op jit(solution)/shard_map/local/pallas_call | solution.py:350
  39.6 0.0 collective-permute-done.7.w1
  39.7 0.0 collective-permute-done.8.w3
  39.7 0.4 collective-permute-done.9.w2
  40.0 0.9 %enter.1 = (f32[32,768]{1,0:T(8,128)S(1)}, f32[32,768]{1,0:T(8,128)S(1)}, f32[32,768]{1,0:T(8,128)S(1)}, f32[32,768]{1,0:T(8,128)S(1)}) custom-call(s32[4]{0:T(128)S(1)} %pad_add_fusion.place, f32[25,8,128]{2,1,0:T(8,128)S(1)} %get-tuple-element.91.w0, f32[25,8,128]{2,1,0:T(8,128)S(1)} %collective-permute-done.7.w1, ...), custom_call_target="tpu_custom_call" | custom-call | tf_op jit(solution)/shard_map/enter/pallas_call | solution.py:146
  40.9 0.2 collective-permute-start.10
  41.2 1.8 %collective-permute-start.11 = (f32[32,768]{1,0:T(8,128)S(1)}, f32[32,768]{1,0:T(8,128)S(1)}, u32[]{:S(2)}, u32[]{:S(2)}) collective-permute-start(f32[32,768]{1,0:T(8,128)S(1)} %get-tuple-element.102), channel_id=1, source_target_pairs={{0,4},{1,5},{2,6},{3,7},{4,0},{5,1},{6,2},{7,3},{8,12},{9,13},{10,... | collective-permute-start | bytes 294920 | tf_op jit(solution)/shard_map/ppermute | solution.py:448
  43.0 0.0 copy-start.5
  43.0 1.5 %collective-permute-start.12 = (f32[32,768]{1,0:T(8,128)S(1)}, f32[32,768]{1,0:T(8,128)S(1)}, u32[]{:S(2)}, u32[]{:S(2)}) collective-permute-start(f32[32,768]{1,0:T(8,128)S(1)} %get-tuple-element.103), channel_id=1, source_target_pairs={{0,6},{1,7},{2,0},{3,1},{4,2},{5,3},{6,4},{7,5},{8,14},{9,15},{10,... | collective-permute-start | bytes 294920 | tf_op jit(solution)/shard_map/ppermute | solution.py:448
  44.5 2.1 %local.11 = (f32[2048,256]{1,0:T(8,128)S(1)}, bf16[2048,256]{1,0:T(8,128)(2,1)S(1)}) custom-call(s32[4]{0:T(128)S(1)} %pad_add_fusion.place, f32[24]{0:T(128)S(1)} %copy-done.4, bf16[2048,768]{1,0:T(8,128)(2,1)S(1)} %get-tuple-element.67.x.x_ref, bf16[2048,1536]{1,0:T(8,128)(2,1)S(1)} %get-tuple-element.74.gate_ref, ...), custom_call_target="tpu_custom_call" | custom-call | tf_op jit(solution)/shard_map/local/pallas_call | solution.py:350
  46.6 0.1 collective-permute-done.10.e1
  46.7 0.0 collective-permute-done.11.e2
  46.8 0.6 collective-permute-done.12.e3
  47.3 0.7 %chip.1 = (f32[128,768]{1,0:T(8,128)S(1)}, f32[128,768]{1,0:T(8,128)S(1)}) custom-call(s32[4]{0:T(128)S(1)} %pad_add_fusion.place, f32[32,768]{1,0:T(8,128)S(1)} %get-tuple-element.100.e0, f32[32,768]{1,0:T(8,128)S(1)} %collective-permute-done.10.e1, f32[32,768]{1,0:T(8,128)S(1)} %collective-permute-done.11.e2, f32[32,768]{1,0:T(8,128)S(1)} %collective-permute-done.12.e3, ...), custom_call_target="tpu_custom_call" | custom-call | tf_op jit(solution)/shard_map/chip/pallas_call | solution.py:146
  48.0 4.0 %collective-permute-start.13 = (f32[128,768]{1,0:T(8,128)S(1)}, f32[128,768]{1,0:T(8,128)S(1)}, u32[]{:S(2)}, u32[]{:S(2)}) collective-permute-start(f32[128,768]{1,0:T(8,128)S(1)} %get-tuple-element.116), channel_id=1, source_target_pairs={{0,1},{1,0},{2,3},{3,2},{4,5},{5,4},{6,7},{7,6},{8,9},{9,8},{10,11... | collective-permute-start | bytes 1179656 | tf_op jit(solution)/shard_map/ppermute | solution.py:448
  52.0 0.0 copy-done.5
  52.0 3.0 %own_output.1.own = bf16[2048,768]{1,0:T(8,128)(2,1)S(1)} custom-call(s32[4]{0:T(128)S(1)} %pad_add_fusion.place, bf16[2048,128]{1,0:T(8,128)(2,1)S(1)} %copy-done, f32[1,1536]{1,0:T(1,128)S(1)} %broadcast_in_dim.3.gain_ref, f32[128,768]{1,0:T(8,128)S(1)} %get-tuple-element.109.state_ref, f32[2048,256]{1,0:T(8,128)S(1)} %get-tuple-element.110.refs_0_, ...), custom_call_target="tpu_custom_call" | custom-call | tf_op jit(solution)/shard_map/own_output/pallas_call | solution.py:386
  55.0 0.0 collective-permute-done.13.state_ref
  55.0 3.8 %output.1 = bf16[2048,1536]{1,0:T(8,128)(2,1)} custom-call(s32[4]{0:T(128)S(1)} %pad_add_fusion.place, bf16[2048,128]{1,0:T(8,128)(2,1)S(1)} %copy-done, f32[1,1536]{1,0:T(1,128)S(1)} %broadcast_in_dim.3.gain_ref, f32[128,768]{1,0:T(8,128)S(1)} %collective-permute-done.13.state_ref, bf16[2048,768]{1,0:T(8,128)(2,1)S(1)} %own_output.1.own, ...), custom_call_target="tpu_custom_call" | custom-call | tf_op jit(solution)/shard_map/output/pallas_call | solution.py:419
  (1 shorter events, 0.0 us)
Async XLA Ops:
  0.1 0.9 %copy-start.2 = (f32[24,2048]{1,0:T(8,128)S(1)}, f32[24,2048]{1,0:T(8,128)}, u32[]{:S(2)}) copy-start(f32[24,2048]{1,0:T(8,128)} %decay_ref.1) | copy-start | bytes 589828
  1.0 3.7 %copy-start.1 = (bf16[2048,128]{1,0:T(8,128)(2,1)S(1)}, bf16[2048,128]{1,0:T(8,128)(2,1)}, u32[]{:S(2)}) copy-start(bf16[2048,128]{1,0:T(8,128)(2,1)} %b_ref.1) | copy-start | bytes 1572868
  6.7 8.6 %copy-start = (bf16[2048,128]{1,0:T(8,128)(2,1)S(1)}, bf16[2048,128]{1,0:T(8,128)(2,1)}, u32[]{:S(2)}) copy-start(bf16[2048,128]{1,0:T(8,128)(2,1)} %c_ref.5) | copy-start | bytes 1572868
  6.7 8.5 %copy-start.3 = (f32[24,2048]{1,0:T(8,128)S(1)}, f32[24,2048]{1,0:T(8,128)}, u32[]{:S(2)}) copy-start(f32[24,2048]{1,0:T(8,128)} %decay_ref.1) | copy-start | bytes 589828
  6.8 3.5 %collective-permute-start = (f32[136,768]{1,0:T(8,128)S(1)}, f32[136,768]{1,0:T(8,128)S(1)}, u32[]{:S(2)}, u32[]{:S(2)}) collective-permute-start(f32[136,768]{1,0:T(8,128)S(1)} %end_state.3), channel_id=1, source_target_pairs={{0,1},{1,0},{2,3},{3,2},{4,5},{5,4},{6,7},{7,6},{8,9},{9,8},{10,11... | collective-permute-start | bytes 1253384 | tf_op jit(solution)/shard_map/ppermute | solution.py:448
  10.9 9.3 %collective-permute-start.1 = (f32[25,8,128]{2,1,0:T(8,128)S(1)}, f32[25,8,128]{2,1,0:T(8,128)S(1)}, u32[]{:S(2)}, u32[]{:S(2)}) collective-permute-start(f32[25,8,128]{2,1,0:T(8,128)S(1)} %get-tuple-element.71), channel_id=1, source_target_pairs={{0,2},{1,3},{2,4},{3,5},{4,6},{5,7},{6,0},{7,1},{8,10},{9,11},{10,... | collective-permute-start | bytes 307208 | tf_op jit(solution)/shard_map/ppermute | solution.py:448
  12.3 8.0 %collective-permute-start.2 = (f32[25,8,128]{2,1,0:T(8,128)S(1)}, f32[25,8,128]{2,1,0:T(8,128)S(1)}, u32[]{:S(2)}, u32[]{:S(2)}) collective-permute-start(f32[25,8,128]{2,1,0:T(8,128)S(1)} %get-tuple-element.72), channel_id=1, source_target_pairs={{0,6},{1,7},{2,0},{3,1},{4,2},{5,3},{6,4},{7,5},{8,14},{9,15},{10,... | collective-permute-start | bytes 307208 | tf_op jit(solution)/shard_map/ppermute | solution.py:448
  13.7 4.4 %copy-start.4 = (f32[24]{0:T(128)S(1)}, f32[24]{0:T(128)}, u32[]{:S(2)}) copy-start(f32[24]{0:T(128)} %skip_ref.11) | copy-start | bytes 292
  13.7 6.6 %collective-permute-start.3 = (f32[25,8,128]{2,1,0:T(8,128)S(1)}, f32[25,8,128]{2,1,0:T(8,128)S(1)}, u32[]{:S(2)}, u32[]{:S(2)}) collective-permute-start(f32[25,8,128]{2,1,0:T(8,128)S(1)} %get-tuple-element.73), channel_id=1, source_target_pairs={{0,4},{1,5},{2,6},{3,7},{4,0},{5,1},{6,2},{7,3},{8,12},{9,13},{10,... | collective-permute-start | bytes 307208 | tf_op jit(solution)/shard_map/ppermute | solution.py:448
  20.9 8.7 %collective-permute-start.4 = (f32[25,8,128]{2,1,0:T(8,128)S(1)}, f32[25,8,128]{2,1,0:T(8,128)S(1)}, u32[]{:S(2)}, u32[]{:S(2)}) collective-permute-start(f32[25,8,128]{2,1,0:T(8,128)S(1)} %line.1.v0), channel_id=1, source_target_pairs={{0,8},{1,9},{2,10},{3,11},{4,12},{5,13},{6,14},{7,15},{8,16},{9,17... | collective-permute-start | bytes 307208 | tf_op jit(solution)/shard_map/ppermute | solution.py:448
  22.3 7.3 %collective-permute-start.5 = (f32[25,8,128]{2,1,0:T(8,128)S(1)}, f32[25,8,128]{2,1,0:T(8,128)S(1)}, u32[]{:S(2)}, u32[]{:S(2)}) collective-permute-start(f32[25,8,128]{2,1,0:T(8,128)S(1)} %line.1.v0), channel_id=1, source_target_pairs={{0,24},{1,25},{2,26},{3,27},{4,28},{5,29},{6,30},{7,31},{8,0},{9,1... | collective-permute-start | bytes 307208 | tf_op jit(solution)/shard_map/ppermute | solution.py:448
  23.8 5.8 %collective-permute-start.6 = (f32[25,8,128]{2,1,0:T(8,128)S(1)}, f32[25,8,128]{2,1,0:T(8,128)S(1)}, u32[]{:S(2)}, u32[]{:S(2)}) collective-permute-start(f32[25,8,128]{2,1,0:T(8,128)S(1)} %line.1.v0), channel_id=1, source_target_pairs={{0,16},{1,17},{2,18},{3,19},{4,20},{5,21},{6,22},{7,23},{8,24},{9,... | collective-permute-start | bytes 307208 | tf_op jit(solution)/shard_map/ppermute | solution.py:448
  30.3 9.3 %collective-permute-start.7 = (f32[25,8,128]{2,1,0:T(8,128)S(1)}, f32[25,8,128]{2,1,0:T(8,128)S(1)}, u32[]{:S(2)}, u32[]{:S(2)}) collective-permute-start(f32[25,8,128]{2,1,0:T(8,128)S(1)} %get-tuple-element.91.w0), channel_id=1, source_target_pairs={{0,32},{1,33},{2,34},{3,35},{4,36},{5,37},{6,38},{7,39},{8,40},{9,... | collective-permute-start | bytes 307208 | tf_op jit(solution)/shard_map/ppermute | solution.py:448
  32.0 7.7 %collective-permute-start.8 = (f32[25,8,128]{2,1,0:T(8,128)S(1)}, f32[25,8,128]{2,1,0:T(8,128)S(1)}, u32[]{:S(2)}, u32[]{:S(2)}) collective-permute-start(f32[25,8,128]{2,1,0:T(8,128)S(1)} %get-tuple-element.91.w0), channel_id=1, source_target_pairs={{0,96},{1,97},{2,98},{3,99},{4,100},{5,101},{6,102},{7,103},{8,104... | collective-permute-start | bytes 307208 | tf_op jit(solution)/shard_map/ppermute | solution.py:448
  34.2 5.8 %collective-permute-start.9 = (f32[25,8,128]{2,1,0:T(8,128)S(1)}, f32[25,8,128]{2,1,0:T(8,128)S(1)}, u32[]{:S(2)}, u32[]{:S(2)}) collective-permute-start(f32[25,8,128]{2,1,0:T(8,128)S(1)} %get-tuple-element.91.w0), channel_id=1, source_target_pairs={{0,64},{1,65},{2,66},{3,67},{4,68},{5,69},{6,70},{7,71},{8,72},{9,... | collective-permute-start | bytes 307208 | tf_op jit(solution)/shard_map/ppermute | solution.py:448
  40.9 5.8 %collective-permute-start.10 = (f32[32,768]{1,0:T(8,128)S(1)}, f32[32,768]{1,0:T(8,128)S(1)}, u32[]{:S(2)}, u32[]{:S(2)}) collective-permute-start(f32[32,768]{1,0:T(8,128)S(1)} %get-tuple-element.101), channel_id=1, source_target_pairs={{0,2},{1,3},{2,4},{3,5},{4,6},{5,7},{6,0},{7,1},{8,10},{9,11},{10,... | collective-permute-start | bytes 294920 | tf_op jit(solution)/shard_map/ppermute | solution.py:448
  41.2 5.6 %collective-permute-start.11 = (f32[32,768]{1,0:T(8,128)S(1)}, f32[32,768]{1,0:T(8,128)S(1)}, u32[]{:S(2)}, u32[]{:S(2)}) collective-permute-start(f32[32,768]{1,0:T(8,128)S(1)} %get-tuple-element.102), channel_id=1, source_target_pairs={{0,4},{1,5},{2,6},{3,7},{4,0},{5,1},{6,2},{7,3},{8,12},{9,13},{10,... | collective-permute-start | bytes 294920 | tf_op jit(solution)/shard_map/ppermute | solution.py:448
  43.0 9.0 %copy-start.5 = (f32[1536]{0:T(1024)S(1)}, f32[1536]{0:T(1024)}, u32[]{:S(2)}) copy-start(f32[1536]{0:T(1024)} %param.13) | copy-start | bytes 18436
  43.0 4.3 %collective-permute-start.12 = (f32[32,768]{1,0:T(8,128)S(1)}, f32[32,768]{1,0:T(8,128)S(1)}, u32[]{:S(2)}, u32[]{:S(2)}) collective-permute-start(f32[32,768]{1,0:T(8,128)S(1)} %get-tuple-element.103), channel_id=1, source_target_pairs={{0,6},{1,7},{2,0},{3,1},{4,2},{5,3},{6,4},{7,5},{8,14},{9,15},{10,... | collective-permute-start | bytes 294920 | tf_op jit(solution)/shard_map/ppermute | solution.py:448
  48.0 7.0 %collective-permute-start.13 = (f32[128,768]{1,0:T(8,128)S(1)}, f32[128,768]{1,0:T(8,128)S(1)}, u32[]{:S(2)}, u32[]{:S(2)}) collective-permute-start(f32[128,768]{1,0:T(8,128)S(1)} %get-tuple-element.116), channel_id=1, source_target_pairs={{0,1},{1,0},{2,3},{3,2},{4,5},{5,4},{6,7},{7,6},{8,9},{9,8},{10,11... | collective-permute-start | bytes 1179656 | tf_op jit(solution)/shard_map/ppermute | solution.py:448

commit v6 on v5

--- a/solution.py
+++ b/solution.py
@@ -19,7 +19,7 @@
 SHIFT = 74
 SHIFT_LOG = 51.29289136
 OUT_STEP = 256
-FETCH = 512
+FETCH = 2048
 QUARTER = STATE // 4
 TILES = QUARTER // 8 * (HALF // 128)
 FETCH_LIMIT = 42 * 1024 * 1024
@@ -478,7 +478,7 @@
     w0, before = small_call(plane_kernel, "plane", place, columns, [piece] * 2)
     planes = [w0] + list(work(2, far_last, *[moved(w0, Z, s) for s in (1, 2, 3)]))
     e0, *sends = small_call(enter_kernel, "enter", place, planes + [before] + lines, [chunk] * 4)
-    entering = [e0] + list(work(1, (0, 1, 2), *[moved(v, X, s + 1) for s, v in enumerate(sends)]))
+    entering = [e0] + list(work(1, (1, 0, 2), *[moved(v, X, s + 1) for s, v in enumerate(sends)]))
     own, send = small_call(chip_kernel, "chip", place, entering + [keep, recv], [(STATE, HALF)] * 2)
     other = moved(send, CORE, 1)
     half = len(parts) // 2

time: 59.2 us -> 58.9 us (level)
  transfers between devices with their start and end apart: 14 -> 14, of which waited for: 3 -> 2; matrix products, arithmetic and copies ran while one was open for 0% -> 0% of each run, Pallas kernels for 35% -> 35%
where the time goes in v6:
time: 58.9 us; the launch traced here: 58.7 us
  Pallas kernels  33.3 us (57%)
  starting transfers between devices  23.1 us (39%)
  local copies, waits for them, and re-layouts  0.96 us (2%)
  waiting for transfers between devices  0.87 us (1%)
    ppermute x14, starting transfers between devices, moved(): return lax.ppermute(value, ('grp', 'dev'), pairs)  23.1 us
    pallas_call x6, Pallas kernels, local(): pl.pallas_call(functools.partial(local_kernel, part), in_specs=[pl.BlockS...  12.6 us
    pallas_call x2, Pallas kernels, end_state(): pl.pallas_call(functools.partial(state_kernel, mine), in_specs=[pl.BlockS...  4.07 us
    pallas_call x1, Pallas kernels, output(): pl.pallas_call(output_kernel, in_specs=[pl.BlockSpec(memory_space=pltpu.S...  3.8 us
    pallas_call x1, Pallas kernels, decay_factors(): pl.pallas_call(factors_kernel, in_specs=[pl.BlockSpec(memory_space=pltpu....  3.56 us
    pallas_call x5, Pallas kernels, small_call(): pl.pallas_call(kernel, in_specs=[pl.BlockSpec(memory_space=pltpu.SMEM)] +...  3.49 us
    pallas_call x1, Pallas kernels, own_output(): pl.pallas_call(own_output_kernel, in_specs=[pl.BlockSpec(memory_space=plt...  2.95 us
    pallas_call x1, Pallas kernels, prepare(): pl.pallas_call(prepare_kernel, in_specs=[pl.BlockSpec(memory_space=pltpu....  2.8 us
  transfers between devices with their start and end apart: 14, of which 2 were waited for; matrix products, arithmetic and copies ran while one was open for 0% of the time, Pallas kernels for 35%

profile of v6, /device:TPU:1, one launch (start us, length us, event | category | flops | bytes accessed | tf_op | source)
XLA Modules:
  0.0 58.7 jit_solution(402014190534057507)
XLA Ops:
  0.0 0.1 pad_add_fusion.place
  0.1 0.0 copy-start.2
  0.1 0.9 %copy-done.2 = f32[24,2048]{1,0:T(8,128)S(1)} copy-done((f32[24,2048]{1,0:T(8,128)S(1)}, f32[24,2048]{1,0:T(8,128)}, u32[]{:S(2)}) %copy-start.2) | copy-done | bytes 196632
  1.0 0.0 copy-start.1
  1.0 3.6 %decay_factors.1 = (bf16[2048,768]{1,0:T(8,128)(2,1)S(1)}, bf16[2048,768]{1,0:T(8,128)(2,1)S(1)}, bf16[2064,72]{1,0:T(8,128)(2,1)S(1)}) custom-call(s32[4]{0:T(128)S(1)} %pad_add_fusion.place, bf16[2048,1536]{1,0:T(8,128)(2,1)} %x_hbm.1, f32[24,2048]{1,0:T(8,128)S(1)} %copy-done.2), custom_call_target="tpu_custom_call" | custom-call | tf_op jit(solution)/shard_map/decay_factors/pallas_call | solution.py:102
  4.6 0.0 copy-done.1
  4.6 2.0 %end_state.3 = f32[136,768]{1,0:T(8,128)S(1)} custom-call(s32[4]{0:T(128)S(1)} %pad_add_fusion.place, bf16[2048,768]{1,0:T(8,128)(2,1)S(1)} %get-tuple-element.67.x.x_ref, bf16[2048,128]{1,0:T(8,128)(2,1)S(1)} %copy-done.1, bf16[2064,72]{1,0:T(8,128)(2,1)S(1)} %get-tuple-element.66.factors), custom_call_target="tpu_custom_call" | custom-call | tf_op jit(solution)/shard_map/end_state/pallas_call | solution.py:133
  6.6 0.0 copy-start
  6.6 0.0 copy-start.3
  6.7 1.5 %collective-permute-start = (f32[136,768]{1,0:T(8,128)S(1)}, f32[136,768]{1,0:T(8,128)S(1)}, u32[]{:S(2)}, u32[]{:S(2)}) collective-permute-start(f32[136,768]{1,0:T(8,128)S(1)} %end_state.3), channel_id=1, source_target_pairs={{0,1},{1,0},{2,3},{3,2},{4,5},{5,4},{6,7},{7,6},{8,9},{9,8},{10,11... | collective-permute-start | bytes 1253384 | tf_op jit(solution)/shard_map/ppermute | solution.py:448
  8.2 2.0 %end_state.2.keep = f32[136,768]{1,0:T(8,128)S(1)} custom-call(s32[4]{0:T(128)S(1)} %pad_add_fusion.place, bf16[2048,768]{1,0:T(8,128)(2,1)S(1)} %get-tuple-element.65.x.x_ref, bf16[2048,128]{1,0:T(8,128)(2,1)S(1)} %copy-done.1, bf16[2064,72]{1,0:T(8,128)(2,1)S(1)} %get-tuple-element.66.factors), custom_call_target="tpu_custom_call" | custom-call | tf_op jit(solution)/shard_map/end_state/pallas_call | solution.py:133
  10.2 0.0 collective-permute-done.recv
  10.2 0.6 %pair.1 = (f32[25,8,128]{2,1,0:T(8,128)S(1)}, f32[25,8,128]{2,1,0:T(8,128)S(1)}, f32[25,8,128]{2,1,0:T(8,128)S(1)}, f32[25,8,128]{2,1,0:T(8,128)S(1)}) custom-call(s32[4]{0:T(128)S(1)} %pad_add_fusion.place, f32[136,768]{1,0:T(8,128)S(1)} %end_state.2.keep, f32[136,768]{1,0:T(8,128)S(1)} %collective-permute-done.recv), custom_call_target="tpu_custom_call" | custom-call | tf_op jit(solution)/shard_map/pair/pallas_call | solution.py:146
  10.8 1.4 %collective-permute-start.1 = (f32[25,8,128]{2,1,0:T(8,128)S(1)}, f32[25,8,128]{2,1,0:T(8,128)S(1)}, u32[]{:S(2)}, u32[]{:S(2)}) collective-permute-start(f32[25,8,128]{2,1,0:T(8,128)S(1)} %get-tuple-element.71), channel_id=1, source_target_pairs={{0,2},{1,3},{2,4},{3,5},{4,6},{5,7},{6,0},{7,1},{8,10},{9,11},{10,... | collective-permute-start | bytes 307208 | tf_op jit(solution)/shard_map/ppermute | solution.py:448
  12.2 1.4 %collective-permute-start.2 = (f32[25,8,128]{2,1,0:T(8,128)S(1)}, f32[25,8,128]{2,1,0:T(8,128)S(1)}, u32[]{:S(2)}, u32[]{:S(2)}) collective-permute-start(f32[25,8,128]{2,1,0:T(8,128)S(1)} %get-tuple-element.72), channel_id=1, source_target_pairs={{0,6},{1,7},{2,0},{3,1},{4,2},{5,3},{6,4},{7,5},{8,14},{9,15},{10,... | collective-permute-start | bytes 307208 | tf_op jit(solution)/shard_map/ppermute | solution.py:448
  13.6 0.0 copy-start.4
  13.6 1.6 %collective-permute-start.3 = (f32[25,8,128]{2,1,0:T(8,128)S(1)}, f32[25,8,128]{2,1,0:T(8,128)S(1)}, u32[]{:S(2)}, u32[]{:S(2)}) collective-permute-start(f32[25,8,128]{2,1,0:T(8,128)S(1)} %get-tuple-element.73), channel_id=1, source_target_pairs={{0,4},{1,5},{2,6},{3,7},{4,0},{5,1},{6,2},{7,3},{8,12},{9,13},{10,... | collective-permute-start | bytes 307208 | tf_op jit(solution)/shard_map/ppermute | solution.py:448
  15.2 0.0 copy-done
  15.2 0.0 copy-done.3
  15.2 2.8 %prepare.1 = (bf16[2048,1536]{1,0:T(8,128)(2,1)S(1)}, bf16[2048,256]{1,0:T(8,128)(2,1)S(1)}, bf16[2048,128]{1,0:T(8,128)(2,1)S(1)}, bf16[2304,72]{1,0:T(8,128)(2,1)S(1)}, bf16[2048,72]{1,0:T(8,128)(2,1)S(1)}) custom-call(bf16[2048,1536]{1,0:T(8,128)(2,1)} %gate_hbm.1, bf16[2048,128]{1,0:T(8,128)(2,1)S(1)} %copy-done.1, bf16[2048,128]{1,0:T(8,128)(2,1)S(1)} %copy-done, ...), custom_call_target="tpu_custom_call" | custom-call | tf_op jit(solution)/shard_map/prepare/pallas_call | solution.py:293
  18.0 0.0 copy-done.4
  18.0 2.1 %local.6 = (f32[2048,256]{1,0:T(8,128)S(1)}, bf16[2048,256]{1,0:T(8,128)(2,1)S(1)}) custom-call(s32[4]{0:T(128)S(1)} %pad_add_fusion.place, f32[24]{0:T(128)S(1)} %copy-done.4, bf16[2048,768]{1,0:T(8,128)(2,1)S(1)} %get-tuple-element.65.x.x_ref, bf16[2048,1536]{1,0:T(8,128)(2,1)S(1)} %get-tuple-element.74.gate_ref, ...), custom_call_target="tpu_custom_call" | custom-call | tf_op jit(solution)/shard_map/local/pallas_call | solution.py:350
  20.1 0.0 collective-permute-done.1.u1
  20.2 0.0 collective-permute-done.2.u3
  20.2 0.0 collective-permute-done.3.u2
  20.2 0.6 %line.1.v0 = f32[25,8,128]{2,1,0:T(8,128)S(1)} custom-call(s32[4]{0:T(128)S(1)} %pad_add_fusion.place, f32[25,8,128]{2,1,0:T(8,128)S(1)} %get-tuple-element.70.u0, f32[25,8,128]{2,1,0:T(8,128)S(1)} %collective-permute-done.1.u1, f32[25,8,128]{2,1,0:T(8,128)S(1)} %collective-permute-done.3.u2, f32[25,8,128]{2,1,0:T(8,128)S(1)} %collective-permute-done.2.u3), custom_call_target="tpu_custom_call" | custom-call | tf_op jit(solution)/shard_map/line/pallas_call | solution.py:146
  20.8 1.4 %collective-permute-start.4 = (f32[25,8,128]{2,1,0:T(8,128)S(1)}, f32[25,8,128]{2,1,0:T(8,128)S(1)}, u32[]{:S(2)}, u32[]{:S(2)}) collective-permute-start(f32[25,8,128]{2,1,0:T(8,128)S(1)} %line.1.v0), channel_id=1, source_target_pairs={{0,8},{1,9},{2,10},{3,11},{4,12},{5,13},{6,14},{7,15},{8,16},{9,17... | collective-permute-start | bytes 307208 | tf_op jit(solution)/shard_map/ppermute | solution.py:448
  22.2 1.5 %collective-permute-start.5 = (f32[25,8,128]{2,1,0:T(8,128)S(1)}, f32[25,8,128]{2,1,0:T(8,128)S(1)}, u32[]{:S(2)}, u32[]{:S(2)}) collective-permute-start(f32[25,8,128]{2,1,0:T(8,128)S(1)} %line.1.v0), channel_id=1, source_target_pairs={{0,24},{1,25},{2,26},{3,27},{4,28},{5,29},{6,30},{7,31},{8,0},{9,1... | collective-permute-start | bytes 307208 | tf_op jit(solution)/shard_map/ppermute | solution.py:448
  23.7 1.6 %collective-permute-start.6 = (f32[25,8,128]{2,1,0:T(8,128)S(1)}, f32[25,8,128]{2,1,0:T(8,128)S(1)}, u32[]{:S(2)}, u32[]{:S(2)}) collective-permute-start(f32[25,8,128]{2,1,0:T(8,128)S(1)} %line.1.v0), channel_id=1, source_target_pairs={{0,16},{1,17},{2,18},{3,19},{4,20},{5,21},{6,22},{7,23},{8,24},{9,... | collective-permute-start | bytes 307208 | tf_op jit(solution)/shard_map/ppermute | solution.py:448
  25.3 2.1 %local.7 = (f32[2048,256]{1,0:T(8,128)S(1)}, bf16[2048,256]{1,0:T(8,128)(2,1)S(1)}) custom-call(s32[4]{0:T(128)S(1)} %pad_add_fusion.place, f32[24]{0:T(128)S(1)} %copy-done.4, bf16[2048,768]{1,0:T(8,128)(2,1)S(1)} %get-tuple-element.65.x.x_ref, bf16[2048,1536]{1,0:T(8,128)(2,1)S(1)} %get-tuple-element.74.gate_ref, ...), custom_call_target="tpu_custom_call" | custom-call | tf_op jit(solution)/shard_map/local/pallas_call | solution.py:350
  27.4 2.1 %local.8 = (f32[2048,256]{1,0:T(8,128)S(1)}, bf16[2048,256]{1,0:T(8,128)(2,1)S(1)}) custom-call(s32[4]{0:T(128)S(1)} %pad_add_fusion.place, f32[24]{0:T(128)S(1)} %copy-done.4, bf16[2048,768]{1,0:T(8,128)(2,1)S(1)} %get-tuple-element.65.x.x_ref, bf16[2048,1536]{1,0:T(8,128)(2,1)S(1)} %get-tuple-element.74.gate_ref, ...), custom_call_target="tpu_custom_call" | custom-call | tf_op jit(solution)/shard_map/local/pallas_call | solution.py:350
  29.5 0.0 collective-permute-done.4.v1
  29.5 0.0 collective-permute-done.5.v3
  29.5 0.0 collective-permute-done.6.v2
  29.5 0.7 %plane.1 = (f32[25,8,128]{2,1,0:T(8,128)S(1)}, f32[25,8,128]{2,1,0:T(8,128)S(1)}) custom-call(s32[4]{0:T(128)S(1)} %pad_add_fusion.place, f32[25,8,128]{2,1,0:T(8,128)S(1)} %line.1.v0, f32[25,8,128]{2,1,0:T(8,128)S(1)} %collective-permute-done.4.v1, f32[25,8,128]{2,1,0:T(8,128)S(1)} %collective-permute-done.6.v2, f32[25,8,128]{2,1,0:T(8,128)S(1)} %collective-permute-done.5.v3), custom_call_target="tpu_custom_call" | custom-call | tf_op jit(solution)/shard_map/plane/pallas_call | solution.py:146
  30.2 1.7 %collective-permute-start.7 = (f32[25,8,128]{2,1,0:T(8,128)S(1)}, f32[25,8,128]{2,1,0:T(8,128)S(1)}, u32[]{:S(2)}, u32[]{:S(2)}) collective-permute-start(f32[25,8,128]{2,1,0:T(8,128)S(1)} %get-tuple-element.91.w0), channel_id=1, source_target_pairs={{0,32},{1,33},{2,34},{3,35},{4,36},{5,37},{6,38},{7,39},{8,40},{9,... | collective-permute-start | bytes 307208 | tf_op jit(solution)/shard_map/ppermute | solution.py:448
  31.9 2.2 %collective-permute-start.8 = (f32[25,8,128]{2,1,0:T(8,128)S(1)}, f32[25,8,128]{2,1,0:T(8,128)S(1)}, u32[]{:S(2)}, u32[]{:S(2)}) collective-permute-start(f32[25,8,128]{2,1,0:T(8,128)S(1)} %get-tuple-element.91.w0), channel_id=1, source_target_pairs={{0,96},{1,97},{2,98},{3,99},{4,100},{5,101},{6,102},{7,103},{8,104... | collective-permute-start | bytes 307208 | tf_op jit(solution)/shard_map/ppermute | solution.py:448
  34.1 1.2 %collective-permute-start.9 = (f32[25,8,128]{2,1,0:T(8,128)S(1)}, f32[25,8,128]{2,1,0:T(8,128)S(1)}, u32[]{:S(2)}, u32[]{:S(2)}) collective-permute-start(f32[25,8,128]{2,1,0:T(8,128)S(1)} %get-tuple-element.91.w0), channel_id=1, source_target_pairs={{0,64},{1,65},{2,66},{3,67},{4,68},{5,69},{6,70},{7,71},{8,72},{9,... | collective-permute-start | bytes 307208 | tf_op jit(solution)/shard_map/ppermute | solution.py:448
  35.3 2.1 %local.9 = (f32[2048,256]{1,0:T(8,128)S(1)}, bf16[2048,256]{1,0:T(8,128)(2,1)S(1)}) custom-call(s32[4]{0:T(128)S(1)} %pad_add_fusion.place, f32[24]{0:T(128)S(1)} %copy-done.4, bf16[2048,768]{1,0:T(8,128)(2,1)S(1)} %get-tuple-element.67.x.x_ref, bf16[2048,1536]{1,0:T(8,128)(2,1)S(1)} %get-tuple-element.74.gate_ref, ...), custom_call_target="tpu_custom_call" | custom-call | tf_op jit(solution)/shard_map/local/pallas_call | solution.py:350
  37.4 2.1 %local.10 = (f32[2048,256]{1,0:T(8,128)S(1)}, bf16[2048,256]{1,0:T(8,128)(2,1)S(1)}) custom-call(s32[4]{0:T(128)S(1)} %pad_add_fusion.place, f32[24]{0:T(128)S(1)} %copy-done.4, bf16[2048,768]{1,0:T(8,128)(2,1)S(1)} %get-tuple-element.67.x.x_ref, bf16[2048,1536]{1,0:T(8,128)(2,1)S(1)} %get-tuple-element.74.gate_ref, ...), custom_call_target="tpu_custom_call" | custom-call | tf_op jit(solution)/shard_map/local/pallas_call | solution.py:350
  39.6 0.0 collective-permute-done.7.w1
  39.6 0.0 collective-permute-done.8.w3
  39.6 0.4 collective-permute-done.9.w2
  39.9 0.9 %enter.1 = (f32[32,768]{1,0:T(8,128)S(1)}, f32[32,768]{1,0:T(8,128)S(1)}, f32[32,768]{1,0:T(8,128)S(1)}, f32[32,768]{1,0:T(8,128)S(1)}) custom-call(s32[4]{0:T(128)S(1)} %pad_add_fusion.place, f32[25,8,128]{2,1,0:T(8,128)S(1)} %get-tuple-element.91.w0, f32[25,8,128]{2,1,0:T(8,128)S(1)} %collective-permute-done.7.w1, ...), custom_call_target="tpu_custom_call" | custom-call | tf_op jit(solution)/shard_map/enter/pallas_call | solution.py:146
  40.8 1.5 %collective-permute-start.10 = (f32[32,768]{1,0:T(8,128)S(1)}, f32[32,768]{1,0:T(8,128)S(1)}, u32[]{:S(2)}, u32[]{:S(2)}) collective-permute-start(f32[32,768]{1,0:T(8,128)S(1)} %get-tuple-element.101), channel_id=1, source_target_pairs={{0,4},{1,5},{2,6},{3,7},{4,0},{5,1},{6,2},{7,3},{8,12},{9,13},{10,... | collective-permute-start | bytes 294920 | tf_op jit(solution)/shard_map/ppermute | solution.py:448
  42.4 0.0 collective-permute-start.11
  42.4 0.0 copy-start.5
  42.4 2.7 %collective-permute-start.12 = (f32[32,768]{1,0:T(8,128)S(1)}, f32[32,768]{1,0:T(8,128)S(1)}, u32[]{:S(2)}, u32[]{:S(2)}) collective-permute-start(f32[32,768]{1,0:T(8,128)S(1)} %get-tuple-element.103), channel_id=1, source_target_pairs={{0,6},{1,7},{2,0},{3,1},{4,2},{5,3},{6,4},{7,5},{8,14},{9,15},{10,... | collective-permute-start | bytes 294920 | tf_op jit(solution)/shard_map/ppermute | solution.py:448
  45.0 2.1 %local.11 = (f32[2048,256]{1,0:T(8,128)S(1)}, bf16[2048,256]{1,0:T(8,128)(2,1)S(1)}) custom-call(s32[4]{0:T(128)S(1)} %pad_add_fusion.place, f32[24]{0:T(128)S(1)} %copy-done.4, bf16[2048,768]{1,0:T(8,128)(2,1)S(1)} %get-tuple-element.67.x.x_ref, bf16[2048,1536]{1,0:T(8,128)(2,1)S(1)} %get-tuple-element.74.gate_ref, ...), custom_call_target="tpu_custom_call" | custom-call | tf_op jit(solution)/shard_map/local/pallas_call | solution.py:350
  47.2 0.0 collective-permute-done.10.e2
  47.2 0.0 collective-permute-done.11.e1
  47.2 0.5 collective-permute-done.12.e3
  47.7 0.7 %chip.1 = (f32[128,768]{1,0:T(8,128)S(1)}, f32[128,768]{1,0:T(8,128)S(1)}) custom-call(s32[4]{0:T(128)S(1)} %pad_add_fusion.place, f32[32,768]{1,0:T(8,128)S(1)} %get-tuple-element.100.e0, f32[32,768]{1,0:T(8,128)S(1)} %collective-permute-done.11.e1, f32[32,768]{1,0:T(8,128)S(1)} %collective-permute-done.10.e2, f32[32,768]{1,0:T(8,128)S(1)} %collective-permute-done.12.e3, ...), custom_call_target="tpu_custom_call" | custom-call | tf_op jit(solution)/shard_map/chip/pallas_call | solution.py:146
  48.3 3.4 %collective-permute-start.13 = (f32[128,768]{1,0:T(8,128)S(1)}, f32[128,768]{1,0:T(8,128)S(1)}, u32[]{:S(2)}, u32[]{:S(2)}) collective-permute-start(f32[128,768]{1,0:T(8,128)S(1)} %get-tuple-element.116), channel_id=1, source_target_pairs={{0,1},{1,0},{2,3},{3,2},{4,5},{5,4},{6,7},{7,6},{8,9},{9,8},{10,11... | collective-permute-start | bytes 1179656 | tf_op jit(solution)/shard_map/ppermute | solution.py:448
  51.8 0.0 copy-done.5
  51.8 3.0 %own_output.1.own = bf16[2048,768]{1,0:T(8,128)(2,1)S(1)} custom-call(s32[4]{0:T(128)S(1)} %pad_add_fusion.place, bf16[2048,128]{1,0:T(8,128)(2,1)S(1)} %copy-done, f32[1,1536]{1,0:T(1,128)S(1)} %broadcast_in_dim.3.gain_ref, f32[128,768]{1,0:T(8,128)S(1)} %get-tuple-element.109.state_ref, f32[2048,256]{1,0:T(8,128)S(1)} %get-tuple-element.110.refs_0_, ...), custom_call_target="tpu_custom_call" | custom-call | tf_op jit(solution)/shard_map/own_output/pallas_call | solution.py:386
  54.7 0.0 collective-permute-done.13.state_ref
  54.7 3.8 %output.1 = bf16[2048,1536]{1,0:T(8,128)(2,1)} custom-call(s32[4]{0:T(128)S(1)} %pad_add_fusion.place, bf16[2048,128]{1,0:T(8,128)(2,1)S(1)} %copy-done, f32[1,1536]{1,0:T(1,128)S(1)} %broadcast_in_dim.3.gain_ref, f32[128,768]{1,0:T(8,128)S(1)} %collective-permute-done.13.state_ref, bf16[2048,768]{1,0:T(8,128)(2,1)S(1)} %own_output.1.own, ...), custom_call_target="tpu_custom_call" | custom-call | tf_op jit(solution)/shard_map/output/pallas_call | solution.py:419
  (1 shorter events, 0.0 us)
Async XLA Ops:
  0.1 0.9 %copy-start.2 = (f32[24,2048]{1,0:T(8,128)S(1)}, f32[24,2048]{1,0:T(8,128)}, u32[]{:S(2)}) copy-start(f32[24,2048]{1,0:T(8,128)} %decay_ref.1) | copy-start | bytes 589828
  1.0 3.6 %copy-start.1 = (bf16[2048,128]{1,0:T(8,128)(2,1)S(1)}, bf16[2048,128]{1,0:T(8,128)(2,1)}, u32[]{:S(2)}) copy-start(bf16[2048,128]{1,0:T(8,128)(2,1)} %b_ref.1) | copy-start | bytes 1572868
  6.6 8.6 %copy-start = (bf16[2048,128]{1,0:T(8,128)(2,1)S(1)}, bf16[2048,128]{1,0:T(8,128)(2,1)}, u32[]{:S(2)}) copy-start(bf16[2048,128]{1,0:T(8,128)(2,1)} %c_ref.5) | copy-start | bytes 1572868
  6.6 8.5 %copy-start.3 = (f32[24,2048]{1,0:T(8,128)S(1)}, f32[24,2048]{1,0:T(8,128)}, u32[]{:S(2)}) copy-start(f32[24,2048]{1,0:T(8,128)} %decay_ref.1) | copy-start | bytes 589828
  6.7 3.5 %collective-permute-start = (f32[136,768]{1,0:T(8,128)S(1)}, f32[136,768]{1,0:T(8,128)S(1)}, u32[]{:S(2)}, u32[]{:S(2)}) collective-permute-start(f32[136,768]{1,0:T(8,128)S(1)} %end_state.3), channel_id=1, source_target_pairs={{0,1},{1,0},{2,3},{3,2},{4,5},{5,4},{6,7},{7,6},{8,9},{9,8},{10,11... | collective-permute-start | bytes 1253384 | tf_op jit(solution)/shard_map/ppermute | solution.py:448
  10.8 9.3 %collective-permute-start.1 = (f32[25,8,128]{2,1,0:T(8,128)S(1)}, f32[25,8,128]{2,1,0:T(8,128)S(1)}, u32[]{:S(2)}, u32[]{:S(2)}) collective-permute-start(f32[25,8,128]{2,1,0:T(8,128)S(1)} %get-tuple-element.71), channel_id=1, source_target_pairs={{0,2},{1,3},{2,4},{3,5},{4,6},{5,7},{6,0},{7,1},{8,10},{9,11},{10,... | collective-permute-start | bytes 307208 | tf_op jit(solution)/shard_map/ppermute | solution.py:448
  12.2 8.0 %collective-permute-start.2 = (f32[25,8,128]{2,1,0:T(8,128)S(1)}, f32[25,8,128]{2,1,0:T(8,128)S(1)}, u32[]{:S(2)}, u32[]{:S(2)}) collective-permute-start(f32[25,8,128]{2,1,0:T(8,128)S(1)} %get-tuple-element.72), channel_id=1, source_target_pairs={{0,6},{1,7},{2,0},{3,1},{4,2},{5,3},{6,4},{7,5},{8,14},{9,15},{10,... | collective-permute-start | bytes 307208 | tf_op jit(solution)/shard_map/ppermute | solution.py:448
  13.6 4.4 %copy-start.4 = (f32[24]{0:T(128)S(1)}, f32[24]{0:T(128)}, u32[]{:S(2)}) copy-start(f32[24]{0:T(128)} %skip_ref.11) | copy-start | bytes 292
  13.6 6.6 %collective-permute-start.3 = (f32[25,8,128]{2,1,0:T(8,128)S(1)}, f32[25,8,128]{2,1,0:T(8,128)S(1)}, u32[]{:S(2)}, u32[]{:S(2)}) collective-permute-start(f32[25,8,128]{2,1,0:T(8,128)S(1)} %get-tuple-element.73), channel_id=1, source_target_pairs={{0,4},{1,5},{2,6},{3,7},{4,0},{5,1},{6,2},{7,3},{8,12},{9,13},{10,... | collective-permute-start | bytes 307208 | tf_op jit(solution)/shard_map/ppermute | solution.py:448
  20.8 8.7 %collective-permute-start.4 = (f32[25,8,128]{2,1,0:T(8,128)S(1)}, f32[25,8,128]{2,1,0:T(8,128)S(1)}, u32[]{:S(2)}, u32[]{:S(2)}) collective-permute-start(f32[25,8,128]{2,1,0:T(8,128)S(1)} %line.1.v0), channel_id=1, source_target_pairs={{0,8},{1,9},{2,10},{3,11},{4,12},{5,13},{6,14},{7,15},{8,16},{9,17... | collective-permute-start | bytes 307208 | tf_op jit(solution)/shard_map/ppermute | solution.py:448
  22.2 7.3 %collective-permute-start.5 = (f32[25,8,128]{2,1,0:T(8,128)S(1)}, f32[25,8,128]{2,1,0:T(8,128)S(1)}, u32[]{:S(2)}, u32[]{:S(2)}) collective-permute-start(f32[25,8,128]{2,1,0:T(8,128)S(1)} %line.1.v0), channel_id=1, source_target_pairs={{0,24},{1,25},{2,26},{3,27},{4,28},{5,29},{6,30},{7,31},{8,0},{9,1... | collective-permute-start | bytes 307208 | tf_op jit(solution)/shard_map/ppermute | solution.py:448
  23.7 5.8 %collective-permute-start.6 = (f32[25,8,128]{2,1,0:T(8,128)S(1)}, f32[25,8,128]{2,1,0:T(8,128)S(1)}, u32[]{:S(2)}, u32[]{:S(2)}) collective-permute-start(f32[25,8,128]{2,1,0:T(8,128)S(1)} %line.1.v0), channel_id=1, source_target_pairs={{0,16},{1,17},{2,18},{3,19},{4,20},{5,21},{6,22},{7,23},{8,24},{9,... | collective-permute-start | bytes 307208 | tf_op jit(solution)/shard_map/ppermute | solution.py:448
  30.2 9.4 %collective-permute-start.7 = (f32[25,8,128]{2,1,0:T(8,128)S(1)}, f32[25,8,128]{2,1,0:T(8,128)S(1)}, u32[]{:S(2)}, u32[]{:S(2)}) collective-permute-start(f32[25,8,128]{2,1,0:T(8,128)S(1)} %get-tuple-element.91.w0), channel_id=1, source_target_pairs={{0,32},{1,33},{2,34},{3,35},{4,36},{5,37},{6,38},{7,39},{8,40},{9,... | collective-permute-start | bytes 307208 | tf_op jit(solution)/shard_map/ppermute | solution.py:448
  31.9 7.7 %collective-permute-start.8 = (f32[25,8,128]{2,1,0:T(8,128)S(1)}, f32[25,8,128]{2,1,0:T(8,128)S(1)}, u32[]{:S(2)}, u32[]{:S(2)}) collective-permute-start(f32[25,8,128]{2,1,0:T(8,128)S(1)} %get-tuple-element.91.w0), channel_id=1, source_target_pairs={{0,96},{1,97},{2,98},{3,99},{4,100},{5,101},{6,102},{7,103},{8,104... | collective-permute-start | bytes 307208 | tf_op jit(solution)/shard_map/ppermute | solution.py:448
  34.1 5.8 %collective-permute-start.9 = (f32[25,8,128]{2,1,0:T(8,128)S(1)}, f32[25,8,128]{2,1,0:T(8,128)S(1)}, u32[]{:S(2)}, u32[]{:S(2)}) collective-permute-start(f32[25,8,128]{2,1,0:T(8,128)S(1)} %get-tuple-element.91.w0), channel_id=1, source_target_pairs={{0,64},{1,65},{2,66},{3,67},{4,68},{5,69},{6,70},{7,71},{8,72},{9,... | collective-permute-start | bytes 307208 | tf_op jit(solution)/shard_map/ppermute | solution.py:448
  40.8 6.3 %collective-permute-start.10 = (f32[32,768]{1,0:T(8,128)S(1)}, f32[32,768]{1,0:T(8,128)S(1)}, u32[]{:S(2)}, u32[]{:S(2)}) collective-permute-start(f32[32,768]{1,0:T(8,128)S(1)} %get-tuple-element.101), channel_id=1, source_target_pairs={{0,4},{1,5},{2,6},{3,7},{4,0},{5,1},{6,2},{7,3},{8,12},{9,13},{10,... | collective-permute-start | bytes 294920 | tf_op jit(solution)/shard_map/ppermute | solution.py:448
  42.4 4.8 %collective-permute-start.11 = (f32[32,768]{1,0:T(8,128)S(1)}, f32[32,768]{1,0:T(8,128)S(1)}, u32[]{:S(2)}, u32[]{:S(2)}) collective-permute-start(f32[32,768]{1,0:T(8,128)S(1)} %get-tuple-element.102), channel_id=1, source_target_pairs={{0,2},{1,3},{2,4},{3,5},{4,6},{5,7},{6,0},{7,1},{8,10},{9,11},{10,... | collective-permute-start | bytes 294920 | tf_op jit(solution)/shard_map/ppermute | solution.py:448
  42.4 9.4 %copy-start.5 = (f32[1536]{0:T(1024)S(1)}, f32[1536]{0:T(1024)}, u32[]{:S(2)}) copy-start(f32[1536]{0:T(1024)} %param.13) | copy-start | bytes 18436
  42.4 5.3 %collective-permute-start.12 = (f32[32,768]{1,0:T(8,128)S(1)}, f32[32,768]{1,0:T(8,128)S(1)}, u32[]{:S(2)}, u32[]{:S(2)}) collective-permute-start(f32[32,768]{1,0:T(8,128)S(1)} %get-tuple-element.103), channel_id=1, source_target_pairs={{0,6},{1,7},{2,0},{3,1},{4,2},{5,3},{6,4},{7,5},{8,14},{9,15},{10,... | collective-permute-start | bytes 294920 | tf_op jit(solution)/shard_map/ppermute | solution.py:448
  48.3 6.4 %collective-permute-start.13 = (f32[128,768]{1,0:T(8,128)S(1)}, f32[128,768]{1,0:T(8,128)S(1)}, u32[]{:S(2)}, u32[]{:S(2)}) collective-permute-start(f32[128,768]{1,0:T(8,128)S(1)} %get-tuple-element.116), channel_id=1, source_target_pairs={{0,1},{1,0},{2,3},{3,2},{4,5},{5,4},{6,7},{7,6},{8,9},{9,8},{10,11... | collective-permute-start | bytes 1179656 | tf_op jit(solution)/shard_map/ppermute | solution.py:448

commit v7 on v6

--- a/solution.py
+++ b/solution.py
@@ -372,22 +372,33 @@
 
 def own_output_kernel(place, c_ref, gain_ref, state_ref, *refs):
     groups = HALF // GROUP
-    out = refs[-1]
+    out_hbm, out, sems = refs[-3:]
     start = place[CORE] * HALF
-    for i in range(out.shape[0] // OUT_STEP):
+    lanes = pl.ds(pl.multiple_of(start, HALF), HALF)
+    steps = out.shape[0] // OUT_STEP
+    copies = []
+    for i in range(steps):
         rows = slice(i * OUT_STEP, (i + 1) * OUT_STEP)
         finish(start, c_ref, gain_ref, state_ref, refs[:groups], refs[groups : 2 * groups], out, rows)
+        if i < steps // 2:
+            where = pl.ds(i * OUT_STEP, OUT_STEP)
+            copies.append(pltpu.make_async_copy(out.at[where], out_hbm.at[where, lanes], sems.at[i]))
+            copies[-1].start()
+    for copy in copies:
+        copy.wait()
 
 
 def own_output(place, c, gain, state, parts):
+    tokens = c.shape[0]
     sums, weights = zip(*parts, strict=True)
     args = (place, c, gain, state, *sums, *weights)
     vmem = pl.BlockSpec(memory_space=pltpu.VMEM)
     return pl.pallas_call(
         own_output_kernel,
         in_specs=[pl.BlockSpec(memory_space=pltpu.SMEM)] + [vmem] * (len(args) - 1),
-        out_specs=vmem,
-        out_shape=jax.ShapeDtypeStruct((c.shape[0], HALF), BF16),
+        out_specs=[pl.BlockSpec(memory_space=pl.ANY), vmem],
+        out_shape=[jax.ShapeDtypeStruct((tokens, WIDTH), BF16), jax.ShapeDtypeStruct((tokens, HALF), BF16)],
+        scratch_shapes=[pltpu.SemaphoreType.DMA((tokens // OUT_STEP // 2,))],
         name="own_output",
         compiler_params=pltpu.CompilerParams(vmem_limit_bytes=LIMIT),
     )(*args)
@@ -399,7 +410,8 @@
     start = (1 - place[CORE]) * HALF
     own_lanes = pl.ds(pl.multiple_of(place[CORE] * HALF, HALF), HALF)
     lanes = pl.ds(pl.multiple_of(start, HALF), HALF)
-    copies = [pltpu.make_async_copy(own, out_hbm.at[:, own_lanes], own_sem)]
+    rest = pl.ds(own.shape[0] // 2, own.shape[0] // 2)
+    copies = [pltpu.make_async_copy(own.at[rest], out_hbm.at[rest, own_lanes], own_sem)]
     copies[0].start()
     for i in range(out.shape[0] // OUT_STEP):
         rows = slice(i * OUT_STEP, (i + 1) * OUT_STEP)
@@ -411,15 +423,16 @@
         copy.wait()
 
 
-def output(place, c, gain, state, own, parts):
+def output(place, c, gain, state, own, parts, begun):
     tokens = c.shape[0]
     sums, weights = zip(*parts, strict=True)
     args = (place, c, gain, state, own, *sums, *weights)
     vmem = pl.BlockSpec(memory_space=pltpu.VMEM)
     return pl.pallas_call(
         output_kernel,
-        in_specs=[pl.BlockSpec(memory_space=pltpu.SMEM)] + [vmem] * (len(args) - 1),
+        in_specs=[pl.BlockSpec(memory_space=pltpu.SMEM)] + [vmem] * (len(args) - 1) + [pl.BlockSpec(memory_space=pl.ANY)],
         out_specs=pl.BlockSpec(memory_space=pl.ANY),
+        input_output_aliases={len(args): 0},
         out_shape=jax.ShapeDtypeStruct((tokens, WIDTH), BF16),
         scratch_shapes=[
             pltpu.VMEM((tokens, HALF), BF16),
@@ -428,7 +441,7 @@
         ],
         name="output",
         compiler_params=pltpu.CompilerParams(vmem_limit_bytes=LIMIT),
-    )(*args)
+    )(*args, begun)
 
 
 def device_of(z, y, x, core):
@@ -483,9 +496,9 @@
     other = moved(send, CORE, 1)
     half = len(parts) // 2
     gain = norm_gain[None]
-    own = own_output(place, c, gain, own, parts[:half])
+    begun, own = own_output(place, c, gain, own, parts[:half])
     own, other = lax.optimization_barrier((own, other))
-    return output(place, c, gain, other, own, parts[half:])
+    return output(place, c, gain, other, own, parts[half:], begun)
 
 
 def solution(mesh):

time: 58.9 us -> 58.9 us (level)
  no operation moved by 1% of the time
where the time goes in v7:
time: 58.9 us; the launch traced here: 58.8 us
  Pallas kernels  33.4 us (57%)
  starting transfers between devices  23.1 us (39%)
  local copies, waits for them, and re-layouts  0.96 us (2%)
  waiting for transfers between devices  0.87 us (1%)
    ppermute x14, starting transfers between devices, moved(): return lax.ppermute(value, ('grp', 'dev'), pairs)  23.1 us
    pallas_call x6, Pallas kernels, local(): pl.pallas_call(functools.partial(local_kernel, part), in_specs=[pl.BlockS...  12.6 us
    pallas_call x2, Pallas kernels, end_state(): pl.pallas_call(functools.partial(state_kernel, mine), in_specs=[pl.BlockS...  4.07 us
    pallas_call x1, Pallas kernels, output(): pl.pallas_call(output_kernel, in_specs=[pl.BlockSpec(memory_space=pltpu.S...  3.8 us
    pallas_call x1, Pallas kernels, decay_factors(): pl.pallas_call(factors_kernel, in_specs=[pl.BlockSpec(memory_space=pltpu....  3.56 us
    pallas_call x5, Pallas kernels, small_call(): pl.pallas_call(kernel, in_specs=[pl.BlockSpec(memory_space=pltpu.SMEM)] +...  3.49 us
    pallas_call x1, Pallas kernels, own_output(): pl.pallas_call(own_output_kernel, in_specs=[pl.BlockSpec(memory_space=plt...  3.01 us
    pallas_call x1, Pallas kernels, prepare(): pl.pallas_call(prepare_kernel, in_specs=[pl.BlockSpec(memory_space=pltpu....  2.8 us
  transfers between devices with their start and end apart: 14, of which 2 were waited for; matrix products, arithmetic and copies ran while one was open for 0% of the time, Pallas kernels for 35%

profile of v7, /device:TPU:1, one launch (start us, length us, event | category | flops | bytes accessed | tf_op | source)
XLA Modules:
  0.0 58.8 jit_solution(14573155755328274737)
XLA Ops:
  0.0 0.1 pad_add_fusion.place
  0.1 0.0 copy-start.2
  0.1 0.9 %copy-done.2 = f32[24,2048]{1,0:T(8,128)S(1)} copy-done((f32[24,2048]{1,0:T(8,128)S(1)}, f32[24,2048]{1,0:T(8,128)}, u32[]{:S(2)}) %copy-start.2) | copy-done | bytes 196632
  1.0 0.0 copy-start
  1.0 3.6 %decay_factors.1 = (bf16[2048,768]{1,0:T(8,128)(2,1)S(1)}, bf16[2048,768]{1,0:T(8,128)(2,1)S(1)}, bf16[2064,72]{1,0:T(8,128)(2,1)S(1)}) custom-call(s32[4]{0:T(128)S(1)} %pad_add_fusion.place, bf16[2048,1536]{1,0:T(8,128)(2,1)} %x_hbm.1, f32[24,2048]{1,0:T(8,128)S(1)} %copy-done.2), custom_call_target="tpu_custom_call" | custom-call | tf_op jit(solution)/shard_map/decay_factors/pallas_call | solution.py:102
  4.6 0.0 copy-done
  4.6 2.0 %end_state.3 = f32[136,768]{1,0:T(8,128)S(1)} custom-call(s32[4]{0:T(128)S(1)} %pad_add_fusion.place, bf16[2048,768]{1,0:T(8,128)(2,1)S(1)} %get-tuple-element.69.x.x_ref, bf16[2048,128]{1,0:T(8,128)(2,1)S(1)} %copy-done, bf16[2064,72]{1,0:T(8,128)(2,1)S(1)} %get-tuple-element.68.factors), custom_call_target="tpu_custom_call" | custom-call | tf_op jit(solution)/shard_map/end_state/pallas_call | solution.py:133
  6.6 0.0 copy-start.1
  6.6 0.0 copy-start.3
  6.7 1.5 %collective-permute-start = (f32[136,768]{1,0:T(8,128)S(1)}, f32[136,768]{1,0:T(8,128)S(1)}, u32[]{:S(2)}, u32[]{:S(2)}) collective-permute-start(f32[136,768]{1,0:T(8,128)S(1)} %end_state.3), channel_id=1, source_target_pairs={{0,1},{1,0},{2,3},{3,2},{4,5},{5,4},{6,7},{7,6},{8,9},{9,8},{10,11... | collective-permute-start | bytes 1253384 | tf_op jit(solution)/shard_map/ppermute | solution.py:461
  8.2 2.0 %end_state.2.keep = f32[136,768]{1,0:T(8,128)S(1)} custom-call(s32[4]{0:T(128)S(1)} %pad_add_fusion.place, bf16[2048,768]{1,0:T(8,128)(2,1)S(1)} %get-tuple-element.67.x.x_ref, bf16[2048,128]{1,0:T(8,128)(2,1)S(1)} %copy-done, bf16[2064,72]{1,0:T(8,128)(2,1)S(1)} %get-tuple-element.68.factors), custom_call_target="tpu_custom_call" | custom-call | tf_op jit(solution)/shard_map/end_state/pallas_call | solution.py:133
  10.2 0.0 collective-permute-done.recv
  10.2 0.6 %pair.1 = (f32[25,8,128]{2,1,0:T(8,128)S(1)}, f32[25,8,128]{2,1,0:T(8,128)S(1)}, f32[25,8,128]{2,1,0:T(8,128)S(1)}, f32[25,8,128]{2,1,0:T(8,128)S(1)}) custom-call(s32[4]{0:T(128)S(1)} %pad_add_fusion.place, f32[136,768]{1,0:T(8,128)S(1)} %end_state.2.keep, f32[136,768]{1,0:T(8,128)S(1)} %collective-permute-done.recv), custom_call_target="tpu_custom_call" | custom-call | tf_op jit(solution)/shard_map/pair/pallas_call | solution.py:146
  10.8 1.4 %collective-permute-start.1 = (f32[25,8,128]{2,1,0:T(8,128)S(1)}, f32[25,8,128]{2,1,0:T(8,128)S(1)}, u32[]{:S(2)}, u32[]{:S(2)}) collective-permute-start(f32[25,8,128]{2,1,0:T(8,128)S(1)} %get-tuple-element.73), channel_id=1, source_target_pairs={{0,2},{1,3},{2,4},{3,5},{4,6},{5,7},{6,0},{7,1},{8,10},{9,11},{10,... | collective-permute-start | bytes 307208 | tf_op jit(solution)/shard_map/ppermute | solution.py:461
  12.2 1.4 %collective-permute-start.2 = (f32[25,8,128]{2,1,0:T(8,128)S(1)}, f32[25,8,128]{2,1,0:T(8,128)S(1)}, u32[]{:S(2)}, u32[]{:S(2)}) collective-permute-start(f32[25,8,128]{2,1,0:T(8,128)S(1)} %get-tuple-element.74), channel_id=1, source_target_pairs={{0,6},{1,7},{2,0},{3,1},{4,2},{5,3},{6,4},{7,5},{8,14},{9,15},{10,... | collective-permute-start | bytes 307208 | tf_op jit(solution)/shard_map/ppermute | solution.py:461
  13.6 0.0 copy-start.4
  13.6 1.6 %collective-permute-start.3 = (f32[25,8,128]{2,1,0:T(8,128)S(1)}, f32[25,8,128]{2,1,0:T(8,128)S(1)}, u32[]{:S(2)}, u32[]{:S(2)}) collective-permute-start(f32[25,8,128]{2,1,0:T(8,128)S(1)} %get-tuple-element.75), channel_id=1, source_target_pairs={{0,4},{1,5},{2,6},{3,7},{4,0},{5,1},{6,2},{7,3},{8,12},{9,13},{10,... | collective-permute-start | bytes 307208 | tf_op jit(solution)/shard_map/ppermute | solution.py:461
  15.2 0.0 copy-done.1
  15.2 0.0 copy-done.3
  15.2 2.8 %prepare.1 = (bf16[2048,1536]{1,0:T(8,128)(2,1)S(1)}, bf16[2048,256]{1,0:T(8,128)(2,1)S(1)}, bf16[2048,128]{1,0:T(8,128)(2,1)S(1)}, bf16[2304,72]{1,0:T(8,128)(2,1)S(1)}, bf16[2048,72]{1,0:T(8,128)(2,1)S(1)}) custom-call(bf16[2048,1536]{1,0:T(8,128)(2,1)} %gate_hbm.1, bf16[2048,128]{1,0:T(8,128)(2,1)S(1)} %copy-done, bf16[2048,128]{1,0:T(8,128)(2,1)S(1)} %copy-done.1, ...), custom_call_target="tpu_custom_call" | custom-call | tf_op jit(solution)/shard_map/prepare/pallas_call | solution.py:293
  18.0 0.0 copy-done.4
  18.0 2.1 %local.6 = (f32[2048,256]{1,0:T(8,128)S(1)}, bf16[2048,256]{1,0:T(8,128)(2,1)S(1)}) custom-call(s32[4]{0:T(128)S(1)} %pad_add_fusion.place, f32[24]{0:T(128)S(1)} %copy-done.4, bf16[2048,768]{1,0:T(8,128)(2,1)S(1)} %get-tuple-element.67.x.x_ref, bf16[2048,1536]{1,0:T(8,128)(2,1)S(1)} %get-tuple-element.76.gate_ref, ...), custom_call_target="tpu_custom_call" | custom-call | tf_op jit(solution)/shard_map/local/pallas_call | solution.py:350
  20.1 0.0 collective-permute-done.1.u1
  20.2 0.0 collective-permute-done.2.u3
  20.2 0.0 collective-permute-done.3.u2
  20.2 0.6 %line.1.v0 = f32[25,8,128]{2,1,0:T(8,128)S(1)} custom-call(s32[4]{0:T(128)S(1)} %pad_add_fusion.place, f32[25,8,128]{2,1,0:T(8,128)S(1)} %get-tuple-element.72.u0, f32[25,8,128]{2,1,0:T(8,128)S(1)} %collective-permute-done.1.u1, f32[25,8,128]{2,1,0:T(8,128)S(1)} %collective-permute-done.3.u2, f32[25,8,128]{2,1,0:T(8,128)S(1)} %collective-permute-done.2.u3), custom_call_target="tpu_custom_call" | custom-call | tf_op jit(solution)/shard_map/line/pallas_call | solution.py:146
  20.8 1.4 %collective-permute-start.4 = (f32[25,8,128]{2,1,0:T(8,128)S(1)}, f32[25,8,128]{2,1,0:T(8,128)S(1)}, u32[]{:S(2)}, u32[]{:S(2)}) collective-permute-start(f32[25,8,128]{2,1,0:T(8,128)S(1)} %line.1.v0), channel_id=1, source_target_pairs={{0,8},{1,9},{2,10},{3,11},{4,12},{5,13},{6,14},{7,15},{8,16},{9,17... | collective-permute-start | bytes 307208 | tf_op jit(solution)/shard_map/ppermute | solution.py:461
  22.2 1.5 %collective-permute-start.5 = (f32[25,8,128]{2,1,0:T(8,128)S(1)}, f32[25,8,128]{2,1,0:T(8,128)S(1)}, u32[]{:S(2)}, u32[]{:S(2)}) collective-permute-start(f32[25,8,128]{2,1,0:T(8,128)S(1)} %line.1.v0), channel_id=1, source_target_pairs={{0,24},{1,25},{2,26},{3,27},{4,28},{5,29},{6,30},{7,31},{8,0},{9,1... | collective-permute-start | bytes 307208 | tf_op jit(solution)/shard_map/ppermute | solution.py:461
  23.7 1.6 %collective-permute-start.6 = (f32[25,8,128]{2,1,0:T(8,128)S(1)}, f32[25,8,128]{2,1,0:T(8,128)S(1)}, u32[]{:S(2)}, u32[]{:S(2)}) collective-permute-start(f32[25,8,128]{2,1,0:T(8,128)S(1)} %line.1.v0), channel_id=1, source_target_pairs={{0,16},{1,17},{2,18},{3,19},{4,20},{5,21},{6,22},{7,23},{8,24},{9,... | collective-permute-start | bytes 307208 | tf_op jit(solution)/shard_map/ppermute | solution.py:461
  25.3 2.1 %local.7 = (f32[2048,256]{1,0:T(8,128)S(1)}, bf16[2048,256]{1,0:T(8,128)(2,1)S(1)}) custom-call(s32[4]{0:T(128)S(1)} %pad_add_fusion.place, f32[24]{0:T(128)S(1)} %copy-done.4, bf16[2048,768]{1,0:T(8,128)(2,1)S(1)} %get-tuple-element.67.x.x_ref, bf16[2048,1536]{1,0:T(8,128)(2,1)S(1)} %get-tuple-element.76.gate_ref, ...), custom_call_target="tpu_custom_call" | custom-call | tf_op jit(solution)/shard_map/local/pallas_call | solution.py:350
  27.4 2.1 %local.8 = (f32[2048,256]{1,0:T(8,128)S(1)}, bf16[2048,256]{1,0:T(8,128)(2,1)S(1)}) custom-call(s32[4]{0:T(128)S(1)} %pad_add_fusion.place, f32[24]{0:T(128)S(1)} %copy-done.4, bf16[2048,768]{1,0:T(8,128)(2,1)S(1)} %get-tuple-element.67.x.x_ref, bf16[2048,1536]{1,0:T(8,128)(2,1)S(1)} %get-tuple-element.76.gate_ref, ...), custom_call_target="tpu_custom_call" | custom-call | tf_op jit(solution)/shard_map/local/pallas_call | solution.py:350
  29.5 0.0 collective-permute-done.4.v1
  29.5 0.0 collective-permute-done.5.v3
  29.5 0.0 collective-permute-done.6.v2
  29.5 0.7 %plane.1 = (f32[25,8,128]{2,1,0:T(8,128)S(1)}, f32[25,8,128]{2,1,0:T(8,128)S(1)}) custom-call(s32[4]{0:T(128)S(1)} %pad_add_fusion.place, f32[25,8,128]{2,1,0:T(8,128)S(1)} %line.1.v0, f32[25,8,128]{2,1,0:T(8,128)S(1)} %collective-permute-done.4.v1, f32[25,8,128]{2,1,0:T(8,128)S(1)} %collective-permute-done.6.v2, f32[25,8,128]{2,1,0:T(8,128)S(1)} %collective-permute-done.5.v3), custom_call_target="tpu_custom_call" | custom-call | tf_op jit(solution)/shard_map/plane/pallas_call | solution.py:146
  30.2 1.7 %collective-permute-start.7 = (f32[25,8,128]{2,1,0:T(8,128)S(1)}, f32[25,8,128]{2,1,0:T(8,128)S(1)}, u32[]{:S(2)}, u32[]{:S(2)}) collective-permute-start(f32[25,8,128]{2,1,0:T(8,128)S(1)} %get-tuple-element.93.w0), channel_id=1, source_target_pairs={{0,32},{1,33},{2,34},{3,35},{4,36},{5,37},{6,38},{7,39},{8,40},{9,... | collective-permute-start | bytes 307208 | tf_op jit(solution)/shard_map/ppermute | solution.py:461
  31.9 2.2 %collective-permute-start.8 = (f32[25,8,128]{2,1,0:T(8,128)S(1)}, f32[25,8,128]{2,1,0:T(8,128)S(1)}, u32[]{:S(2)}, u32[]{:S(2)}) collective-permute-start(f32[25,8,128]{2,1,0:T(8,128)S(1)} %get-tuple-element.93.w0), channel_id=1, source_target_pairs={{0,96},{1,97},{2,98},{3,99},{4,100},{5,101},{6,102},{7,103},{8,104... | collective-permute-start | bytes 307208 | tf_op jit(solution)/shard_map/ppermute | solution.py:461
  34.1 1.2 %collective-permute-start.9 = (f32[25,8,128]{2,1,0:T(8,128)S(1)}, f32[25,8,128]{2,1,0:T(8,128)S(1)}, u32[]{:S(2)}, u32[]{:S(2)}) collective-permute-start(f32[25,8,128]{2,1,0:T(8,128)S(1)} %get-tuple-element.93.w0), channel_id=1, source_target_pairs={{0,64},{1,65},{2,66},{3,67},{4,68},{5,69},{6,70},{7,71},{8,72},{9,... | collective-permute-start | bytes 307208 | tf_op jit(solution)/shard_map/ppermute | solution.py:461
  35.3 2.1 %local.9 = (f32[2048,256]{1,0:T(8,128)S(1)}, bf16[2048,256]{1,0:T(8,128)(2,1)S(1)}) custom-call(s32[4]{0:T(128)S(1)} %pad_add_fusion.place, f32[24]{0:T(128)S(1)} %copy-done.4, bf16[2048,768]{1,0:T(8,128)(2,1)S(1)} %get-tuple-element.69.x.x_ref, bf16[2048,1536]{1,0:T(8,128)(2,1)S(1)} %get-tuple-element.76.gate_ref, ...), custom_call_target="tpu_custom_call" | custom-call | tf_op jit(solution)/shard_map/local/pallas_call | solution.py:350
  37.4 2.1 %local.10 = (f32[2048,256]{1,0:T(8,128)S(1)}, bf16[2048,256]{1,0:T(8,128)(2,1)S(1)}) custom-call(s32[4]{0:T(128)S(1)} %pad_add_fusion.place, f32[24]{0:T(128)S(1)} %copy-done.4, bf16[2048,768]{1,0:T(8,128)(2,1)S(1)} %get-tuple-element.69.x.x_ref, bf16[2048,1536]{1,0:T(8,128)(2,1)S(1)} %get-tuple-element.76.gate_ref, ...), custom_call_target="tpu_custom_call" | custom-call | tf_op jit(solution)/shard_map/local/pallas_call | solution.py:350
  39.6 0.0 collective-permute-done.7.w1
  39.6 0.0 collective-permute-done.8.w3
  39.6 0.4 collective-permute-done.9.w2
  39.9 0.9 %enter.1 = (f32[32,768]{1,0:T(8,128)S(1)}, f32[32,768]{1,0:T(8,128)S(1)}, f32[32,768]{1,0:T(8,128)S(1)}, f32[32,768]{1,0:T(8,128)S(1)}) custom-call(s32[4]{0:T(128)S(1)} %pad_add_fusion.place, f32[25,8,128]{2,1,0:T(8,128)S(1)} %get-tuple-element.93.w0, f32[25,8,128]{2,1,0:T(8,128)S(1)} %collective-permute-done.7.w1, ...), custom_call_target="tpu_custom_call" | custom-call | tf_op jit(solution)/shard_map/enter/pallas_call | solution.py:146
  40.8 1.5 %collective-permute-start.10 = (f32[32,768]{1,0:T(8,128)S(1)}, f32[32,768]{1,0:T(8,128)S(1)}, u32[]{:S(2)}, u32[]{:S(2)}) collective-permute-start(f32[32,768]{1,0:T(8,128)S(1)} %get-tuple-element.103), channel_id=1, source_target_pairs={{0,4},{1,5},{2,6},{3,7},{4,0},{5,1},{6,2},{7,3},{8,12},{9,13},{10,... | collective-permute-start | bytes 294920 | tf_op jit(solution)/shard_map/ppermute | solution.py:461
  42.4 0.0 collective-permute-start.11
  42.4 0.0 copy-start.5
  42.4 2.7 %collective-permute-start.12 = (f32[32,768]{1,0:T(8,128)S(1)}, f32[32,768]{1,0:T(8,128)S(1)}, u32[]{:S(2)}, u32[]{:S(2)}) collective-permute-start(f32[32,768]{1,0:T(8,128)S(1)} %get-tuple-element.105), channel_id=1, source_target_pairs={{0,6},{1,7},{2,0},{3,1},{4,2},{5,3},{6,4},{7,5},{8,14},{9,15},{10,... | collective-permute-start | bytes 294920 | tf_op jit(solution)/shard_map/ppermute | solution.py:461
  45.0 2.1 %local.11 = (f32[2048,256]{1,0:T(8,128)S(1)}, bf16[2048,256]{1,0:T(8,128)(2,1)S(1)}) custom-call(s32[4]{0:T(128)S(1)} %pad_add_fusion.place, f32[24]{0:T(128)S(1)} %copy-done.4, bf16[2048,768]{1,0:T(8,128)(2,1)S(1)} %get-tuple-element.69.x.x_ref, bf16[2048,1536]{1,0:T(8,128)(2,1)S(1)} %get-tuple-element.76.gate_ref, ...), custom_call_target="tpu_custom_call" | custom-call | tf_op jit(solution)/shard_map/local/pallas_call | solution.py:350
  47.2 0.0 collective-permute-done.10.e2
  47.2 0.0 collective-permute-done.11.e1
  47.2 0.5 collective-permute-done.12.e3
  47.7 0.7 %chip.1 = (f32[128,768]{1,0:T(8,128)S(1)}, f32[128,768]{1,0:T(8,128)S(1)}) custom-call(s32[4]{0:T(128)S(1)} %pad_add_fusion.place, f32[32,768]{1,0:T(8,128)S(1)} %get-tuple-element.102.e0, f32[32,768]{1,0:T(8,128)S(1)} %collective-permute-done.11.e1, f32[32,768]{1,0:T(8,128)S(1)} %collective-permute-done.10.e2, f32[32,768]{1,0:T(8,128)S(1)} %collective-permute-done.12.e3, ...), custom_call_target="tpu_custom_call" | custom-call | tf_op jit(solution)/shard_map/chip/pallas_call | solution.py:146
  48.3 3.4 %collective-permute-start.13 = (f32[128,768]{1,0:T(8,128)S(1)}, f32[128,768]{1,0:T(8,128)S(1)}, u32[]{:S(2)}, u32[]{:S(2)}) collective-permute-start(f32[128,768]{1,0:T(8,128)S(1)} %get-tuple-element.119), channel_id=1, source_target_pairs={{0,1},{1,0},{2,3},{3,2},{4,5},{5,4},{6,7},{7,6},{8,9},{9,8},{10,11... | collective-permute-start | bytes 1179656 | tf_op jit(solution)/shard_map/ppermute | solution.py:461
  51.8 0.0 copy-done.5
  51.8 3.0 %own_output.1 = (bf16[2048,1536]{1,0:T(8,128)(2,1)}, bf16[2048,768]{1,0:T(8,128)(2,1)S(1)}) custom-call(s32[4]{0:T(128)S(1)} %pad_add_fusion.place, bf16[2048,128]{1,0:T(8,128)(2,1)S(1)} %copy-done.1, f32[1,1536]{1,0:T(1,128)S(1)} %broadcast_in_dim.3.gain_ref, f32[128,768]{1,0:T(8,128)S(1)} %get-tuple-element.111.state_ref, ...), custom_call_target="tpu_custom_call" | custom-call | tf_op jit(solution)/shard_map/own_output/pallas_call | solution.py:396
  54.8 0.0 collective-permute-done.13.state_ref
  54.8 3.8 %output.1 = bf16[2048,1536]{1,0:T(8,128)(2,1)} custom-call(s32[4]{0:T(128)S(1)} %pad_add_fusion.place, bf16[2048,128]{1,0:T(8,128)(2,1)S(1)} %copy-done.1, f32[1,1536]{1,0:T(1,128)S(1)} %broadcast_in_dim.3.gain_ref, f32[128,768]{1,0:T(8,128)S(1)} %collective-permute-done.13.state_ref, ...), custom_call_target="tpu_custom_call", output_to_operand_aliasing={{}: (11, {})} | custom-call | tf_op jit(solution)/shard_map/output/pallas_call | solution.py:431
  (1 shorter events, 0.0 us)
Async XLA Ops:
  0.1 0.9 %copy-start.2 = (f32[24,2048]{1,0:T(8,128)S(1)}, f32[24,2048]{1,0:T(8,128)}, u32[]{:S(2)}) copy-start(f32[24,2048]{1,0:T(8,128)} %decay_ref.1) | copy-start | bytes 589828
  1.0 3.6 %copy-start = (bf16[2048,128]{1,0:T(8,128)(2,1)S(1)}, bf16[2048,128]{1,0:T(8,128)(2,1)}, u32[]{:S(2)}) copy-start(bf16[2048,128]{1,0:T(8,128)(2,1)} %b_ref.1) | copy-start | bytes 1572868
  6.6 8.6 %copy-start.1 = (bf16[2048,128]{1,0:T(8,128)(2,1)S(1)}, bf16[2048,128]{1,0:T(8,128)(2,1)}, u32[]{:S(2)}) copy-start(bf16[2048,128]{1,0:T(8,128)(2,1)} %c_ref.5) | copy-start | bytes 1572868
  6.6 8.5 %copy-start.3 = (f32[24,2048]{1,0:T(8,128)S(1)}, f32[24,2048]{1,0:T(8,128)}, u32[]{:S(2)}) copy-start(f32[24,2048]{1,0:T(8,128)} %decay_ref.1) | copy-start | bytes 589828
  6.7 3.5 %collective-permute-start = (f32[136,768]{1,0:T(8,128)S(1)}, f32[136,768]{1,0:T(8,128)S(1)}, u32[]{:S(2)}, u32[]{:S(2)}) collective-permute-start(f32[136,768]{1,0:T(8,128)S(1)} %end_state.3), channel_id=1, source_target_pairs={{0,1},{1,0},{2,3},{3,2},{4,5},{5,4},{6,7},{7,6},{8,9},{9,8},{10,11... | collective-permute-start | bytes 1253384 | tf_op jit(solution)/shard_map/ppermute | solution.py:461
  10.8 9.3 %collective-permute-start.1 = (f32[25,8,128]{2,1,0:T(8,128)S(1)}, f32[25,8,128]{2,1,0:T(8,128)S(1)}, u32[]{:S(2)}, u32[]{:S(2)}) collective-permute-start(f32[25,8,128]{2,1,0:T(8,128)S(1)} %get-tuple-element.73), channel_id=1, source_target_pairs={{0,2},{1,3},{2,4},{3,5},{4,6},{5,7},{6,0},{7,1},{8,10},{9,11},{10,... | collective-permute-start | bytes 307208 | tf_op jit(solution)/shard_map/ppermute | solution.py:461
  12.2 8.0 %collective-permute-start.2 = (f32[25,8,128]{2,1,0:T(8,128)S(1)}, f32[25,8,128]{2,1,0:T(8,128)S(1)}, u32[]{:S(2)}, u32[]{:S(2)}) collective-permute-start(f32[25,8,128]{2,1,0:T(8,128)S(1)} %get-tuple-element.74), channel_id=1, source_target_pairs={{0,6},{1,7},{2,0},{3,1},{4,2},{5,3},{6,4},{7,5},{8,14},{9,15},{10,... | collective-permute-start | bytes 307208 | tf_op jit(solution)/shard_map/ppermute | solution.py:461
  13.6 4.4 %copy-start.4 = (f32[24]{0:T(128)S(1)}, f32[24]{0:T(128)}, u32[]{:S(2)}) copy-start(f32[24]{0:T(128)} %skip_ref.11) | copy-start | bytes 292
  13.6 6.6 %collective-permute-start.3 = (f32[25,8,128]{2,1,0:T(8,128)S(1)}, f32[25,8,128]{2,1,0:T(8,128)S(1)}, u32[]{:S(2)}, u32[]{:S(2)}) collective-permute-start(f32[25,8,128]{2,1,0:T(8,128)S(1)} %get-tuple-element.75), channel_id=1, source_target_pairs={{0,4},{1,5},{2,6},{3,7},{4,0},{5,1},{6,2},{7,3},{8,12},{9,13},{10,... | collective-permute-start | bytes 307208 | tf_op jit(solution)/shard_map/ppermute | solution.py:461
  20.8 8.7 %collective-permute-start.4 = (f32[25,8,128]{2,1,0:T(8,128)S(1)}, f32[25,8,128]{2,1,0:T(8,128)S(1)}, u32[]{:S(2)}, u32[]{:S(2)}) collective-permute-start(f32[25,8,128]{2,1,0:T(8,128)S(1)} %line.1.v0), channel_id=1, source_target_pairs={{0,8},{1,9},{2,10},{3,11},{4,12},{5,13},{6,14},{7,15},{8,16},{9,17... | collective-permute-start | bytes 307208 | tf_op jit(solution)/shard_map/ppermute | solution.py:461
  22.2 7.3 %collective-permute-start.5 = (f32[25,8,128]{2,1,0:T(8,128)S(1)}, f32[25,8,128]{2,1,0:T(8,128)S(1)}, u32[]{:S(2)}, u32[]{:S(2)}) collective-permute-start(f32[25,8,128]{2,1,0:T(8,128)S(1)} %line.1.v0), channel_id=1, source_target_pairs={{0,24},{1,25},{2,26},{3,27},{4,28},{5,29},{6,30},{7,31},{8,0},{9,1... | collective-permute-start | bytes 307208 | tf_op jit(solution)/shard_map/ppermute | solution.py:461
  23.7 5.8 %collective-permute-start.6 = (f32[25,8,128]{2,1,0:T(8,128)S(1)}, f32[25,8,128]{2,1,0:T(8,128)S(1)}, u32[]{:S(2)}, u32[]{:S(2)}) collective-permute-start(f32[25,8,128]{2,1,0:T(8,128)S(1)} %line.1.v0), channel_id=1, source_target_pairs={{0,16},{1,17},{2,18},{3,19},{4,20},{5,21},{6,22},{7,23},{8,24},{9,... | collective-permute-start | bytes 307208 | tf_op jit(solution)/shard_map/ppermute | solution.py:461
  30.2 9.4 %collective-permute-start.7 = (f32[25,8,128]{2,1,0:T(8,128)S(1)}, f32[25,8,128]{2,1,0:T(8,128)S(1)}, u32[]{:S(2)}, u32[]{:S(2)}) collective-permute-start(f32[25,8,128]{2,1,0:T(8,128)S(1)} %get-tuple-element.93.w0), channel_id=1, source_target_pairs={{0,32},{1,33},{2,34},{3,35},{4,36},{5,37},{6,38},{7,39},{8,40},{9,... | collective-permute-start | bytes 307208 | tf_op jit(solution)/shard_map/ppermute | solution.py:461
  31.9 7.7 %collective-permute-start.8 = (f32[25,8,128]{2,1,0:T(8,128)S(1)}, f32[25,8,128]{2,1,0:T(8,128)S(1)}, u32[]{:S(2)}, u32[]{:S(2)}) collective-permute-start(f32[25,8,128]{2,1,0:T(8,128)S(1)} %get-tuple-element.93.w0), channel_id=1, source_target_pairs={{0,96},{1,97},{2,98},{3,99},{4,100},{5,101},{6,102},{7,103},{8,104... | collective-permute-start | bytes 307208 | tf_op jit(solution)/shard_map/ppermute | solution.py:461
  34.1 5.8 %collective-permute-start.9 = (f32[25,8,128]{2,1,0:T(8,128)S(1)}, f32[25,8,128]{2,1,0:T(8,128)S(1)}, u32[]{:S(2)}, u32[]{:S(2)}) collective-permute-start(f32[25,8,128]{2,1,0:T(8,128)S(1)} %get-tuple-element.93.w0), channel_id=1, source_target_pairs={{0,64},{1,65},{2,66},{3,67},{4,68},{5,69},{6,70},{7,71},{8,72},{9,... | collective-permute-start | bytes 307208 | tf_op jit(solution)/shard_map/ppermute | solution.py:461
  40.8 6.3 %collective-permute-start.10 = (f32[32,768]{1,0:T(8,128)S(1)}, f32[32,768]{1,0:T(8,128)S(1)}, u32[]{:S(2)}, u32[]{:S(2)}) collective-permute-start(f32[32,768]{1,0:T(8,128)S(1)} %get-tuple-element.103), channel_id=1, source_target_pairs={{0,4},{1,5},{2,6},{3,7},{4,0},{5,1},{6,2},{7,3},{8,12},{9,13},{10,... | collective-permute-start | bytes 294920 | tf_op jit(solution)/shard_map/ppermute | solution.py:461
  42.4 4.8 %collective-permute-start.11 = (f32[32,768]{1,0:T(8,128)S(1)}, f32[32,768]{1,0:T(8,128)S(1)}, u32[]{:S(2)}, u32[]{:S(2)}) collective-permute-start(f32[32,768]{1,0:T(8,128)S(1)} %get-tuple-element.104), channel_id=1, source_target_pairs={{0,2},{1,3},{2,4},{3,5},{4,6},{5,7},{6,0},{7,1},{8,10},{9,11},{10,... | collective-permute-start | bytes 294920 | tf_op jit(solution)/shard_map/ppermute | solution.py:461
  42.4 9.4 %copy-start.5 = (f32[1536]{0:T(1024)S(1)}, f32[1536]{0:T(1024)}, u32[]{:S(2)}) copy-start(f32[1536]{0:T(1024)} %param.13) | copy-start | bytes 18436
  42.4 5.3 %collective-permute-start.12 = (f32[32,768]{1,0:T(8,128)S(1)}, f32[32,768]{1,0:T(8,128)S(1)}, u32[]{:S(2)}, u32[]{:S(2)}) collective-permute-start(f32[32,768]{1,0:T(8,128)S(1)} %get-tuple-element.105), channel_id=1, source_target_pairs={{0,6},{1,7},{2,0},{3,1},{4,2},{5,3},{6,4},{7,5},{8,14},{9,15},{10,... | collective-permute-start | bytes 294920 | tf_op jit(solution)/shard_map/ppermute | solution.py:461
  48.3 6.4 %collective-permute-start.13 = (f32[128,768]{1,0:T(8,128)S(1)}, f32[128,768]{1,0:T(8,128)S(1)}, u32[]{:S(2)}, u32[]{:S(2)}) collective-permute-start(f32[128,768]{1,0:T(8,128)S(1)} %get-tuple-element.119), channel_id=1, source_target_pairs={{0,1},{1,0},{2,3},{3,2},{4,5},{5,4},{6,7},{7,6},{8,9},{9,8},{10,11... | collective-permute-start | bytes 1179656 | tf_op jit(solution)/shard_map/ppermute | solution.py:461
